TPU v7x, 32 devices: a whole 2x2x4 slice. The times are simulated.
32 devices in a mesh: fsdp: 8 (over y, x, core), ctx: 4 (over z).
Axes of the slice: x: 2, y: 2, z: 4, core: 2. Of those that a mesh axis runs over, the one named last changes fastest.
Arguments:
- inputs: bfloat16 [2, 8192, 2048], P(None, ('fsdp', 'ctx')), may hold values from -6 to 6
- depths: int32 [2, 8192], P(None, ('fsdp', 'ctx')), may hold values from 0 to 767, as said below
- parents: int32 [2, 8, 8], P(None, 'fsdp'), may hold values from 0 to 6, as said below
- layout: int32 [2, 8, 8], P(None, 'fsdp'), may hold values from 0 to 7, as said below
- gain_attn: bfloat16 [2048], P('fsdp'), may hold values from 0.5 to 1.5
- w_query: bfloat16 [2048, 2048], P('fsdp'), may hold values from -0.125 to 0.125
- w_key: bfloat16 [2048, 1024], P('fsdp'), may hold values from -0.125 to 0.125
- w_value: bfloat16 [2048, 1024], P('fsdp'), may hold values from -0.125 to 0.125
- query_gain: bfloat16 [128], P('fsdp'), may hold values from 0.099609375 to 1.8984375
- key_gain: bfloat16 [128], P('fsdp'), may hold values from 0.099609375 to 1.8984375
- w_output: bfloat16 [2048, 2048], P('fsdp'), may hold values from -1 to 1
- gain_ffn: bfloat16 [2048], P('fsdp'), may hold values from 0.5 to 1.5
- w_gate: bfloat16 [2048, 6144], P('fsdp'), may hold values from -0.125 to 0.125
- w_up: bfloat16 [2048, 6144], P('fsdp'), may hold values from -0.125 to 0.125
- w_down: bfloat16 [6144, 2048], P('fsdp'), may hold values from -0.078125 to 0.078125
- cotangent: bfloat16 [2, 8192, 2048], P(None, ('fsdp', 'ctx')), may hold values from -6 to 6
Outputs:
- outputs: bfloat16 [2, 8192, 2048], P(None, ('fsdp', 'ctx'))
- grad_inputs: float32 [2, 8192, 2048], P(None, ('fsdp', 'ctx'))
- grad_gain_attn: float32 [2048], P('fsdp')
- grad_w_query: float32 [2048, 2048], P('fsdp')
- grad_w_key: float32 [2048, 1024], P('fsdp')
- grad_w_value: float32 [2048, 1024], P('fsdp')
- grad_query_gain: float32 [128], P('fsdp')
- grad_key_gain: float32 [128], P('fsdp')
- grad_w_output: float32 [2048, 2048], P('fsdp')
- grad_gain_ffn: float32 [2048], P('fsdp')
- grad_w_gate: float32 [2048, 6144], P('fsdp')
- grad_w_up: float32 [2048, 6144], P('fsdp')
- grad_w_down: float32 [6144, 2048], P('fsdp')
Inputs may be any that keep to these rules, and one draw needn't show every extreme that they name: `parents`: for each tree, entry 0 (the root) is 0 and every other entry b is less than b. `layout`: for each tree, each segment appears once. `depths`: A token's depth is 128 times the number of proper ancestors of its segment plus its place within the segment.
All inputs are finite; a program needn't handle non-finite values.
Results may differ from a plain program's by a relative error of at most 0.025.
Values may be sent and summed in bfloat16 or wider, within the bound.
No kernel may reach another device: no remote copies, remote signals or barrier semaphores. Data moves between devices by JAX's collectives and lax.ppermute only.
A program may use at most 576 MiB of HBM per device.

v0:
```python
import jax
import jax.numpy as jnp
from jax import lax
from jax.sharding import PartitionSpec as P

D = 2048
QH = 16
KVH = 8
DH = 128
FF = 6144
BLK = 128


EPS = 1e-06
NEG = -1e30
BASE = 1000000.0


def rms_gain(values, gain):
    return values * lax.rsqrt(jnp.mean(values * values, axis=-1, keepdims=True) + EPS) * gain


def rotate(values, depth):
    half = values.shape[-1] // 2
    freq = jnp.power(BASE, -jnp.arange(half, dtype=jnp.float32) / half)
    angle = depth.astype(jnp.float32)[:, None] * freq[None, :]
    cosine = jnp.cos(angle)[:, None, :]
    sine = jnp.sin(angle)[:, None, :]
    first = values[..., :half]
    second = values[..., half:]
    return jnp.concatenate(
        [first * cosine - second * sine, second * cosine + first * sine], axis=-1
    )


def head_post(raw, gain, depth, heads):
    shaped = raw.reshape(raw.shape[0], heads, DH)
    return rotate(rms_gain(shaped, gain), depth)


def swiglu(gate, up):
    return jax.nn.silu(gate) * up


def visibility(parent, layout, offset, count):
    blocks = parent.shape[0]
    ident = jnp.arange(blocks, dtype=jnp.int32)

    def climb(step, carry):
        current, reach = carry
        current = jnp.sum(jnp.where(current[:, None] == ident[None, :], parent[None, :], 0), axis=1)
        return (current, reach | (current[:, None] == ident[None, :]))

    current, reach = lax.fori_loop(0, blocks, climb, (ident, ident[:, None] == ident[None, :]))
    place = (layout[:, None] == ident[None, :]).astype(jnp.int32)
    row_reach = jnp.dot(jnp.dot(place, reach.astype(jnp.int32)), place.T) > 0
    mine = lax.dynamic_slice_in_dim(row_reach, offset // BLK, count // BLK, 0)
    spread = jnp.repeat(jnp.repeat(mine, BLK, axis=0), BLK, axis=1)
    query_rows = offset + jnp.arange(count, dtype=jnp.int32)
    key_rows = jnp.arange(blocks * BLK, dtype=jnp.int32)
    same = query_rows[:, None] // BLK == key_rows[None, :] // BLK
    return spread & (jnp.logical_not(same) | (key_rows[None, :] <= query_rows[:, None]))


def mat(left, right):
    return jnp.dot(left, right, preferred_element_type=jnp.float32)


def dot_last(left, right):
    return lax.dot_general(
        left, right, (((1,), (1,)), ((), ())), preferred_element_type=jnp.float32
    )


def outer_piece(left, right):
    return lax.dot_general(
        left, right, (((0,), (0,)), ((), ())), preferred_element_type=jnp.float32
    )


def outer_term(left, right):

    def term(start, count):
        return outer_piece(left, right)

    return term


def vector_term(vector):

    def term(start, count):
        return vector

    return term


def reduce_apart(term, total):
    return lax.psum_scatter(
        term(jnp.int32(0), total // lax.axis_size("fsdp") * lax.axis_size("fsdp")).astype(
            jnp.bfloat16
        ),
        "fsdp",
        scatter_dimension=0,
        tiled=True,
    ).astype(jnp.float32)


def scores_of(queries, keys_all, visible, scale):
    scores = (
        jnp.einsum("qgjd,kgd->gjqk", queries, keys_all, preferred_element_type=jnp.float32) * scale
    )
    return jnp.where(visible[None, None], scores, NEG)


def body(
    inputs,
    depths,
    parents,
    layout,
    gain_attn,
    w_query,
    w_key,
    w_value,
    query_gain,
    key_gain,
    w_output,
    gain_ffn,
    w_gate,
    w_up,
    w_down,
    cotangent,
):
    micro = inputs.shape[0]
    local_rows = inputs.shape[1]
    blocks = parents.shape[2]
    tree_rows = blocks * BLK
    group = QH // KVH
    scale = DH ** (-0.5)
    offset = lax.axis_index("ctx") * local_rows
    results = []
    grad_list = []
    kept = [[] for index in range(11)]
    gain_sums = [None, None, None, None]
    for micro_index in range(micro):
        visible = visibility(parents[micro_index, 0], layout[micro_index, 0], offset, local_rows)
        depth_now = depths[micro_index]
        weight_set = (
            lax.all_gather(gain_attn, "fsdp", axis=0, tiled=True),
            lax.all_gather(w_query, "fsdp", axis=0, tiled=True),
            lax.all_gather(w_key, "fsdp", axis=0, tiled=True),
            lax.all_gather(w_value, "fsdp", axis=0, tiled=True),
            lax.all_gather(query_gain, "fsdp", axis=0, tiled=True),
            lax.all_gather(key_gain, "fsdp", axis=0, tiled=True),
            lax.all_gather(w_output, "fsdp", axis=0, tiled=True),
            lax.all_gather(gain_ffn, "fsdp", axis=0, tiled=True),
            lax.all_gather(w_gate, "fsdp", axis=0, tiled=True),
            lax.all_gather(w_up, "fsdp", axis=0, tiled=True),
            lax.all_gather(w_down, "fsdp", axis=0, tiled=True),
        )
        attn_gain = weight_set[0].astype(jnp.float32)
        qgain_full = weight_set[4].astype(jnp.float32)
        kgain_full = weight_set[5].astype(jnp.float32)
        ffn_gain = weight_set[7].astype(jnp.float32)
        source = inputs[micro_index].astype(jnp.float32)
        normed_f, normed_back = jax.vjp(rms_gain, source, attn_gain)
        normed_b = normed_f.astype(jnp.bfloat16)
        query_raw = mat(normed_b, weight_set[1])
        key_raw = mat(normed_b, weight_set[2])
        value_b = mat(normed_b, weight_set[3]).astype(jnp.bfloat16)

        def query_post(raw, gain):
            return head_post(raw, gain, depth_now, QH)

        def key_post(raw, gain):
            return head_post(raw, gain, depth_now, KVH)

        query_f, query_back = jax.vjp(query_post, query_raw, qgain_full)
        key_f, key_back = jax.vjp(key_post, key_raw, kgain_full)
        queries = query_f.astype(jnp.bfloat16).reshape(local_rows, KVH, group, DH)
        key_b = key_f.astype(jnp.bfloat16).reshape(local_rows, KVH * DH)
        keys_flat, values_flat = (
            lax.all_gather(key_b, "ctx", axis=0, tiled=True),
            lax.all_gather(value_b, "ctx", axis=0, tiled=True),
        )
        keys_all = keys_flat.reshape(tree_rows, KVH, DH)
        values_all = values_flat.reshape(tree_rows, KVH, DH)
        scores = scores_of(queries, keys_all, visible, scale)
        top = jnp.max(scores, axis=-1, keepdims=True)
        lse = top + jnp.log(jnp.sum(jnp.exp(scores - top), axis=-1, keepdims=True))
        probs_low = jnp.exp(scores - lse).astype(jnp.bfloat16)
        attended = jnp.einsum(
            "gjqk,kgd->qgjd", probs_low, values_all, preferred_element_type=jnp.float32
        )
        attended_b = attended.reshape(local_rows, QH * DH).astype(jnp.bfloat16)
        middle = source + mat(attended_b, weight_set[6])
        mid_f, mid_back = jax.vjp(rms_gain, middle, ffn_gain)
        mid_b = mid_f.astype(jnp.bfloat16)
        gate = mat(mid_b, weight_set[8])
        up_proj = mat(mid_b, weight_set[9])
        act_f, act_back = jax.vjp(swiglu, gate, up_proj)
        act_b = act_f.astype(jnp.bfloat16)
        results.append((middle + mat(act_b, weight_set[10])).astype(jnp.bfloat16))
        cot_b = cotangent[micro_index]
        d_act = dot_last(cot_b, weight_set[10])
        d_gate, d_up = act_back(d_act)
        dgate_b = d_gate.astype(jnp.bfloat16)
        dup_b = d_up.astype(jnp.bfloat16)
        d_mid = dot_last(dgate_b, weight_set[8]) + dot_last(dup_b, weight_set[9])
        d_middle_part, d_ffn_gain = mid_back(d_mid)
        d_middle = cot_b.astype(jnp.float32) + d_middle_part
        dproj_b = d_middle.astype(jnp.bfloat16)
        d_attended = (
            dot_last(dproj_b, weight_set[6])
            .astype(jnp.bfloat16)
            .reshape(local_rows, KVH, group, DH)
        )
        scores = scores_of(queries, keys_all, visible, scale)
        probs = jnp.exp(scores - lse)
        probs_low = probs.astype(jnp.bfloat16)
        d_probs = jnp.einsum(
            "qgjd,kgd->gjqk", d_attended, values_all, preferred_element_type=jnp.float32
        )
        d_scores = (probs * (d_probs - jnp.sum(probs * d_probs, axis=-1, keepdims=True))).astype(
            jnp.bfloat16
        )
        d_queries = (
            jnp.einsum("gjqk,kgd->qgjd", d_scores, keys_all, preferred_element_type=jnp.float32)
            * scale
        )
        dkeys_all = (
            jnp.einsum("gjqk,qgjd->kgd", d_scores, queries, preferred_element_type=jnp.float32)
            * scale
        )
        dvalues_all = jnp.einsum(
            "gjqk,qgjd->kgd", probs_low, d_attended, preferred_element_type=jnp.float32
        )
        d_keys, d_values = (
            lax.psum_scatter(
                dkeys_all.reshape(tree_rows, KVH * DH).astype(jnp.bfloat16),
                "ctx",
                scatter_dimension=0,
                tiled=True,
            ).astype(jnp.float32),
            lax.psum_scatter(
                dvalues_all.reshape(tree_rows, KVH * DH).astype(jnp.bfloat16),
                "ctx",
                scatter_dimension=0,
                tiled=True,
            ).astype(jnp.float32),
        )
        dquery_raw, dquery_gain = query_back(d_queries.reshape(local_rows, QH, DH))
        dkey_raw, dkey_gain = key_back(d_keys.reshape(local_rows, KVH, DH))
        dquery_b = dquery_raw.astype(jnp.bfloat16)
        dkey_b = dkey_raw.astype(jnp.bfloat16)
        dvalue_b = d_values.astype(jnp.bfloat16)
        d_normed = (
            dot_last(dquery_b, weight_set[1])
            + dot_last(dkey_b, weight_set[2])
            + dot_last(dvalue_b, weight_set[3])
        )
        d_source, d_attn_gain = normed_back(d_normed)
        grad_list.append(d_middle + d_source)
        for slot, item in enumerate(
            (
                normed_b,
                dquery_b,
                dkey_b,
                dvalue_b,
                attended_b,
                dproj_b,
                mid_b,
                dgate_b,
                dup_b,
                act_b,
                cot_b,
            )
        ):
            kept[slot].append(item)
        for slot, item in enumerate((d_attn_gain, dquery_gain, dkey_gain, d_ffn_gain)):
            gain_sums[slot] = item if gain_sums[slot] is None else gain_sums[slot] + item
    joined = [jnp.concatenate(items, axis=0) for items in kept]
    (
        normed_all,
        dquery_all,
        dkey_all,
        dvalue_all,
        attended_all,
        dproj_all,
        mid_all,
        dgate_all,
        dup_all,
        act_all,
        cot_all,
    ) = joined
    terms = [
        vector_term(gain_sums[0]),
        outer_term(normed_all, dquery_all),
        outer_term(normed_all, dkey_all),
        outer_term(normed_all, dvalue_all),
        vector_term(gain_sums[1]),
        vector_term(gain_sums[2]),
        outer_term(attended_all, dproj_all),
        vector_term(gain_sums[3]),
        outer_term(mid_all, dgate_all),
        outer_term(mid_all, dup_all),
        outer_term(act_all, cot_all),
    ]
    extents = [D, D, D, D, DH, DH, QH * DH, D, D, D, FF]
    shards = [reduce_apart(term_fn, extent) for term_fn, extent in zip(terms, extents)]
    summed = (
        lax.psum(shards[0].astype(jnp.bfloat16), "ctx").astype(jnp.float32),
        lax.psum(shards[1].astype(jnp.bfloat16), "ctx").astype(jnp.float32),
        lax.psum(shards[2].astype(jnp.bfloat16), "ctx").astype(jnp.float32),
        lax.psum(shards[3].astype(jnp.bfloat16), "ctx").astype(jnp.float32),
        lax.psum(shards[4].astype(jnp.bfloat16), "ctx").astype(jnp.float32),
        lax.psum(shards[5].astype(jnp.bfloat16), "ctx").astype(jnp.float32),
        lax.psum(shards[6].astype(jnp.bfloat16), "ctx").astype(jnp.float32),
        lax.psum(shards[7].astype(jnp.bfloat16), "ctx").astype(jnp.float32),
        lax.psum(shards[8].astype(jnp.bfloat16), "ctx").astype(jnp.float32),
        lax.psum(shards[9].astype(jnp.bfloat16), "ctx").astype(jnp.float32),
        lax.psum(shards[10].astype(jnp.bfloat16), "ctx").astype(jnp.float32),
    )
    return (
        jnp.stack(results),
        jnp.stack(grad_list),
        summed[0],
        summed[1],
        summed[2],
        summed[3],
        summed[4],
        summed[5],
        summed[6],
        summed[7],
        summed[8],
        summed[9],
        summed[10],
    )


def solution(mesh):
    in_specs = (
        P(None, ("fsdp", "ctx"), None),
        P(None, ("fsdp", "ctx")),
        P(None, "fsdp", None),
        P(None, "fsdp", None),
        P("fsdp"),
        P("fsdp", None),
        P("fsdp", None),
        P("fsdp", None),
        P("fsdp"),
        P("fsdp"),
        P("fsdp", None),
        P("fsdp"),
        P("fsdp", None),
        P("fsdp", None),
        P("fsdp", None),
        P(None, ("fsdp", "ctx"), None),
    )
    out_specs = (
        P(None, ("fsdp", "ctx"), None),
        P(None, ("fsdp", "ctx"), None),
        P("fsdp"),
        P("fsdp", None),
        P("fsdp", None),
        P("fsdp", None),
        P("fsdp"),
        P("fsdp"),
        P("fsdp", None),
        P("fsdp"),
        P("fsdp", None),
        P("fsdp", None),
        P("fsdp", None),
    )
    return jax.shard_map(body, mesh=mesh, in_specs=in_specs, out_specs=out_specs, check_vma=False)
```

profile of v0, /device:TPU:0, one launch (start us, length us, event | category | flops | bytes accessed | tf_op | source)
XLA Modules:
  0.0 2325.9 jit_solution(18062956885824340002)
XLA Ops:
  23.8 25.5 %all-gather.14.cloned.1.call-done = bf16[2048,1024]{1,0:T(8,128)(2,1)} async-done(((bf16[256,1024]{1,0:T(8,128)(2,1)}), bf16[2048,1024]{1,0:T(8,128)(2,1)}) %all-gather.14.cloned.1.call-update) | async-done | bytes 4194320 | tf_op jit(solution)/shard_map/all_gather | solution.py:151
  120.4 15.9 all-gather.32.cloned.1.call-done
  138.4 44.5 %all-gather.16.cloned.1.call-done = bf16[1024,1024]{1,0:T(8,128)(2,1)} async-done(((bf16[256,1024]{1,0:T(8,128)(2,1)}), bf16[1024,1024]{1,0:T(8,128)(2,1)}) %all-gather.16.cloned.1.call-update) | async-done | bytes 2097168 | tf_op jit(solution)/shard_map/all_gather | solution.py:183
  186.4 51.3 %all-gather.22.cloned.1.call-done = bf16[2048,2048]{1,0:T(8,128)(2,1)} async-done(((bf16[256,2048]{1,0:T(8,128)(2,1)}), bf16[2048,2048]{1,0:T(8,128)(2,1)}) %all-gather.22.cloned.1.call-update) | async-done | bytes 8388624 | tf_op jit(solution)/shard_map/all_gather | solution.py:149
  316.4 24.2 %all-gather.24.cloned.1.call-done = bf16[2048,2048]{1,0:T(8,128)(2,1)} async-done(((bf16[256,2048]{1,0:T(8,128)(2,1)}), bf16[2048,2048]{1,0:T(8,128)(2,1)}) %all-gather.24.cloned.1.call-update) | async-done | bytes 8388624 | tf_op jit(solution)/shard_map/all_gather | solution.py:154
  348.3 40.7 %all-gather.34.cloned.1.call-done = bf16[1024,1024]{0,1:T(8,128)(2,1)} async-done(((bf16[256,1024]{0,1:T(8,128)(2,1)}), bf16[1024,1024]{0,1:T(8,128)(2,1)}) %all-gather.34.cloned.1.call-update) | async-done | bytes 2097168 | tf_op jit(solution)/shard_map/all_gather | solution.py:182
  389.0 14.5 fusion.174
  425.4 89.1 %all-gather.26.cloned.1.call-done = bf16[2048,6144]{1,0:T(8,128)(2,1)} async-done(((bf16[256,6144]{1,0:T(8,128)(2,1)}), bf16[2048,6144]{1,0:T(8,128)(2,1)}) %all-gather.26.cloned.1.call-update) | async-done | bytes 25165840 | tf_op jit(solution)/shard_map/all_gather | solution.py:156
  514.5 13.7 fusion.176
  528.2 113.4 %all-gather.28.cloned.1.call-done = bf16[2048,6144]{1,0:T(8,128)(2,1)} async-done(((bf16[256,6144]{1,0:T(8,128)(2,1)}), bf16[2048,6144]{1,0:T(8,128)(2,1)}) %all-gather.28.cloned.1.call-update) | async-done | bytes 25165840 | tf_op jit(solution)/shard_map/all_gather | solution.py:157
  655.2 113.6 %all-gather.30.cloned.1.call-done = bf16[6144,2048]{1,0:T(8,128)(2,1)} async-done(((bf16[768,2048]{1,0:T(8,128)(2,1)}), bf16[6144,2048]{1,0:T(8,128)(2,1)}) %all-gather.30.cloned.1.call-update) | async-done | bytes 25165840 | tf_op jit(solution)/shard_map/all_gather | solution.py:158
  768.8 20.6 multiply_convert_fusion.1
  802.8 15.6 multiply_reduce_fusion.1
  818.4 14.7 fusion.178
  833.1 14.7 fusion.179
  847.9 20.3 multiply_convert_fusion
  881.7 15.7 multiply_reduce_fusion
  910.3 14.7 fusion.9
  953.6 14.8 fusion.6
  1012.7 22.8 reduce-scatter.16.cloned.1.call-done
  1045.8 35.7 %reduce-scatter.18.cloned.1.call-done = bf16[256,1024]{0,1:T(8,128)(2,1)} async-done(((bf16[1024,1024]{0,1:T(8,128)(2,1)}), bf16[256,1024]{0,1:T(8,128)(2,1)}) %reduce-scatter.18.cloned.1.call-update) | async-done | bytes 524304 | tf_op jit(solution)/shard_map/reduce_scatter | solution.py:244
  1081.5 45.5 %reduce-scatter.14.cloned.1.call-done = bf16[256,1024]{0,1:T(8,128)(2,1)} async-done(((bf16[1024,1024]{0,1:T(8,128)(2,1)}), bf16[256,1024]{0,1:T(8,128)(2,1)}) %reduce-scatter.14.cloned.1.call-update) | async-done | bytes 524304 | tf_op jit(solution)/shard_map/reduce_scatter | solution.py:244
  1171.4 19.8 convolution_convert_fusion.2
  1191.3 19.9 convolution_convert_fusion.1
  1214.7 18.5 convolution_convert_fusion
  1237.0 74.6 %reduce-scatter.20.cloned.1.call-done = bf16[256,2048]{1,0:T(8,128)(2,1)} async-done(((bf16[2048,2048]{1,0:T(8,128)(2,1)}), bf16[256,2048]{1,0:T(8,128)(2,1)}) %reduce-scatter.20.cloned.1.call-update) | async-done | bytes 1048592 | tf_op jit(solution)/shard_map/reduce_scatter | solution.py:98
  1311.6 75.2 %reduce-scatter.26.cloned.1.call-done = bf16[256,2048]{1,0:T(8,128)(2,1)} async-done(((bf16[2048,2048]{1,0:T(8,128)(2,1)}), bf16[256,2048]{1,0:T(8,128)(2,1)}) %reduce-scatter.26.cloned.1.call-update) | async-done | bytes 1048592 | tf_op jit(solution)/shard_map/reduce_scatter | solution.py:98
  1386.8 160.4 %reduce-scatter.28.cloned.1.call-done = bf16[256,6144]{1,0:T(8,128)(2,1)} async-done(((bf16[2048,6144]{1,0:T(8,128)(2,1)}), bf16[256,6144]{1,0:T(8,128)(2,1)}) %reduce-scatter.28.cloned.1.call-update) | async-done | bytes 3145744 | tf_op jit(solution)/shard_map/reduce_scatter | solution.py:98
  1547.2 160.5 %reduce-scatter.30.cloned.1.call-done = bf16[256,6144]{1,0:T(8,128)(2,1)} async-done(((bf16[2048,6144]{1,0:T(8,128)(2,1)}), bf16[256,6144]{1,0:T(8,128)(2,1)}) %reduce-scatter.30.cloned.1.call-update) | async-done | bytes 3145744 | tf_op jit(solution)/shard_map/reduce_scatter | solution.py:98
  1707.7 160.5 %reduce-scatter.32.cloned.1.call-done = bf16[768,2048]{1,0:T(8,128)(2,1)} async-done(((bf16[6144,2048]{1,0:T(8,128)(2,1)}), bf16[768,2048]{1,0:T(8,128)(2,1)}) %reduce-scatter.32.cloned.1.call-update) | async-done | bytes 3145744 | tf_op jit(solution)/shard_map/reduce_scatter | solution.py:98
  1869.6 14.3 fusion.49
  1950.5 351.5 %all-reduce.20.cloned.1.call-done = (bf16[256,2048]{1,0:T(8,128)(2,1)}, bf16[256,1024]{1,0:T(8,128)(2,1)}, bf16[256,1024]{1,0:T(8,128)(2,1)}, bf16[256,2048]{1,0...) async-done(((bf16[256,2048]{1,0:T(8,128)(2,1)}, bf16[256,1024]{1,0:T(8,128)(2,1)}, bf16[256,1024]{1,0:T(8,128)(2,1)}, ...) | async-done | bytes 12582928 | tf_op jit(solution)/shard_map/psum | solution.py:312
  (527 shorter events, 475.3 us)
Async XLA Ops:
  7.2 42.2 %all-gather.14.cloned.1.call-start = ((), (), s32[]{:S(2)}) async-start(), calls=%async_computation.11 | async-start | bytes 4718592 | tf_op jit(solution)/shard_map/all_gather | solution.py:151
  7.9 80.2 %all-gather.18.cloned.1.call-start = ((), (), s32[]{:S(2)}) async-start(), calls=%async_computation.13 | async-start | bytes 4718592 | tf_op jit(solution)/shard_map/all_gather | solution.py:150
  8.7 127.5 %all-gather.32.cloned.1.call-start = ((), (), s32[]{:S(2)}) async-start(), calls=%async_computation.20 | async-start | bytes 2621440 | tf_op jit(solution)/shard_map/all_gather | solution.py:183
  19.7 236.9 %copy-start.75 = (f32[8,1,256]{2,1,0:T(1,128)}, f32[8,1,256]{2,1,0:T(1,128)S(1)}, u32[]{:S(2)}) copy-start(f32[8,1,256]{2,1,0:T(1,128)S(1)} %convert_element_type.428) | copy-start | bytes 24580
  21.9 228.4 %copy-start.103 = (f32[256]{0:T(256)}, f32[256]{0:T(256)S(1)}, u32[]{:S(2)}) copy-start(f32[256]{0:T(256)S(1)} %fusion.153) | copy-start | bytes 3076
  22.4 234.2 %copy-start.105 = (f32[256]{0:T(256)}, f32[256]{0:T(256)S(1)}, u32[]{:S(2)}) copy-start(f32[256]{0:T(256)S(1)} %fusion.155) | copy-start | bytes 3076
  53.9 129.0 %all-gather.16.cloned.1.call-start = ((), (), s32[]{:S(2)}) async-start(), calls=%async_computation.12 | async-start | bytes 2621440 | tf_op jit(solution)/shard_map/all_gather | solution.py:183
  58.3 179.5 %all-gather.22.cloned.1.call-start = ((), (), s32[]{:S(2)}) async-start(), calls=%async_computation.15 | async-start | bytes 9437184 | tf_op jit(solution)/shard_map/all_gather | solution.py:149
  58.9 227.1 %all-gather.20.cloned.1.call-start = ((), (), s32[]{:S(2)}) async-start(), calls=%async_computation.14 | async-start | bytes 2621440 | tf_op jit(solution)/shard_map/all_gather | solution.py:182
  74.5 193.1 %copy-start.45 = (f32[256,64]{0,1:T(8,128)}, f32[256,64]{0,1:T(8,128)S(1)}, u32[]{:S(2)}) copy-start(f32[256,64]{0,1:T(8,128)S(1)} %get-tuple-element.209) | copy-start | bytes 196612
  74.6 193.1 %copy-start.47 = (f32[256,64]{0,1:T(8,128)}, f32[256,64]{0,1:T(8,128)S(1)}, u32[]{:S(2)}) copy-start(f32[256,64]{0,1:T(8,128)S(1)} %get-tuple-element.210) | copy-start | bytes 196612
  101.8 238.8 %all-gather.24.cloned.1.call-start = ((), (), s32[]{:S(2)}) async-start(), calls=%async_computation.16 | async-start | bytes 9437184 | tf_op jit(solution)/shard_map/all_gather | solution.py:154
  102.5 286.4 %all-gather.34.cloned.1.call-start = ((), (), s32[]{:S(2)}) async-start(), calls=%async_computation.21 | async-start | bytes 2621440 | tf_op jit(solution)/shard_map/all_gather | solution.py:182
  103.6 410.9 %all-gather.26.cloned.1.call-start = ((), (), s32[]{:S(2)}) async-start(), calls=%async_computation.17 | async-start | bytes 28311552 | tf_op jit(solution)/shard_map/all_gather | solution.py:156
  104.3 537.2 %all-gather.28.cloned.1.call-start = ((), (), s32[]{:S(2)}) async-start(), calls=%async_computation.18 | async-start | bytes 28311552 | tf_op jit(solution)/shard_map/all_gather | solution.py:157
  105.0 663.9 %all-gather.30.cloned.1.call-start = ((), (), s32[]{:S(2)}) async-start(), calls=%async_computation.19 | async-start | bytes 28311552 | tf_op jit(solution)/shard_map/all_gather | solution.py:158
  105.7 905.8 %reduce-scatter.12.cloned.1.call-start = ((), (), s32[]{:S(2)}) async-start(), calls=%async_computation.22 | async-start | bytes 2621440 | tf_op jit(solution)/shard_map/reduce_scatter | solution.py:238
  114.6 782.8 %copy-start.73 = (f32[8,1,256]{2,1,0:T(1,128)}, f32[8,1,256]{2,1,0:T(1,128)S(1)}, u32[]{:S(2)}) copy-start(f32[8,1,256]{2,1,0:T(1,128)S(1)} %convert_element_type.429) | copy-start | bytes 24580
  138.4 273.5 %copy-start.1 = (bf16[128,8,8,128]{3,2,1,0:T(8,128)(2,1)}, bf16[128,8,8,128]{3,2,1,0:T(8,128)(2,1)S(1)}, u32[]{:S(2)}) copy-start(bf16[128,8,8,128]{3,2,1,0:T(8,128)(2,1)S(1)} %copy.144) | copy-start | bytes 6291460
  348.3 549.1 %copy-start.89 = (f32[256]{0:T(256)}, f32[256]{0:T(256)S(1)}, u32[]{:S(2)}) copy-start(f32[256]{0:T(256)S(1)} %fusion.154) | copy-start | bytes 3076
  424.1 473.3 %copy-start.99 = (f32[256]{0:T(256)}, f32[256]{0:T(256)S(1)}, u32[]{:S(2)}) copy-start(f32[256]{0:T(256)S(1)} %fusion.156) | copy-start | bytes 3076
  945.3 90.2 %reduce-scatter.16.cloned.1.call-start = ((), (), s32[]{:S(2)}) async-start(), calls=%async_computation.24 | async-start | bytes 2621440 | tf_op jit(solution)/shard_map/reduce_scatter | solution.py:238
  989.3 92.2 %reduce-scatter.18.cloned.1.call-start = ((), (), s32[]{:S(2)}) async-start(), calls=%async_computation.25 | async-start | bytes 2621440 | tf_op jit(solution)/shard_map/reduce_scatter | solution.py:244
  1000.6 126.4 %reduce-scatter.14.cloned.1.call-start = ((), (), s32[]{:S(2)}) async-start(), calls=%async_computation.23 | async-start | bytes 2621440 | tf_op jit(solution)/shard_map/reduce_scatter | solution.py:244
  1011.4 221.9 %reduce-scatter.22.cloned.1.call-start = ((), (), s32[]{:S(2)}) async-start(), calls=%async_computation.27 | async-start | bytes 4718592 | tf_op jit(solution)/shard_map/reduce_scatter | solution.py:98
  1045.8 191.2 %reduce-scatter.24.cloned.1.call-start = ((), (), s32[]{:S(2)}) async-start(), calls=%async_computation.28 | async-start | bytes 4718592 | tf_op jit(solution)/shard_map/reduce_scatter | solution.py:98
  1132.6 179.0 %reduce-scatter.20.cloned.1.call-start = ((), (), s32[]{:S(2)}) async-start(), calls=%async_computation.26 | async-start | bytes 9437184 | tf_op jit(solution)/shard_map/reduce_scatter | solution.py:98
  1160.1 226.7 %reduce-scatter.26.cloned.1.call-start = ((), (), s32[]{:S(2)}) async-start(), calls=%async_computation.29 | async-start | bytes 9437184 | tf_op jit(solution)/shard_map/reduce_scatter | solution.py:98
  1169.9 377.3 %reduce-scatter.28.cloned.1.call-start = ((), (), s32[]{:S(2)}) async-start(), calls=%async_computation.30 | async-start | bytes 28311552 | tf_op jit(solution)/shard_map/reduce_scatter | solution.py:98
  1191.2 516.5 %reduce-scatter.30.cloned.1.call-start = ((), (), s32[]{:S(2)}) async-start(), calls=%async_computation.31 | async-start | bytes 28311552 | tf_op jit(solution)/shard_map/reduce_scatter | solution.py:98
  1211.2 657.0 %reduce-scatter.32.cloned.1.call-start = ((), (), s32[]{:S(2)}) async-start(), calls=%async_computation.32 | async-start | bytes 28311552 | tf_op jit(solution)/shard_map/reduce_scatter | solution.py:98
  1233.3 1068.8 %all-reduce.20.cloned.1.call-start = ((), (), s32[]{:S(2)}) async-start(), calls=%async_computation.33 | async-start | bytes 25165824 | tf_op jit(solution)/shard_map/psum | solution.py:312
  (130 other events, 1600.4 us)
Sparse Core Ops, SparseCore 0:
  9.9 39.4 all-gather.13
  51.2 36.8 all-gather.17
  90.2 45.9 all-gather.31
  138.2 44.6 all-gather.15
  184.6 53.0 all-gather.21
  239.8 46.2 all-gather.19
  287.9 52.6 all-gather.23
  342.7 46.2 all-gather.33
  390.9 123.5 all-gather.25
  516.2 125.3 all-gather.27
  643.4 125.3 all-gather.29
  945.5 43.8 reduce-scatter.11
  992.3 43.1 reduce-scatter.15
  1038.2 43.2 reduce-scatter.17
  1083.8 43.1 reduce-scatter.13
  1130.8 50.6 reduce-scatter.21
  1185.6 51.3 reduce-scatter.23
  1240.3 71.2 reduce-scatter.19
  1315.5 71.2 reduce-scatter.25
  1390.3 156.8 reduce-scatter.27
  1550.8 156.8 reduce-scatter.29
  1711.3 156.8 reduce-scatter.31
  1871.6 430.3 all-reduce.19
where the time goes:
time: 2340 us; the launch traced here: 2330 us
  waiting for transfers between devices  1640 us (70%)
  matrix products  444 us (19%)
  other arithmetic  99.1 us (4%)
  local copies, waits for them, and re-layouts  66.5 us (3%)
  blocking collectives  58.2 us (2%)
    reduce_scatter x7, waiting for transfers between devices, reduce_apart(): lax.psum_scatter(term(jnp.int32(0), total // lax.axis_size('fsdp') * lax....  635 us
    psum x1, waiting for transfers between devices, body(): lax.psum(shards[1].astype(jnp.bfloat16), 'ctx').astype(jnp.float32)  352 us
    dot_general x14, matrix products, dot_last(): lax.dot_general(left, right, (((1,), (1,)), ((), ())), preferred_element_...  123 us
    dot_general x14, matrix products, mat(): return jnp.dot(left, right, preferred_element_type=jnp.float32)  118 us
    all_gather x1, waiting for transfers between devices, body(): lax.all_gather(w_down, 'fsdp', axis=0, tiled=True)  114 us
    all_gather x1, waiting for transfers between devices, body(): lax.all_gather(w_up, 'fsdp', axis=0, tiled=True)  113 us
    all_gather x1, waiting for transfers between devices, body(): lax.all_gather(w_gate, 'fsdp', axis=0, tiled=True)  89.1 us
    dot_general x7, matrix products, outer_piece(): lax.dot_general(left, right, (((0,), (0,)), ((), ())), preferred_element_...  83.1 us
  transfers between devices with their start and end apart: 23, of which 21 were waited for; matrix products, arithmetic and copies ran while one was open for 17% of the time, Pallas kernels for 0%

commit v1 on v0

v1 whole, which is shorter than its diff:
```python
import jax
import jax.numpy as jnp
from jax import lax
from jax.sharding import PartitionSpec as P

D = 2048
QH = 16
KVH = 8
DH = 128
FF = 6144
BLK = 128
GROUP = QH // KVH
SCALE = DH ** (-0.5)

EPS = 1e-06
NEG = -1e30
BASE = 1000000.0
BF = jnp.bfloat16
F32 = jnp.float32


def mat(left, right):
    return jnp.dot(left, right, preferred_element_type=F32)


def dot_last(left, right):
    return lax.dot_general(left, right, (((1,), (1,)), ((), ())), preferred_element_type=F32)


def outer(left, right):
    return lax.dot_general(left, right, (((0,), (0,)), ((), ())), preferred_element_type=F32)


def swap(value, bits):
    count = lax.axis_size("fsdp")
    return lax.ppermute(value, "fsdp", [(i, i ^ bits) for i in range(count)])


def inv_rms(values):
    return lax.rsqrt(jnp.mean(values * values, axis=-1, keepdims=True) + EPS)


def rms_back(values, inv, gain, dy):
    product = dy * values
    dv = inv * (gain * dy) - values * (inv * inv * inv) * jnp.mean(
        product * gain, axis=-1, keepdims=True
    )
    dg = jnp.sum(product * inv, axis=tuple(range(values.ndim - 1)))
    return dv, dg


def rotate(values, cosine, sine):
    half = values.shape[-1] // 2
    first = values[..., :half]
    second = values[..., half:]
    return jnp.concatenate(
        [first * cosine - second * sine, second * cosine + first * sine], axis=-1
    )


def visibility(parent, layout, offset, count):
    blocks = parent.shape[0]
    ident = jnp.arange(blocks, dtype=jnp.int32)
    current = ident
    reach = ident[:, None] == ident[None, :]
    for step in range(blocks):
        current = jnp.sum(jnp.where(current[:, None] == ident[None, :], parent[None, :], 0), axis=1)
        reach = reach | (current[:, None] == ident[None, :])
    place = (layout[:, None] == ident[None, :]).astype(jnp.int32)
    row_reach = jnp.dot(jnp.dot(place, reach.astype(jnp.int32)), place.T) > 0
    mine = lax.dynamic_slice_in_dim(row_reach, offset // BLK, count // BLK, 0)
    spread = jnp.repeat(jnp.repeat(mine, BLK, axis=0), BLK, axis=1)
    query_rows = offset + jnp.arange(count, dtype=jnp.int32)
    key_rows = jnp.arange(blocks * BLK, dtype=jnp.int32)
    same = query_rows[:, None] // BLK == key_rows[None, :] // BLK
    return spread & (jnp.logical_not(same) | (key_rows[None, :] <= query_rows[:, None]))


def gather_small(vector, me):
    count = lax.axis_size("fsdp")
    buffer = jnp.zeros((count,) + vector.shape, vector.dtype)
    buffer = lax.dynamic_update_index_in_dim(buffer, vector, me, 0)
    step = 1
    while step < count:
        buffer = buffer + swap(buffer, step)
        step *= 2
    return buffer


def gather_columns(shard, me):
    count = lax.axis_size("fsdp")
    high = count // 4
    slot = me % 4
    mine_high = me // 4
    rows = shard.shape[0]
    unit = shard.shape[1] // count
    split = shard.reshape(rows, high, 4, unit)

    def part(which):
        return lax.dynamic_index_in_dim(split, which, axis=2, keepdims=False).reshape(
            rows, high * unit
        )

    own = part(slot)
    from_x_mate = swap(part(slot ^ 3), 2)
    from_x = swap(part(slot ^ 2), 2)
    from_core = swap(part(slot ^ 1), 1)
    from_both = swap(from_x_mate, 1)
    pieces = [own, from_core, from_x, from_both]
    buffer = jnp.zeros((count * rows, high * unit), shard.dtype)
    for far in range(high):
        for near in range(4):
            piece = pieces[near] if far == 0 else swap(pieces[near], 4 * far)
            place = (mine_high ^ far) * 4 + (slot ^ near)
            buffer = lax.dynamic_update_slice_in_dim(buffer, piece, place * rows, 0)
    return buffer


def gather_rows(shard, me):
    count = lax.axis_size("fsdp")
    high = count // 4
    mine_high = me // 4
    unit = shard.shape[0]
    buffer = jnp.zeros((high * unit, shard.shape[1]), shard.dtype)
    for far in range(high):
        piece = shard if far == 0 else swap(shard, 4 * far)
        buffer = lax.dynamic_update_slice_in_dim(buffer, piece, (mine_high ^ far) * unit, 0)
    return buffer


def group_rows(rows):
    from_x = swap(rows, 2)
    from_core = swap(rows, 1)
    from_both = swap(from_x, 1)
    return jnp.concatenate([rows, from_core, from_x, from_both], axis=0)


def group_sum(partial):
    rows = partial.shape[0] // 4
    part = [partial[i * rows : (i + 1) * rows] for i in range(4)]
    for_x = part[2] + swap(part[3].astype(BF), 1).astype(F32)
    got_x = swap(for_x.astype(BF), 2)
    got_core = swap(part[1].astype(BF), 1)
    return part[0] + got_core.astype(F32) + got_x.astype(F32)


def sum_high(gradient, me):
    count = lax.axis_size("fsdp")
    high = count // 4
    mine_high = me // 4
    rows = gradient.shape[0] // high

    def part(which):
        return lax.dynamic_slice_in_dim(gradient, which * rows, rows, 0)

    total = None
    for far in range(1, high):
        got = swap(part(mine_high ^ far).astype(BF), 4 * far).astype(F32)
        total = got if total is None else total + got
    own = part(mine_high)
    return (own if total is None else own + total).astype(BF)


def spread_columns(gradient, me):
    count = lax.axis_size("fsdp")
    high = count // 4
    depth = lax.axis_size("ctx")
    slot = me % 4
    summed = sum_high(gradient, me)
    rows = summed.shape[0] // 4
    cols = summed.shape[1]
    unit = cols // high
    chunks = jnp.swapaxes(summed.reshape(4, depth, rows // depth, cols), 0, 1)
    piece = lax.psum_scatter(
        chunks.reshape(4 * rows, cols), "ctx", scatter_dimension=0, tiled=True
    ).reshape(4, rows // depth, cols)

    def part(which):
        return lax.dynamic_index_in_dim(piece, which, axis=0, keepdims=False)

    result = jnp.zeros((rows // depth, high, 4, unit), BF)
    for near in range(4):
        got = part(slot ^ near)
        if near:
            got = swap(got, near)
        result = lax.dynamic_update_slice(
            result, got.reshape(rows // depth, high, 1, unit), (0, 0, slot ^ near, 0)
        )
    result = result.reshape(rows // depth, count * unit)
    return lax.all_gather(result, "ctx", axis=0, tiled=True)


def spread_rows(gradient, me):
    summed = sum_high(gradient, me)
    piece = lax.psum_scatter(summed, "ctx", scatter_dimension=0, tiled=True)
    return lax.all_gather(piece, "ctx", axis=0, tiled=True)


def scatter_plain(gradient):
    piece = lax.psum_scatter(gradient.astype(BF), "fsdp", scatter_dimension=0, tiled=True)
    return lax.psum(piece, "ctx")


def scores_of(queries, keys_all, visible):
    scores = (
        jnp.einsum("qgjd,kgd->gjqk", queries, keys_all, preferred_element_type=F32) * SCALE
    )
    return jnp.where(visible[None, None], scores, NEG)


def body(
    inputs,
    depths,
    parents,
    layout,
    gain_attn,
    w_query,
    w_key,
    w_value,
    query_gain,
    key_gain,
    w_output,
    gain_ffn,
    w_gate,
    w_up,
    w_down,
    cotangent,
):
    me = lax.axis_index("fsdp")
    micro, local, _ = inputs.shape
    total = micro * local
    blocks = parents.shape[2]
    tree_rows = blocks * BLK
    offset = lax.axis_index("ctx") * local
    count = lax.axis_size("fsdp")

    w_qkv = lax.all_gather(
        jnp.concatenate([w_query, w_key, w_value], axis=1), "fsdp", axis=0, tiled=True
    )
    w_out = lax.all_gather(w_output, "fsdp", axis=0, tiled=True)
    gains = gather_small(jnp.concatenate([gain_attn, gain_ffn, query_gain, key_gain]), me)
    shard = D // count
    head_shard = DH // count
    attn_gain = gains[:, :shard].reshape(D).astype(F32)
    ffn_gain = gains[:, shard : 2 * shard].reshape(D).astype(F32)
    q_gain = gains[:, 2 * shard : 2 * shard + head_shard].reshape(DH).astype(F32)
    k_gain = gains[:, 2 * shard + head_shard :].reshape(DH).astype(F32)

    cot_b = cotangent.reshape(total, D)
    wd = gather_rows(w_down, me)
    wg = gather_columns(w_gate, me)
    wu = gather_columns(w_up, me)
    cot_rows = group_rows(cot_b)

    source = inputs.reshape(total, D).astype(F32)
    inv_in = inv_rms(source)
    normed_b = (source * inv_in * attn_gain).astype(BF)
    raw = mat(normed_b, w_qkv)
    query_raw = raw[:, : QH * DH].reshape(total, QH, DH)
    key_raw = raw[:, QH * DH : (QH + KVH) * DH].reshape(total, KVH, DH)
    value_b = raw[:, (QH + KVH) * DH :].astype(BF)
    freq = jnp.power(BASE, -jnp.arange(DH // 2, dtype=F32) / (DH // 2))
    angle = depths.reshape(total).astype(F32)[:, None] * freq[None, :]
    cosine = jnp.cos(angle)[:, None, :]
    sine = jnp.sin(angle)[:, None, :]
    inv_q = inv_rms(query_raw)
    inv_k = inv_rms(key_raw)
    key_b = rotate(key_raw * inv_k * k_gain, cosine, sine).astype(BF).reshape(total, KVH * DH)
    queries = rotate(query_raw * inv_q * q_gain, cosine, sine).astype(BF)

    attended = []
    saved = []
    for index in range(micro):
        part = slice(index * local, (index + 1) * local)
        visible = visibility(parents[index, 0], layout[index, 0], offset, local)
        both = lax.all_gather(
            jnp.concatenate([key_b[part], value_b[part]], axis=1), "ctx", axis=0, tiled=True
        )
        keys_all = both[:, : KVH * DH].reshape(tree_rows, KVH, DH)
        values_all = both[:, KVH * DH :].reshape(tree_rows, KVH, DH)
        query_part = queries[part].reshape(local, KVH, GROUP, DH)
        scores = scores_of(query_part, keys_all, visible)
        top = jnp.max(scores, axis=-1, keepdims=True)
        lse = top + jnp.log(jnp.sum(jnp.exp(scores - top), axis=-1, keepdims=True))
        probs_low = jnp.exp(scores - lse).astype(BF)
        out = jnp.einsum("gjqk,kgd->qgjd", probs_low, values_all, preferred_element_type=F32)
        attended.append(out.reshape(local, QH * DH).astype(BF))
        saved.append((query_part, keys_all, values_all, visible, lse))
    attended_b = jnp.concatenate(attended, axis=0)

    middle = source + mat(attended_b, w_out)
    inv_mid = inv_rms(middle)
    mid_b = (middle * inv_mid * ffn_gain).astype(BF)
    mid_rows = group_rows(mid_b)
    d_act = dot_last(cot_rows, wd)
    gate = mat(mid_rows, wg)
    up = mat(mid_rows, wu)
    sig = jax.nn.sigmoid(gate)
    silu = gate * sig
    act_b = (silu * up).astype(BF)
    dup_b = (d_act * silu).astype(BF)
    dgate_b = (d_act * up * (sig * (1.0 + gate * (1.0 - sig)))).astype(BF)
    outputs = (middle + group_sum(mat(act_b, wd))).astype(BF)
    d_mid = group_sum(dot_last(dgate_b, wg) + dot_last(dup_b, wu))
    grad_down = spread_rows(outer(act_b, cot_rows), me)
    grad_gate = spread_columns(outer(mid_rows, dgate_b), me)
    grad_up = spread_columns(outer(mid_rows, dup_b), me)

    d_part, d_ffn_gain = rms_back(middle, inv_mid, ffn_gain, d_mid)
    d_middle = cot_b.astype(F32) + d_part
    dproj_b = d_middle.astype(BF)
    d_attended = dot_last(dproj_b, w_out).astype(BF)
    grad_output = scatter_plain(outer(attended_b, dproj_b))

    d_query_parts = []
    d_kv_parts = []
    for index in range(micro):
        part = slice(index * local, (index + 1) * local)
        query_part, keys_all, values_all, visible, lse = saved[index]
        d_out = d_attended[part].reshape(local, KVH, GROUP, DH)
        probs = jnp.exp(scores_of(query_part, keys_all, visible) - lse)
        probs_low = probs.astype(BF)
        d_probs = jnp.einsum("qgjd,kgd->gjqk", d_out, values_all, preferred_element_type=F32)
        d_scores = (probs * (d_probs - jnp.sum(probs * d_probs, axis=-1, keepdims=True))).astype(BF)
        d_query = (
            jnp.einsum("gjqk,kgd->qgjd", d_scores, keys_all, preferred_element_type=F32) * SCALE
        )
        d_key = (
            jnp.einsum("gjqk,qgjd->kgd", d_scores, query_part, preferred_element_type=F32) * SCALE
        )
        d_value = jnp.einsum("gjqk,qgjd->kgd", probs_low, d_out, preferred_element_type=F32)
        d_query_parts.append(d_query.reshape(local, QH, DH))
        d_kv_parts.append(
            lax.psum_scatter(
                jnp.concatenate(
                    [
                        d_key.reshape(tree_rows, KVH * DH).astype(BF),
                        d_value.reshape(tree_rows, KVH * DH).astype(BF),
                    ],
                    axis=1,
                ),
                "ctx",
                scatter_dimension=0,
                tiled=True,
            )
        )
    d_queries = jnp.concatenate(d_query_parts, axis=0)
    d_kv = jnp.concatenate(d_kv_parts, axis=0)
    d_keys = d_kv[:, : KVH * DH].astype(F32).reshape(total, KVH, DH)
    dvalue_b = d_kv[:, KVH * DH :]
    dquery_raw, d_q_gain = rms_back(query_raw, inv_q, q_gain, rotate(d_queries, cosine, -sine))
    dkey_raw, d_k_gain = rms_back(key_raw, inv_k, k_gain, rotate(d_keys, cosine, -sine))
    d_q_gain = d_q_gain
    dqkv_b = jnp.concatenate(
        [
            dquery_raw.astype(BF).reshape(total, QH * DH),
            dkey_raw.astype(BF).reshape(total, KVH * DH),
            dvalue_b,
        ],
        axis=1,
    )
    grad_qkv = scatter_plain(outer(normed_b, dqkv_b))
    d_normed = dot_last(dqkv_b, w_qkv)
    d_source, d_attn_gain = rms_back(source, inv_in, attn_gain, d_normed)
    grad_inputs = (d_middle + d_source).reshape(micro, local, D)

    sums = lax.psum(
        jnp.concatenate([d_attn_gain, d_ffn_gain, d_q_gain, d_k_gain]), ("fsdp", "ctx")
    )

    def own(vector):
        size = vector.shape[0] // count
        return lax.dynamic_slice_in_dim(vector, me * size, size, 0)

    return (
        outputs.reshape(micro, local, D),
        grad_inputs,
        own(sums[:D]),
        grad_qkv[:, : QH * DH].astype(F32),
        grad_qkv[:, QH * DH : (QH + KVH) * DH].astype(F32),
        grad_qkv[:, (QH + KVH) * DH :].astype(F32),
        own(sums[2 * D : 2 * D + DH]),
        own(sums[2 * D + DH :]),
        grad_output.astype(F32),
        own(sums[D : 2 * D]),
        grad_gate.astype(F32),
        grad_up.astype(F32),
        grad_down.astype(F32),
    )


def solution(mesh):
    rows = P(None, ("fsdp", "ctx"), None)
    tree = P(None, "fsdp", None)
    vector = P("fsdp")
    weight = P("fsdp", None)
    in_specs = (
        rows,
        P(None, ("fsdp", "ctx")),
        tree,
        tree,
        vector,
        weight,
        weight,
        weight,
        vector,
        vector,
        weight,
        vector,
        weight,
        weight,
        weight,
        rows,
    )
    out_specs = (
        rows,
        rows,
        vector,
        weight,
        weight,
        weight,
        vector,
        vector,
        weight,
        vector,
        weight,
        weight,
        weight,
    )
    return jax.shard_map(body, mesh=mesh, in_specs=in_specs, out_specs=out_specs, check_vma=False)
```

time: 2340 us -> 1710 us (0.73)
  waiting for transfers between devices: 1640 us -> 868 us
  local copies, waits for them, and re-layouts: 66.5 us -> 199 us
  matrix products: 444 us -> 365 us
  other arithmetic: 99.1 us -> 168 us
  starting transfers between devices: 1.92 us -> 37.5 us
    reduce_scatter x11 -> x7, waiting for transfers between devices: 739 us -> 119 us  [the longest x2 119 us: scatter_plain(): lax.psum_scatter(gradient.astype(BF), 'fsdp', scatter_dimension=0, tiled=...]
    ppermute x0 -> x41, waiting for transfers between devices: none -> 390 us  [swap(): return lax.ppermute(value, 'fsdp', [(i, i ^ bits) for i in range(count)])]
    all_gather x11 -> x7, waiting for transfers between devices: 543 us -> 241 us  [the longest x2 116 us: spread_columns(): return lax.all_gather(result, 'ctx', axis=0, tiled=True)]
    psum x1, waiting for transfers between devices: 352 us -> 117 us  [scatter_plain(): return lax.psum(piece, 'ctx')]
    dynamic_update_slice x0 -> x27, local copies, waits for them, and re-layouts: none -> 71.4 us  [the longest x8 41.7 us: spread_columns(): lax.dynamic_update_slice(result, got.reshape(rows // depth, high, 1, unit...]
    dot_general x31 -> x20, matrix products: 303 us -> 264 us  [the longest x5 95.1 us: mat(): return jnp.dot(left, right, preferred_element_type=F32)]
    ppermute x0 -> x41, starting transfers between devices: none -> 36.7 us  [swap(): return lax.ppermute(value, 'fsdp', [(i, i ^ bits) for i in range(count)])]
    dot_general x14 -> x5, matrix products: 123 us -> 86.8 us  [dot_last(): lax.dot_general(left, right, (((1,), (1,)), ((), ())), preferred_element_...]
  transfers between devices with their start and end apart: 23 -> 56, of which waited for: 21 -> 23; matrix products, arithmetic and copies ran while one was open for 17% -> 31% of each run, Pallas kernels for 0% -> 0%
where the time goes in v1:
time: 1710 us; the launch traced here: 1700 us
  waiting for transfers between devices  868 us (51%)
  matrix products  365 us (21%)
  local copies, waits for them, and re-layouts  199 us (12%)
  other arithmetic  168 us (10%)
  blocking collectives  43.5 us (3%)
  starting transfers between devices  37.5 us (2%)
    ppermute x41, waiting for transfers between devices, swap(): return lax.ppermute(value, 'fsdp', [(i, i ^ bits) for i in range(count)])  390 us
    reduce_scatter x2, waiting for transfers between devices, scatter_plain(): lax.psum_scatter(gradient.astype(BF), 'fsdp', scatter_dimension=0, tiled=...  119 us
    psum x1, waiting for transfers between devices, scatter_plain(): return lax.psum(piece, 'ctx')  117 us
    all_gather x2, waiting for transfers between devices, spread_columns(): return lax.all_gather(result, 'ctx', axis=0, tiled=True)  116 us
    dot_general x5, matrix products, mat(): return jnp.dot(left, right, preferred_element_type=F32)  95.1 us
    dot_general x5, matrix products, dot_last(): lax.dot_general(left, right, (((1,), (1,)), ((), ())), preferred_element_...  86.8 us
    dot_general x5, matrix products, outer(): lax.dot_general(left, right, (((0,), (0,)), ((), ())), preferred_element_...  85.1 us
    all_gather x1, waiting for transfers between devices, body(): lax.all_gather(jnp.concatenate([w_query, w_key, w_value], axis=1), 'fsdp'...  80 us
  transfers between devices with their start and end apart: 56, of which 23 were waited for; matrix products, arithmetic and copies ran while one was open for 31% of the time, Pallas kernels for 0%

profile of v1, /device:TPU:0, one launch (start us, length us, event | category | flops | bytes accessed | tf_op | source)
XLA Modules:
  0.0 1697.6 jit_solution(2197660594951123018)
XLA Ops:
  23.2 80.0 %all-gather.8.cloned.1.call-done = bf16[2048,4096]{1,0:T(8,128)(2,1)} async-done(((bf16[256,4096]{1,0:T(8,128)(2,1)}), bf16[2048,4096]{1,0:T(8,128)(2,1)}) %all-gather.8.cloned.1.call-update) | async-done | bytes 16777232 | tf_op jit(solution)/shard_map/all_gather | solution.py:237
  103.2 14.3 fusion.158
  183.6 13.9 collective-permute-done.8
  200.3 13.3 collective-permute-done.7
  245.3 45.2 %all-gather.12.cloned.1.call-done = bf16[1024,2048]{1,0:T(8,128)(2,1)} async-done(((bf16[256,2048]{1,0:T(8,128)(2,1)}), bf16[1024,2048]{1,0:T(8,128)(2,1)}) %all-gather.12.cloned.1.call-update) | async-done | bytes 4194320 | tf_op jit(solution)/shard_map/all_gather | solution.py:276
  372.6 14.7 collective-permute-done.11
  387.8 16.3 collective-permute-done.12
  425.3 13.4 collective-permute-done.13
  449.9 22.2 %fusion.63 = f32[2048,1536]{1,0:T(8,128)} fusion(bf16[1536,2048]{1,0:T(8,128)(2,1)} %constant_dynamic-update-slice_fusion, bf16[512,2048]{1,0:T(8,128)(2,1)} %collective-permute-done.28, bf16[512,2048]{1,0:T(8,128)(2,1)} %collective-permute-done.27, bf16[512,2048]{1,0:T(8,128)(2,1)} %collective-permute-done.26, bf16[512,2048]{1,0:T(8,128)(2,1)} %bitcast.32), kind=kOutput, calls=%fused_computation.135 | convolution fusion | flops 12918456320 | bytes 27262976 | tf_op jit(solution)/shard_map/dot_general | solution.py:27
  472.1 21.6 %fusion.150 = f32[2048,1536]{1,0:T(8,128)} fusion(bf16[2048,1536]{0,1:T(8,128)(2,1)} %constant_dynamic-update-slice_fusion.2, bf16[512,2048]{1,0:T(8,128)(2,1)} %collective-permute-done.5, bf16[512,2048]{1,0:T(8,128)(2,1)} %collective-permute-done.4, bf16[512,2048]{1,0:T(8,128)(2,1)} %collective-permute-done.3, ...), kind=kOutput, calls=%fused_computation.325 | convolution fusion | flops 12918456320 | bytes 27262976 | tf_op jit(solution)/shard_map/dot_general | solution.py:23
  493.7 29.6 %multiply_convert_fusion.1 = (bf16[2048,1536]{1,0:T(8,128)(2,1)}, bf16[2048,1536]{1,0:T(8,128)(2,1)}, bf16[2048,1536]{1,0:T(8,128)(2,1)}) fusion(f32[2048,1536]{1,0:T(8,128)} %fusion.63, f32[2048,1536]{1,0:T(8,128)} %fusion.150, bf16[2048,1536]{0,1:T(8,128)(2,1)} %constant_dynamic-update-slice_fusion.10, bf16[512,2048]{1,0:T(8,128)(2,1)} %collective-permute-done.5, ...), kind=kOutput, calls=%fused_computation.20 | convolution fusion | flops 12965642240 | bytes 58720256 | tf_op jit(solution)/shard_map/dot_general | solution.py:23
  523.3 19.9 %fusion.163 = f32[2048,2048]{1,0:T(8,128)} fusion(bf16[2048,1536]{1,0:T(8,128)(2,1)} %get-tuple-element.24, bf16[2048,1536]{0,1:T(8,128)(2,1)} %constant_dynamic-update-slice_fusion.2), kind=kOutput, calls=%fused_computation.338 | convolution fusion | flops 12884901888 | bytes 29360128 | tf_op jit(solution)/shard_map/dot_general | solution.py:27
  543.2 24.2 %fusion.161 = (bf16[2048,2048]{1,0:T(8,128)(2,1)}, f32[2048,2048]{1,0:T(8,128)}) fusion(f32[2048,2048]{1,0:T(8,128)} %fusion.163, bf16[2048,1536]{1,0:T(8,128)(2,1)} %get-tuple-element.23, bf16[2048,1536]{0,1:T(8,128)(2,1)} %constant_dynamic-update-slice_fusion.10), kind=kOutput, calls=%fused_computation.336 | convolution fusion | flops 12893290496 | bytes 54525952 | tf_op jit(solution)/shard_map/dot_general | solution.py:27
  570.7 19.6 %fusion.162 = (bf16[2048,2048]{1,0:T(8,128)(2,1)S(1)}, f32[2048,2048]{1,0:T(8,128)}) fusion(bf16[2048,1536]{1,0:T(8,128)(2,1)} %get-tuple-element.25, bf16[1536,2048]{1,0:T(8,128)(2,1)} %constant_dynamic-update-slice_fusion), kind=kOutput, calls=%fused_computation.337 | convolution fusion | flops 12889096192 | bytes 37748736 | tf_op jit(solution)/shard_map/dot_general | solution.py:23
  599.6 43.2 %collective-permute-done.31 = bf16[512,2048]{1,0:T(8,128)(2,1)S(1)} collective-permute-done((bf16[512,2048]{1,0:T(8,128)(2,1)S(1)}, bf16[512,2048]{1,0:T(8,128)(2,1)S(1)}, u32[]{:S(2)}, u32[]{:S(2)}) %collective-permute-start.31) | collective-permute-done | bytes 2097184 | tf_op jit(solution)/shard_map/ppermute | solution.py:36
  647.3 39.6 %collective-permute-done.25 = bf16[512,2048]{1,0:T(8,128)(2,1)S(1)} collective-permute-done((bf16[512,2048]{1,0:T(8,128)(2,1)S(1)}, bf16[512,2048]{1,0:T(8,128)(2,1)S(1)}, u32[]{:S(2)}, u32[]{:S(2)}) %collective-permute-start.25) | collective-permute-done | bytes 2097184 | tf_op jit(solution)/shard_map/ppermute | solution.py:36
  702.3 10.9 fusion.3
  723.3 11.7 fusion.5
  751.1 15.5 fusion
  806.5 20.8 %fusion.62 = f32[1536,2048]{1,0:T(8,128)} fusion(bf16[2048,1536]{1,0:T(8,128)(2,1)} %get-tuple-element.25, bf16[512,2048]{1,0:T(8,128)(2,1)} %collective-permute-done.28, bf16[512,2048]{1,0:T(8,128)(2,1)} %collective-permute-done.27, bf16[512,2048]{1,0:T(8,128)(2,1)} %collective-permute-done.26, bf16[512,2048]{1,0:T(8,128)(2,1)} %bitcast.32), kind=kOutput, calls=%fused_computation.134 | convolution fusion | flops 12918456320 | bytes 27262976 | tf_op jit(solution)/shard_map/dot_general | solution.py:31
  832.1 67.9 %collective-permute-done.40 = bf16[768,2048]{1,0:T(8,128)(2,1)} collective-permute-done((bf16[768,2048]{1,0:T(8,128)(2,1)S(1)}, bf16[768,2048]{1,0:T(8,128)(2,1)}, u32[]{:S(2)}, u32[]{:S(2)}) %collective-permute-start.40) | collective-permute-done | bytes 3145760 | tf_op jit(solution)/shard_map/ppermute | solution.py:36
  906.9 20.2 %fusion.148 = f32[2048,1536]{1,0:T(8,128)} fusion(bf16[2048,1536]{1,0:T(8,128)(2,1)} %get-tuple-element.24, bf16[512,2048]{1,0:T(8,128)(2,1)} %collective-permute-done.5, bf16[512,2048]{1,0:T(8,128)(2,1)} %collective-permute-done.4, bf16[512,2048]{1,0:T(8,128)(2,1)} %collective-permute-done.3, bf16[512,2048]{1,0:T(8,128)(2,1)S(1)} %copy-done.38), kind=kOutput, calls=%fused_computation.323 | convolution fusion | flops 12918456320 | bytes 27262976 | tf_op jit(solution)/shard_map/dot_general | solution.py:31
  932.0 66.9 %collective-permute-done.36 = bf16[1024,1536]{1,0:T(8,128)(2,1)} collective-permute-done((bf16[1024,1536]{1,0:T(8,128)(2,1)S(1)}, bf16[1024,1536]{1,0:T(8,128)(2,1)}, u32[]{:S(2)}, u32[]{:S(2)}) %collective-permute-start.36) | collective-permute-done | bytes 3145760 | tf_op jit(solution)/shard_map/ppermute | solution.py:36
  1006.0 20.2 %fusion.149 = f32[2048,1536]{1,0:T(8,128)} fusion(bf16[2048,1536]{1,0:T(8,128)(2,1)} %get-tuple-element.23, bf16[512,2048]{1,0:T(8,128)(2,1)} %collective-permute-done.5, bf16[512,2048]{1,0:T(8,128)(2,1)} %collective-permute-done.4, bf16[512,2048]{1,0:T(8,128)(2,1)} %collective-permute-done.3, bf16[512,2048]{1,0:T(8,128)(2,1)S(1)} %copy-done.39), kind=kOutput, calls=%fused_computation.324 | convolution fusion | flops 12918456320 | bytes 27262976 | tf_op jit(solution)/shard_map/dot_general | solution.py:31
  1031.2 65.9 %collective-permute-done.32 = bf16[1024,1536]{1,0:T(8,128)(2,1)S(1)} collective-permute-done((bf16[1024,1536]{1,0:T(8,128)(2,1)S(1)}, bf16[1024,1536]{1,0:T(8,128)(2,1)S(1)}, u32[]{:S(2)}, u32[]{:S(2)}) %collective-permute-start.32) | collective-permute-done | bytes 3145760 | tf_op jit(solution)/shard_map/ppermute | solution.py:36
  1173.8 15.1 convolution_convert_fusion
  1247.5 118.8 %reduce-scatter.12.cloned.1.call-done = bf16[256,4096]{1,0:T(8,128)(2,1)} async-done(((bf16[2048,4096]{1,0:T(8,128)(2,1)}), bf16[256,4096]{1,0:T(8,128)(2,1)}) %reduce-scatter.12.cloned.1.call-update) | async-done | bytes 2097168 | tf_op jit(solution)/shard_map/reduce_scatter | solution.py:200
  1366.4 15.7 multiply_reduce_fusion.1
  1382.1 43.5 %psum.21 = f32[4352]{0:T(1024)S(1)} all-reduce(f32[4352]{0:T(1024)S(1)} %pad_maximum_fusion.20), channel_id=1, replica_groups=mesh['fsdp'=8,'ctx'=4] {'fsdp','ctx'}, use_global_device_ids=true, to_apply=%region_38.39 | all-reduce | flops 4352 | bytes 34816 | tf_op jit(solution)/shard_map/psum | solution.py:367
  1440.0 56.7 %all-gather.18.cloned.1.call-done = bf16[256,6144]{1,0:T(8,128)(2,1)} async-done(((bf16[64,6144]{1,0:T(8,128)(2,1)}), bf16[256,6144]{1,0:T(8,128)(2,1)}) %all-gather.18.cloned.1.call-update) | async-done | bytes 3145744 | tf_op jit(solution)/shard_map/all_gather | solution.py:190
  1502.0 58.9 %all-gather.16.cloned.1.call-done = bf16[256,6144]{1,0:T(8,128)(2,1)} async-done(((bf16[64,6144]{1,0:T(8,128)(2,1)}), bf16[256,6144]{1,0:T(8,128)(2,1)}) %all-gather.16.cloned.1.call-update) | async-done | bytes 3145744 | tf_op jit(solution)/shard_map/all_gather | solution.py:190
  1566.3 117.2 %all-reduce.3.cloned.1.call-done = (bf16[256,4096]{1,0:T(8,128)(2,1)}, bf16[256,2048]{1,0:T(8,128)(2,1)}) async-done(((bf16[256,4096]{1,0:T(8,128)(2,1)}, bf16[256,2048]{1,0:T(8,128)(2,1)}), (bf16[256,4096]{1,0:T(8,128)(2,1)}, bf16[256,2048]{1,0:T(8,128)(2,1)})) %all-reduce.3.cloned.1.call-update) | async-done | bytes 3145744 | tf_op jit(solution)/shard_map/psum | solution.py:201
  (512 shorter events, 524.7 us)
Async XLA Ops:
  7.2 96.0 %all-gather.8.cloned.1.call-start = ((), (), s32[]{:S(2)}) async-start(), calls=%async_computation.7 | async-start | bytes 18874368 | tf_op jit(solution)/shard_map/all_gather | solution.py:237
  10.5 223.1 %all-gather.10.cloned.1.call-start = ((), (), s32[]{:S(2)}) async-start(), calls=%async_computation.8 | async-start | bytes 5242880 | tf_op jit(solution)/shard_map/all_gather | solution.py:276
  128.2 162.4 %all-gather.12.cloned.1.call-start = ((), (), s32[]{:S(2)}) async-start(), calls=%async_computation.9 | async-start | bytes 5242880 | tf_op jit(solution)/shard_map/all_gather | solution.py:276
  129.4 222.1 %all-gather.14.cloned.1.call-start = ((), (), s32[]{:S(2)}) async-start(), calls=%async_computation.10 | async-start | bytes 9437184 | tf_op jit(solution)/shard_map/all_gather | solution.py:240
  130.0 1030.0 %reduce-scatter.8.cloned.1.call-start = ((), (), s32[]{:S(2)}) async-start(), calls=%async_computation.11 | async-start | bytes 5242880 | tf_op jit(solution)/shard_map/reduce_scatter | solution.py:334
  143.1 55.3 %collective-permute-start.15 = (bf16[256,1536]{0,1:T(8,128)(2,1)}, bf16[256,1536]{0,1:T(8,128)(2,1)S(1)}, u32[]{:S(2)}, u32[]{:S(2)}) collective-permute-start(bf16[256,1536]{0,1:T(8,128)(2,1)} %bitcast.29), channel_id=1, source_target_pairs={{0,8},{4,12},{8,0},{12,4},{16,24},{20,28},{24,16},{28,20},{1,9},{5... | collective-permute-start | bytes 2359304 | tf_op jit(solution)/shard_map/ppermute | solution.py:36
  145.1 52.4 %collective-permute-start.8 = (bf16[256,1536]{0,1:T(8,128)(2,1)}, bf16[256,1536]{0,1:T(8,128)(2,1)}, u32[]{:S(2)}, u32[]{:S(2)}) collective-permute-start(bf16[256,1536]{0,1:T(8,128)(2,1)} %bitcast.25), channel_id=1, source_target_pairs={{0,8},{4,12},{8,0},{12,4},{16,24},{20,28},{24,16},{28,20},{1,9},{5... | collective-permute-start | bytes 2359304 | tf_op jit(solution)/shard_map/ppermute | solution.py:36
  182.7 167.0 %collective-permute-start.18 = (bf16[256,1536]{0,1:T(8,128)(2,1)}, bf16[256,1536]{0,1:T(8,128)(2,1)}, u32[]{:S(2)}, u32[]{:S(2)}) collective-permute-start(bf16[256,1536]{0,1:T(8,128)(2,1)} %bitcast.27), channel_id=1, source_target_pairs={{0,16},{4,20},{8,24},{12,28},{16,0},{20,4},{24,8},{28,12},{1,17},{... | collective-permute-start | bytes 2359304 | tf_op jit(solution)/shard_map/ppermute | solution.py:36
  198.4 163.0 %collective-permute-start.10 = (bf16[256,1536]{0,1:T(8,128)(2,1)}, bf16[256,1536]{0,1:T(8,128)(2,1)}, u32[]{:S(2)}, u32[]{:S(2)}) collective-permute-start(bf16[256,1536]{0,1:T(8,128)(2,1)} %bitcast.22), channel_id=1, source_target_pairs={{0,16},{4,20},{8,24},{12,28},{16,0},{20,4},{24,8},{28,12},{1,17},{... | collective-permute-start | bytes 2359304 | tf_op jit(solution)/shard_map/ppermute | solution.py:36
  213.6 226.1 %collective-permute-start.22 = (bf16[768,2048]{1,0:T(8,128)(2,1)}, bf16[768,2048]{1,0:T(8,128)(2,1)}, u32[]{:S(2)}, u32[]{:S(2)}) collective-permute-start(bf16[768,2048]{1,0:T(8,128)(2,1)} %param.30), channel_id=1, source_target_pairs={{0,16},{4,20},{8,24},{12,28},{16,0},{20,4},{24,8},{28,12},{1,17},{... | collective-permute-start | bytes 9437192 | tf_op jit(solution)/shard_map/ppermute | solution.py:36
  215.4 171.9 %collective-permute-start.27 = (bf16[512,2048]{1,0:T(8,128)(2,1)}, bf16[512,2048]{1,0:T(8,128)(2,1)}, u32[]{:S(2)}, u32[]{:S(2)}) collective-permute-start(bf16[512,2048]{1,0:T(8,128)(2,1)} %bitcast.32), channel_id=1, source_target_pairs={{0,8},{4,12},{8,0},{12,4},{16,24},{20,28},{24,16},{28,20},{1,9},{5... | collective-permute-start | bytes 6291464 | tf_op jit(solution)/shard_map/ppermute | solution.py:36
  217.6 144.3 %collective-permute-start.19 = (bf16[256,1536]{0,1:T(8,128)(2,1)}, bf16[256,1536]{0,1:T(8,128)(2,1)}, u32[]{:S(2)}, u32[]{:S(2)}) collective-permute-start(bf16[256,1536]{0,1:T(8,128)(2,1)} %collective-permute-done.14), channel_id=1, source_target_pairs={{0,16},{4,20},{8,24},{12,28},{16,0},{20,4},{24,8},{28,12},{1,17},{... | collective-permute-start | bytes 2359304 | tf_op jit(solution)/shard_map/ppermute | solution.py:36
  370.4 49.6 %collective-permute-start.21 = (bf16[256,1536]{0,1:T(8,128)(2,1)S(1)}, bf16[256,1536]{0,1:T(8,128)(2,1)S(1)}, u32[]{:S(2)}, u32[]{:S(2)}) collective-permute-start(bf16[256,1536]{0,1:T(8,128)(2,1)S(1)} %copy-done.53), channel_id=1, source_target_pairs={{0,16},{4,20},{8,24},{12,28},{16,0},{20,4},{24,8},{28,12},{1,17},{... | collective-permute-start | bytes 2359304 | tf_op jit(solution)/shard_map/ppermute | solution.py:36
  387.3 62.7 %collective-permute-start.26 = (bf16[512,2048]{1,0:T(8,128)(2,1)}, bf16[512,2048]{1,0:T(8,128)(2,1)}, u32[]{:S(2)}, u32[]{:S(2)}) collective-permute-start(bf16[512,2048]{1,0:T(8,128)(2,1)} %bitcast.32), channel_id=1, source_target_pairs={{0,4},{4,0},{8,12},{12,8},{16,20},{20,16},{24,28},{28,24},{1,5},{5... | collective-permute-start | bytes 6291464 | tf_op jit(solution)/shard_map/ppermute | solution.py:36
  387.3 62.7 %collective-permute-start.28 = (bf16[512,2048]{1,0:T(8,128)(2,1)}, bf16[512,2048]{1,0:T(8,128)(2,1)}, u32[]{:S(2)}, u32[]{:S(2)}) collective-permute-start(bf16[512,2048]{1,0:T(8,128)(2,1)} %collective-permute-done.27), channel_id=1, source_target_pairs={{0,4},{4,0},{8,12},{12,8},{16,20},{20,16},{24,28},{28,24},{1,5},{5... | collective-permute-start | bytes 6291464 | tf_op jit(solution)/shard_map/ppermute | solution.py:36
  404.1 45.8 %collective-permute-start.4 = (bf16[512,2048]{1,0:T(8,128)(2,1)S(1)}, bf16[512,2048]{1,0:T(8,128)(2,1)}, u32[]{:S(2)}, u32[]{:S(2)}) collective-permute-start(bf16[512,2048]{1,0:T(8,128)(2,1)S(1)} %multiply_convert_fusion.3), channel_id=1, source_target_pairs={{0,8},{4,12},{8,0},{12,4},{16,24},{20,28},{24,16},{28,20},{1,9},{5... | collective-permute-start | bytes 6291464 | tf_op jit(solution)/shard_map/ppermute | solution.py:36
  594.3 48.6 %collective-permute-start.31 = (bf16[512,2048]{1,0:T(8,128)(2,1)S(1)}, bf16[512,2048]{1,0:T(8,128)(2,1)S(1)}, u32[]{:S(2)}, u32[]{:S(2)}) collective-permute-start(bf16[512,2048]{1,0:T(8,128)(2,1)S(1)} %fusion.14), channel_id=1, source_target_pairs={{0,8},{4,12},{8,0},{12,4},{16,24},{20,28},{24,16},{28,20},{1,9},{5... | collective-permute-start | bytes 6291464 | tf_op jit(solution)/shard_map/ppermute | solution.py:36
  595.8 51.5 %collective-permute-start.23 = (bf16[512,2048]{1,0:T(8,128)(2,1)S(1)}, bf16[512,2048]{1,0:T(8,128)(2,1)S(1)}, u32[]{:S(2)}, u32[]{:S(2)}) collective-permute-start(bf16[512,2048]{1,0:T(8,128)(2,1)S(1)} %get-tuple-element.32), channel_id=1, source_target_pairs={{0,4},{4,0},{8,12},{12,8},{16,20},{20,16},{24,28},{28,24},{1,5},{5... | collective-permute-start | bytes 6291464 | tf_op jit(solution)/shard_map/ppermute | solution.py:36
  599.0 88.0 %collective-permute-start.25 = (bf16[512,2048]{1,0:T(8,128)(2,1)S(1)}, bf16[512,2048]{1,0:T(8,128)(2,1)S(1)}, u32[]{:S(2)}, u32[]{:S(2)}) collective-permute-start(bf16[512,2048]{1,0:T(8,128)(2,1)S(1)} %fusion.16), channel_id=1, source_target_pairs={{0,8},{4,12},{8,0},{12,4},{16,24},{20,28},{24,16},{28,20},{1,9},{5... | collective-permute-start | bytes 6291464 | tf_op jit(solution)/shard_map/ppermute | solution.py:36
  749.1 412.2 %reduce-scatter.10.cloned.1.call-start = ((), (), s32[]{:S(2)}) async-start(), calls=%async_computation.12 | async-start | bytes 5242880 | tf_op jit(solution)/shard_map/reduce_scatter | solution.py:334
  806.4 382.6 %reduce-scatter.20.cloned.1.call-start = ((), (), s32[]{:S(2)}) async-start(), calls=%async_computation.19 | async-start | bytes 3932160 | tf_op jit(solution)/shard_map/reduce_scatter | solution.py:195
  830.5 69.5 %collective-permute-start.40 = (bf16[768,2048]{1,0:T(8,128)(2,1)S(1)}, bf16[768,2048]{1,0:T(8,128)(2,1)}, u32[]{:S(2)}, u32[]{:S(2)}) collective-permute-start(bf16[768,2048]{1,0:T(8,128)(2,1)S(1)} %dynamic-slice_convert_fusion), channel_id=1, source_target_pairs={{0,16},{4,20},{8,24},{12,28},{16,0},{20,4},{24,8},{28,12},{1,17},{... | collective-permute-start | bytes 9437192 | tf_op jit(solution)/shard_map/ppermute | solution.py:36
  906.9 282.7 %reduce-scatter.18.cloned.1.call-start = ((), (), s32[]{:S(2)}) async-start(), calls=%async_computation.17 | async-start | bytes 3932160 | tf_op jit(solution)/shard_map/reduce_scatter | solution.py:174
  930.3 68.6 %collective-permute-start.36 = (bf16[1024,1536]{1,0:T(8,128)(2,1)S(1)}, bf16[1024,1536]{1,0:T(8,128)(2,1)}, u32[]{:S(2)}, u32[]{:S(2)}) collective-permute-start(bf16[1024,1536]{1,0:T(8,128)(2,1)S(1)} %dynamic-slice_convert_fusion.1), channel_id=1, source_target_pairs={{0,16},{4,20},{8,24},{12,28},{16,0},{20,4},{24,8},{28,12},{1,17},{... | collective-permute-start | bytes 9437192 | tf_op jit(solution)/shard_map/ppermute | solution.py:36
  1005.6 212.3 %reduce-scatter.16.cloned.1.call-start = ((), (), s32[]{:S(2)}) async-start(), calls=%async_computation.15 | async-start | bytes 3932160 | tf_op jit(solution)/shard_map/reduce_scatter | solution.py:174
  1029.4 67.7 %collective-permute-start.32 = (bf16[1024,1536]{1,0:T(8,128)(2,1)S(1)}, bf16[1024,1536]{1,0:T(8,128)(2,1)S(1)}, u32[]{:S(2)}, u32[]{:S(2)}) collective-permute-start(bf16[1024,1536]{1,0:T(8,128)(2,1)S(1)} %dynamic-slice_convert_fusion.2), channel_id=1, source_target_pairs={{0,16},{4,20},{8,24},{12,28},{16,0},{20,4},{24,8},{28,12},{1,17},{... | collective-permute-start | bytes 9437192 | tf_op jit(solution)/shard_map/ppermute | solution.py:36
  1102.9 144.6 %reduce-scatter.14.cloned.1.call-start = ((), (), s32[]{:S(2)}) async-start(), calls=%async_computation.14 | async-start | bytes 9437184 | tf_op jit(solution)/shard_map/reduce_scatter | solution.py:200
  1112.1 254.2 %reduce-scatter.12.cloned.1.call-start = ((), (), s32[]{:S(2)}) async-start(), calls=%async_computation.13 | async-start | bytes 18874368 | tf_op jit(solution)/shard_map/reduce_scatter | solution.py:200
  1188.9 245.7 %all-gather.20.cloned.1.call-start = ((), (), s32[]{:S(2)}) async-start(), calls=%async_computation.20 | async-start | bytes 3932160 | tf_op jit(solution)/shard_map/all_gather | solution.py:196
  1189.5 307.2 %all-gather.18.cloned.1.call-start = ((), (), s32[]{:S(2)}) async-start(), calls=%async_computation.18 | async-start | bytes 3932160 | tf_op jit(solution)/shard_map/all_gather | solution.py:190
  1217.8 343.1 %all-gather.16.cloned.1.call-start = ((), (), s32[]{:S(2)}) async-start(), calls=%async_computation.16 | async-start | bytes 3932160 | tf_op jit(solution)/shard_map/all_gather | solution.py:190
  1247.4 436.0 %all-reduce.3.cloned.1.call-start = ((), (), s32[]{:S(2)}) async-start(), calls=%async_computation.21 | async-start | bytes 6291456 | tf_op jit(solution)/shard_map/psum | solution.py:201
  (116 other events, 2652.2 us)
Sparse Core Ops, SparseCore 0:
  10.6 92.5 all-gather.7
  128.3 80.7 all-gather.9
  211.2 79.2 all-gather.11
  292.3 55.1 all-gather.13
  749.2 75.3 reduce-scatter.7
  827.4 77.2 reduce-scatter.9
  907.0 60.7 reduce-scatter.19
  1005.7 58.7 reduce-scatter.17
  1103.0 58.7 reduce-scatter.15
  1165.1 81.2 reduce-scatter.13
  1250.4 115.8 reduce-scatter.11
  1367.8 64.4 all-gather.19
  1434.6 62.0 all-gather.17
  1498.8 62.1 all-gather.15
  1563.4 120.0 all-reduce.2

commit v2 on v1

v2 whole, which is shorter than its diff:
```python
import functools

import jax
import jax.numpy as jnp
from jax import lax
from jax.experimental import pallas as pl
from jax.experimental.pallas import tpu as pltpu
from jax.sharding import PartitionSpec as P

D = 2048
QH = 16
KVH = 8
DH = 128
FF = 6144
BLK = 128
GROUP = QH // KVH
SCALE = DH ** (-0.5)
LOG2E = 1.4426950408889634

EPS = 1e-06
BASE = 1000000.0
BF = jnp.bfloat16
F32 = jnp.float32
BLOCK = 512
COST = 100.0
LOW = 0.01
VMEM = 60 * 1024 * 1024


def mat(left, right):
    return jnp.dot(left, right, preferred_element_type=F32)


def dot_last(left, right):
    return lax.dot_general(left, right, (((1,), (1,)), ((), ())), preferred_element_type=F32)


def outer(left, right):
    return lax.dot_general(left, right, (((0,), (0,)), ((), ())), preferred_element_type=F32)


def after(value, *others):
    return lax.optimization_barrier((value,) + others)[0]


def swap(value, bits):
    count = lax.axis_size("fsdp")
    return lax.ppermute(value, "fsdp", [(i, i ^ bits) for i in range(count)])


def inv_rms(values):
    return lax.rsqrt(jnp.mean(values * values, axis=-1, keepdims=True) + EPS)


def rms_back(values, inv, gain, dy):
    product = dy * values
    dv = inv * (gain * dy) - values * (inv * inv * inv) * jnp.mean(
        product * gain, axis=-1, keepdims=True
    )
    return dv, jnp.sum(product * inv, axis=0)


def call(
    kernel,
    name,
    grid,
    in_specs,
    out_specs,
    out_shape,
    flops,
    moved,
    scratch=(),
    aliases=None,
    scalars=0,
    cost=COST,
):
    return pl.pallas_call(
        kernel,
        name=name,
        grid_spec=pltpu.PrefetchScalarGridSpec(
            num_scalar_prefetch=scalars,
            grid=grid,
            in_specs=in_specs,
            out_specs=out_specs,
            scratch_shapes=list(scratch),
        ),
        out_shape=out_shape,
        input_output_aliases=aliases or {},
        compiler_params=pltpu.CompilerParams(vmem_limit_bytes=VMEM),
        cost_estimate=pl.CostEstimate(
            flops=int(flops * cost), bytes_accessed=int(moved * cost), transcendentals=0
        ),
    )


def fixed(shape):
    return pl.BlockSpec(
        shape, lambda *index: tuple(0 for _ in shape), pipeline_mode=pl.Buffered(1)
    )


def project(x, weight, first, cols, cosine, sine, gain, kinds, name):
    rows, depth = x.shape
    width = DH * len(kinds)

    def kernel(x_ref, w_ref, c_ref, s_ref, g_ref, out_ref, raw_ref):
        raw = mat(x_ref[...], w_ref[...])
        raw_ref[...] = raw.astype(BF)
        for index, kind in enumerate(kinds):
            part = raw[:, index * DH : (index + 1) * DH]
            if kind == "r":
                part = part * inv_rms(part) * g_ref[...]
                part = part * c_ref[...] + pltpu.roll(part, DH // 2, 1) * s_ref[...]
            out_ref[:, index * DH : (index + 1) * DH] = part.astype(BF)

    whole = lambda j: (0, 0)
    block = lambda j: (0, j)
    return call(
        kernel,
        name,
        (cols // width,),
        [
            pl.BlockSpec((rows, depth), whole),
            pl.BlockSpec((depth, width), lambda j: (0, j + first // width)),
            pl.BlockSpec((rows, DH), whole),
            pl.BlockSpec((rows, DH), whole),
            pl.BlockSpec((1, DH), whole),
        ],
        [pl.BlockSpec((rows, width), block)] * 2,
        [jax.ShapeDtypeStruct((rows, cols), BF)] * 2,
        2 * rows * depth * cols,
        2 * (rows * depth + depth * cols + 2 * rows * cols),
    )(x, weight, cosine, sine, gain)


def stack_heads(block):
    return jnp.concatenate([block[:, i * DH : (i + 1) * DH] for i in range(GROUP)], axis=0)


def attention(queries, pairs, mask):
    rows = queries.shape[0]
    keys = pairs.shape[0]

    def kernel(q_ref, kv_ref, m_ref, out_ref, inv_ref):
        stacked = stack_heads(q_ref[...])
        scores = dot_last(kv_ref[:, :DH], stacked)
        mask_now = jnp.concatenate([m_ref[...]] * GROUP, axis=1)
        powers = jnp.exp2(scores * (SCALE * LOG2E)) * mask_now
        inv = 1.0 / jnp.sum(powers, axis=0, keepdims=True)
        inv_ref[0] = inv
        out = (outer(kv_ref[:, DH:], powers.astype(BF)) * inv).T
        for index in range(GROUP):
            out_ref[:, index * DH : (index + 1) * DH] = out[
                index * rows : (index + 1) * rows
            ].astype(BF)

    return call(
        kernel,
        "attention",
        (KVH,),
        [
            pl.BlockSpec((rows, GROUP * DH), lambda g: (0, g)),
            pl.BlockSpec((keys, 2 * DH), lambda g: (0, g)),
            pl.BlockSpec((keys, rows), lambda g: (0, 0)),
        ],
        [
            pl.BlockSpec((rows, GROUP * DH), lambda g: (0, g)),
            pl.BlockSpec((1, 1, GROUP * rows), lambda g: (g, 0, 0)),
        ],
        [
            jax.ShapeDtypeStruct((rows, QH * DH), BF),
            jax.ShapeDtypeStruct((KVH, 1, GROUP * rows), F32),
        ],
        4 * QH * rows * keys * DH,
        2 * (2 * rows * QH * DH + 2 * keys * KVH * DH),
    )(queries, pairs, mask)


def head_back(dy, raw, cosine, sine, gain):
    turned = dy * cosine - pltpu.roll(dy, DH // 2, 1) * sine
    inv = inv_rms(raw)
    product = turned * raw
    dv = inv * (gain * turned) - raw * (inv * inv * inv) * jnp.mean(
        product * gain, axis=-1, keepdims=True
    )
    return dv, jnp.sum(product * inv, axis=0, keepdims=True)


def attention_back(queries, raw, pairs, mask, d_out, out, inv, cosine, sine, gain):
    rows = queries.shape[0]
    keys = pairs.shape[0]

    def kernel(
        q_ref, r_ref, kv_ref, m_ref, do_ref, o_ref, inv_ref, c_ref, s_ref, g_ref,
        dq_ref, dkv_ref, dg_ref,
    ):
        stacked = stack_heads(q_ref[...])
        d_stacked = stack_heads(do_ref[...])
        o_stacked = stack_heads(o_ref[...])
        dots = jnp.sum((d_stacked.astype(F32) * o_stacked.astype(F32)).T, axis=0, keepdims=True)
        scores = dot_last(kv_ref[:, :DH], stacked)
        mask_now = jnp.concatenate([m_ref[...]] * GROUP, axis=1)
        probs = jnp.exp2(scores * (SCALE * LOG2E)) * (mask_now * inv_ref[0])
        d_probs = dot_last(kv_ref[:, DH:], d_stacked)
        d_scores = (probs * (d_probs - dots)).astype(BF)
        dkv_ref[:, DH:] = mat(probs.astype(BF), d_stacked).astype(BF)
        dkv_ref[:, :DH] = (mat(d_scores, stacked) * SCALE).astype(BF)
        d_query = outer(d_scores, kv_ref[:, :DH]) * SCALE
        total = jnp.zeros((1, DH), F32)
        for index in range(GROUP):
            part = slice(index * DH, (index + 1) * DH)
            dv, dg = head_back(
                d_query[index * rows : (index + 1) * rows],
                r_ref[:, part].astype(F32),
                c_ref[...],
                s_ref[...],
                g_ref[...],
            )
            dq_ref[:, part] = dv.astype(BF)
            total = total + dg

        @pl.when(pl.program_id(0) == 0)
        def _():
            dg_ref[...] = jnp.zeros_like(dg_ref)

        dg_ref[...] += total

    head = pl.BlockSpec((rows, GROUP * DH), lambda g: (0, g))
    pair = pl.BlockSpec((keys, 2 * DH), lambda g: (0, g))
    whole = lambda shape: pl.BlockSpec(shape, lambda g: (0, 0))
    return call(
        kernel,
        "attention_back",
        (KVH,),
        [
            head,
            head,
            pair,
            whole((keys, rows)),
            head,
            head,
            pl.BlockSpec((1, 1, GROUP * rows), lambda g: (g, 0, 0)),
            whole((rows, DH)),
            whole((rows, DH)),
            whole((1, DH)),
        ],
        [head, pair, whole((1, DH))],
        [
            jax.ShapeDtypeStruct((rows, QH * DH), BF),
            jax.ShapeDtypeStruct((keys, 2 * KVH * DH), BF),
            jax.ShapeDtypeStruct((1, DH), F32),
        ],
        10 * QH * rows * keys * DH,
        2 * (5 * rows * QH * DH + 4 * keys * KVH * DH),
    )(queries, raw, pairs, mask, d_out, out, inv, cosine, sine, gain)


def pair_back(d_pairs, raw, cosine, sine, gain):
    rows, cols = d_pairs.shape

    def kernel(d_ref, r_ref, c_ref, s_ref, g_ref, out_ref, dg_ref):
        total = jnp.zeros((1, DH), F32)
        for index in range(BLOCK // (2 * DH)):
            part = slice(index * 2 * DH, index * 2 * DH + DH)
            rest = slice(index * 2 * DH + DH, (index + 1) * 2 * DH)
            dv, dg = head_back(
                d_ref[:, part].astype(F32),
                r_ref[:, part].astype(F32),
                c_ref[...],
                s_ref[...],
                g_ref[...],
            )
            out_ref[:, part] = dv.astype(BF)
            out_ref[:, rest] = d_ref[:, rest]
            total = total + dg

        @pl.when(pl.program_id(0) == 0)
        def _():
            dg_ref[...] = jnp.zeros_like(dg_ref)

        dg_ref[...] += total

    block = pl.BlockSpec((rows, BLOCK), lambda j: (0, j))
    whole = lambda shape: pl.BlockSpec(shape, lambda j: (0, 0))
    return call(
        kernel,
        "pair_back",
        (cols // BLOCK,),
        [block, block, whole((rows, DH)), whole((rows, DH)), whole((1, DH))],
        [block, whole((1, DH))],
        [jax.ShapeDtypeStruct((rows, cols), BF), jax.ShapeDtypeStruct((1, DH), F32)],
        20 * rows * cols,
        6 * rows * cols,
        cost=LOW,
    )(d_pairs, raw, cosine, sine, gain)


def feed(mids, cots, pieces, w_down, index, total, earlier, place):
    rows, depth = mids[0].shape
    parts = len(mids)
    hidden = w_down.shape[0]
    count = len(pieces)
    unit = place[1]
    steps = hidden // unit
    block_rows = depth // (4 * count)

    def kernel(me_ref, *refs):
        mid_refs = refs[:parts]
        cot_refs = refs[parts : 2 * parts]
        piece_refs = refs[2 * parts : 2 * parts + count]
        wd_ref = refs[2 * parts + count]
        if count > 1:
            act_ref, d_ref, wp_ref = refs[-3:]
            for which in range(4 * count):
                start = pl.multiple_of((me_ref[0] ^ which) * block_rows, block_rows)
                near = which % 4 * block_rows
                wp_ref[pl.ds(start, block_rows), :] = piece_refs[which // 4][
                    near : near + block_rows
                ]
        else:
            act_ref, d_ref = refs[-2:]
            wp_ref = piece_refs[0]
        for part in range(parts):
            now = slice(part * rows, (part + 1) * rows)
            both = mat(mid_refs[part][...], wp_ref[...])
            gate = both[:, :unit]
            up = both[:, unit:]
            d_act = dot_last(cot_refs[part][...], wd_ref[...])
            sig = 1.0 / (1.0 + jnp.exp2(gate * (-LOG2E)))
            silu = gate * sig
            act_ref[now] = (silu * up).astype(BF)
            d_ref[now, unit:] = (d_act * silu).astype(BF)
            d_ref[now, :unit] = (d_act * up * (sig + silu * (1.0 - sig))).astype(BF)

    def piece_spec(far):
        return pl.BlockSpec((pieces[0].shape[0], 2 * unit), lambda j, me: (0, j ^ far))

    out_specs = [
        pl.BlockSpec((parts * rows, unit), lambda j, me: (index, j)),
        pl.BlockSpec((parts * rows, 2 * unit), lambda j, me: (index, j)),
    ]
    out_shape = [
        jax.ShapeDtypeStruct((total * parts * rows, hidden), BF),
        jax.ShapeDtypeStruct((total * parts * rows, 2 * hidden), BF),
    ]
    if count > 1:
        out_specs.append(pl.BlockSpec((depth, 2 * unit), lambda j, me: (0, j)))
        out_shape.append(jax.ShapeDtypeStruct((depth, 2 * hidden), BF))
    before = 1 + 2 * parts + count + 1
    return call(
        kernel,
        "feed",
        (steps,),
        [fixed((rows, depth))] * parts
        + [
            pl.BlockSpec(
                (rows, depth), lambda j, me: (index, 0), pipeline_mode=pl.Buffered(1)
            )
        ]
        * parts
        + [piece_spec(which) for which in range(count)]
        + [pl.BlockSpec((unit, depth), lambda j, me: (j, 0))]
        + [pl.BlockSpec(memory_space=pl.ANY)] * len(earlier),
        out_specs,
        out_shape,
        6 * parts * rows * depth * hidden,
        2 * (2 * parts * rows * depth + 3 * depth * hidden + 3 * parts * rows * hidden),
        aliases={before + i: i for i in range(len(earlier))},
        scalars=1,
    )(place[0], *mids, *cots, *pieces, w_down, *earlier)


def feed_out(left, weight, index, parts, transposed, name):
    depth = left.shape[1]
    cols = weight.shape[0] if transposed else weight.shape[1]
    rows = parts[1]

    def kernel(a_ref, w_ref, *outs):
        for part in range(parts[0]):
            now = a_ref[part * rows : (part + 1) * rows]
            result = dot_last(now, w_ref[...]) if transposed else mat(now, w_ref[...])
            outs[part][...] = result.astype(BF)

    return call(
        kernel,
        name,
        (cols // BLOCK,),
        [
            pl.BlockSpec((parts[0] * rows, depth), lambda j: (index, 0)),
            pl.BlockSpec((BLOCK, depth), lambda j: (j, 0))
            if transposed
            else pl.BlockSpec((depth, BLOCK), lambda j: (0, j)),
        ],
        [pl.BlockSpec((rows, BLOCK), lambda j: (0, j))] * parts[0],
        [jax.ShapeDtypeStruct((rows, cols), BF)] * parts[0],
        2 * parts[0] * rows * depth * cols,
        2 * (parts[0] * rows * (depth + cols) + depth * cols),
    )(left, weight)


def weight_terms(lefts, block, starts, width, size, rights, step, added, chunked, name, turn=0, cost=COST):
    depth = sum(left.shape[0] for left in lefts)
    cols = rights[0][0].shape[1]
    size_right = depth // len(rights)
    blocks = starts.shape[0]
    rows = blocks * size
    steps = cols // step
    nl, nr = len(lefts), len(rights)

    def kernel(block_ref, start_ref, *refs):
        left_refs = refs[:nl]
        right_refs = refs[nl : nl + nr]
        add_refs = refs[nl + nr : nl + nr + len(added)]
        out_ref, turned = refs[-2:]

        @pl.when(pl.program_id(0) == 0)
        def _():
            for which in range(blocks):
                start = pl.multiple_of(start_ref[which], 128)
                at = 0
                for ref in left_refs:
                    turned[which * size : (which + 1) * size, at : at + ref.shape[0]] = ref[
                        :, pl.ds(start, size)
                    ].T
                    at += ref.shape[0]

        right = [ref[...] for ref in right_refs]
        right = right[0] if nr == 1 else jnp.concatenate(right, axis=0)
        result = mat(turned[...], right)
        for ref in add_refs:
            result = result + ref[...].astype(F32)
        out_ref[...] = result.astype(BF)

    if chunked:
        out_spec = pl.BlockSpec((rows, step), lambda j, b, s: (j ^ turn, 0))
        shape = (steps * rows, step)
    else:
        out_spec = pl.BlockSpec((rows, step), lambda j, b, s: (0, j))
        shape = (rows, cols)
    return call(
        kernel,
        name,
        (steps,),
        [
            pl.BlockSpec(
                (left.shape[0], width), lambda j, b, s: (0, b[0]), pipeline_mode=pl.Buffered(1)
            )
            for left in lefts
        ]
        + [
            pl.BlockSpec((size_right, step), functools.partial(lambda at, j, b, s: (at, j), at))
            for right, at in rights
        ]
        + [out_spec] * len(added),
        out_spec,
        jax.ShapeDtypeStruct(shape, BF),
        2 * rows * depth * cols,
        2 * (rows * depth + depth * cols + (1 + len(added)) * rows * cols),
        scratch=[pltpu.VMEM((rows, depth), BF)],
        scalars=2,
        cost=cost,
    )(block, starts, *lefts, *[right for right, at in rights], *added)


def column_parts(gate, up, high, slots, number):
    rows, cols = gate.shape
    unit = cols // (4 * high)

    def kernel(slot_ref, gate_ref, up_ref, out_ref):
        out_ref[:, :unit] = gate_ref[...]
        out_ref[:, unit:] = up_ref[...]

    block = pl.BlockSpec((rows, unit), lambda i, j, at: (0, (at[0] ^ j) * 4 + at[i + 1]))
    return call(
        kernel,
        "column_parts",
        (number, high),
        [block, block],
        pl.BlockSpec((rows, 2 * unit), lambda i, j, at: (i, j)),
        jax.ShapeDtypeStruct((number * rows, 2 * unit * high), BF),
        0,
        8 * number * rows * unit * high,
        scalars=1,
    )(slots, gate, up)


def lay_pairs(chunks, place, high, unit):
    depth = len(chunks)
    rows = chunks[0].shape[1]
    cols = 4 * high * unit
    size = rows // 4

    def kernel(place_ref, *refs):
        gate_ref, up_ref = refs[-2:]
        for which in range(depth):
            chunk = place_ref[0] ^ which
            far = place_ref[1] ^ (chunk // 2)
            for near in range(4):
                start = pl.multiple_of((far * 4 + (place_ref[2] ^ near)) * unit, 128)

                @pl.when(chunk % 2 == 0)
                def _():
                    gate_ref[:, pl.ds(start, unit)] = refs[which][near].astype(F32)

                @pl.when(chunk % 2 == 1)
                def _():
                    up_ref[:, pl.ds(start, unit)] = refs[which][near].astype(F32)

    return call(
        kernel,
        "lay_pairs",
        (4,),
        [pl.BlockSpec((4, size, unit), lambda i, at: (0, i, 0))] * depth,
        [pl.BlockSpec((size, cols), lambda i, at: (i, 0))] * 2,
        [jax.ShapeDtypeStruct((rows, cols), F32)] * 2,
        0,
        12 * rows * cols,
        scalars=1,
    )(place, *chunks)


def visibility(parent, layout, offset, count):
    blocks = parent.shape[0]
    ident = jnp.arange(blocks, dtype=jnp.int32)
    current = ident
    reach = ident[:, None] == ident[None, :]
    for step in range(blocks):
        current = jnp.sum(jnp.where(current[:, None] == ident[None, :], parent[None, :], 0), axis=1)
        reach = reach | (current[:, None] == ident[None, :])
    place = (layout[:, None] == ident[None, :]).astype(jnp.int32)
    picked = jnp.sum(place[:, :, None] * reach.astype(jnp.int32)[None, :, :], axis=1)
    row_reach = jnp.sum(picked[:, None, :] * place[None, :, :], axis=2) > 0
    mine = lax.dynamic_slice_in_dim(row_reach, offset // BLK, count // BLK, 0).T
    spread = jnp.broadcast_to(
        mine[:, None, :, None], (blocks, BLK, count // BLK, BLK)
    ).reshape(blocks * BLK, count)
    query_rows = offset + lax.broadcasted_iota(jnp.int32, (blocks * BLK, count), 1)
    key_rows = lax.broadcasted_iota(jnp.int32, (blocks * BLK, count), 0)
    same = query_rows // BLK == key_rows // BLK
    return (spread & (jnp.logical_not(same) | (key_rows <= query_rows))).astype(F32)


def gather_small(vector, me):
    count = lax.axis_size("fsdp")
    buffer = jnp.zeros((count,) + vector.shape, vector.dtype)
    buffer = lax.dynamic_update_index_in_dim(buffer, vector, me, 0)
    step = 1
    while step < count:
        buffer = buffer + swap(buffer, step)
        step *= 2
    return buffer


def gather_rows(shard):
    high = lax.axis_size("fsdp") // 4
    return jnp.concatenate(
        [shard] + [swap(shard, 4 * far) for far in range(1, high)], axis=0
    )


def group_rows(rows):
    from_x = swap(rows, 2)
    from_core = swap(rows, 1)
    from_both = swap(from_x, 1)
    return [rows, from_core, from_x, from_both]


def group_sum(parts):
    for_x = (parts[2].astype(F32) + swap(parts[3], 1).astype(F32)).astype(BF)
    got_x = swap(for_x, 2)
    got_core = swap(parts[1], 1)
    return parts[0].astype(F32) + got_core.astype(F32) + got_x.astype(F32)


def group_half(parts):
    got = swap(jnp.concatenate([parts[1], parts[3]], axis=0), 1)
    rows = parts[0].shape[0]
    own = parts[0].astype(F32) + got[:rows].astype(F32)
    return own, (parts[2].astype(F32) + got[rows:].astype(F32)).astype(BF)


def gather_ctx(chunk):
    count = lax.axis_size("ctx")
    return [chunk] + [
        lax.ppermute(chunk, "ctx", [(i, i ^ step) for i in range(count)])
        for step in range(1, count)
    ]


def scatter_ctx(array):
    return lax.psum_scatter(array, "ctx", scatter_dimension=0, tiled=True)


def spread_pairs(piece, me, unit):
    high = lax.axis_size("fsdp") // 4
    slot = me % 4
    rows = piece.shape[0] // 4
    near = [lax.dynamic_slice_in_dim(piece, (slot ^ which) * rows, rows, 0) for which in range(4)]
    near = [near[0]] + [swap(near[which], which) for which in range(1, 4)]
    chunks = gather_ctx(jnp.stack(near))
    place = jnp.stack([lax.axis_index("ctx"), me // 4, slot])
    return lay_pairs(chunks, place, high, unit)


def fold(value, bits, *others):
    for bit in bits:
        half = value.shape[0] // 2
        got = swap(value[half:], bit)
        keep = after(value[:half], *others) if others else value[:half]
        value = (keep.astype(F32) + got.astype(F32)).astype(BF)
        others = ()
    return value


def order_of(bits):
    order = [0]
    for bit in reversed(bits):
        order = order + [entry ^ bit for entry in order]
    return order


def body(
    inputs,
    depths,
    parents,
    layout,
    gain_attn,
    w_query,
    w_key,
    w_value,
    query_gain,
    key_gain,
    w_output,
    gain_ffn,
    w_gate,
    w_up,
    w_down,
    cotangent,
):
    me = lax.axis_index("fsdp")
    micro, local, _ = inputs.shape
    total = micro * local
    offset = lax.axis_index("ctx") * local
    count = lax.axis_size("fsdp")
    shard = D // count
    head_shard = DH // count

    def rows_of(index):
        return slice(index * local, (index + 1) * local)

    pair_shard = jnp.stack(
        [w_key.reshape(shard, KVH, DH), w_value.reshape(shard, KVH, DH)], axis=2
    ).reshape(shard, 2 * KVH * DH)
    gains = gather_small(jnp.concatenate([gain_attn, gain_ffn, query_gain, key_gain]), me)
    w_qkv = lax.all_gather(
        jnp.concatenate([w_query, pair_shard], axis=1), "fsdp", axis=0, tiled=True
    )
    attn_gain = gains[:, :shard].reshape(D).astype(F32)
    ffn_gain = gains[:, shard : 2 * shard].reshape(D).astype(F32)
    q_gain = gains[:, 2 * shard : 2 * shard + head_shard].reshape(1, DH).astype(F32)
    k_gain = gains[:, 2 * shard + head_shard :].reshape(1, DH).astype(F32)

    unit = FF // count
    high = count // 4
    slot = me % 4
    parts_x = column_parts(w_gate, w_up, high, jnp.stack([me // 4, slot ^ 2, slot ^ 3]), 2)
    parts_own = column_parts(
        after(w_gate, parts_x), w_up, high, jnp.stack([me // 4, slot, slot ^ 1]), 2
    )
    got_x = swap(after(parts_x, w_qkv, gains), 2)
    wd = gather_rows(after(w_down, w_qkv, gains))
    out_pieces = [w_output]
    out_order = [0]
    bit = count // 2
    while bit > 2:
        out_pieces += [swap(piece, bit) for piece in out_pieces]
        out_order += [entry ^ bit for entry in out_order]
        bit //= 2
    out_block = jnp.concatenate(out_pieces, axis=0)
    cot_all = cotangent.reshape(total, D)

    freq = jnp.power(BASE, -jnp.arange(DH // 2, dtype=F32) / (DH // 2))
    angle = depths.reshape(total).astype(F32)[:, None] * freq[None, :]
    cosine = jnp.cos(angle)
    sine = jnp.sin(angle)
    cosine = jnp.concatenate([cosine, cosine], axis=1)
    sine = jnp.concatenate([-sine, sine], axis=1)
    masks = [
        visibility(parents[index, 0], layout[index, 0], offset, local) for index in range(micro)
    ]

    source = inputs.reshape(total, D).astype(F32)
    inv_in = inv_rms(source)
    normed_b = (source * inv_in * attn_gain).astype(BF)
    normed_now = after(normed_b, parts_own, out_block, *masks)
    got_core = swap(jnp.concatenate([parts_own[shard:], got_x[shard:]], axis=0), 1)
    pairs, pairs_raw = project(
        normed_now,
        w_qkv,
        QH * DH,
        2 * KVH * DH,
        cosine,
        sine,
        k_gain,
        "r-r-",
        "project_pairs",
    )
    everyone = [
        lax.all_gather(pairs[rows_of(index)], "ctx", axis=0, tiled=True) for index in range(micro)
    ]
    near = jnp.concatenate(
        [parts_own[:shard], got_core[:shard], got_x[:shard], got_core[shard:]], axis=0
    )
    queries, queries_raw = project(
        after(normed_b, pairs, near, wd),
        w_qkv,
        0,
        QH * DH,
        cosine,
        sine,
        q_gain,
        "rrrr",
        "project_queries",
    )
    pieces = [near] + [swap(near, 4 * far) for far in range(1, high)]
    for bit, earlier in ((2, queries), (1, everyone[0])):
        out_block = jnp.concatenate([out_block, swap(after(out_block, earlier), bit)], axis=0)
        out_order = out_order + [entry ^ bit for entry in out_order]
    w_out = jnp.zeros((QH * DH, D), BF)
    for index, entry in enumerate(out_order):
        w_out = lax.dynamic_update_slice_in_dim(
            w_out, out_block[index * shard : (index + 1) * shard], (me ^ entry) * shard, 0
        )
    cot_x = swap(after(cot_all, queries), 2)
    cot_rows = [cot_all, swap(cot_all, 1), cot_x, swap(cot_x, 1)]

    attended = []
    inverses = []
    middles = []
    mid_inverses = []
    mid_rows = []
    token = queries
    for index in range(micro):
        part = rows_of(index)
        if index == 0:
            token = (token,)
        else:
            token = (token, cot_x)
        out, inverse = attention(after(queries[part], *token), everyone[index], masks[index])
        middle = source[part] + mat(after(out, w_out) if index == 0 else out, w_out)
        inv_mid = inv_rms(middle)
        mid_b = (middle * inv_mid * ffn_gain).astype(BF)
        attended.append(out)
        inverses.append(inverse)
        middles.append(middle)
        mid_inverses.append(inv_mid)
        mid_rows.append(group_rows(mid_b))
        token = mid_b

    mid_pieces = [piece for rows in mid_rows for piece in rows]
    cot_pieces = [(piece, index) for index in range(micro) for piece in cot_rows]
    zero = jnp.zeros((1,), jnp.int32)

    def down_terms(act, far, added, cost=COST):
        return weight_terms(
            [act],
            zero + far,
            zero,
            unit,
            unit,
            cot_pieces,
            BLOCK,
            added,
            False,
            "grad_down",
            cost=cost,
        )

    def pair_terms(first, far, added, cost=COST):
        return weight_terms(
            [first] + mid_pieces[1:],
            ((me // 4) ^ far)[None],
            zero,
            D // high,
            D // high,
            [(dgu_b, 0)],
            unit,
            added,
            True,
            "grad_pair",
            2 * far,
            cost,
        )

    d_mids = []
    sent_pair = []
    me_array = me[None]
    act_b, dgu_b, wgu = feed(
        [after(mid_rows[0][0], token)] + mid_rows[0][1:],
        cot_rows,
        pieces,
        wd,
        0,
        micro,
        (),
        (me_array, unit),
    )
    for index in range(micro):
        if index:
            act_b, dgu_b = feed(
                [after(mid_rows[index][0], token)] + mid_rows[index][1:],
                cot_rows,
                [wgu],
                wd,
                index,
                micro,
                (act_b, dgu_b),
                (me_array, unit),
            )
        if index == micro - 1:
            token = act_b
            for far in range(1, high):
                sent_pair.append(pair_terms(after(mid_pieces[0], token), far, []))
                token = sent_pair[-1]
            dgu_now = after(dgu_b, token, d_mids[0][1])
        else:
            dgu_now = dgu_b
        parts = feed_out(dgu_now, wgu, index, (4, local), True, "feed_back")
        d_mids.append(group_half(parts))
        token = parts[0]
    got_pair = [swap(piece, 4 * (far + 1)) for far, piece in enumerate(sent_pair)]

    d_middles = []
    d_projs = []
    d_query_parts = []
    d_pair_parts = []
    d_ffn_gain = jnp.zeros((D,), F32)
    d_q_gain = jnp.zeros((1, DH), F32)
    for index in range(micro):
        part = rows_of(index)
        d_mid = d_mids[index][0] + swap(d_mids[index][1], 2).astype(F32)
        d_part, d_gain = rms_back(
            middles[index], mid_inverses[index], ffn_gain, after(d_mid, token)
        )
        d_ffn_gain = d_ffn_gain + d_gain
        d_middle = cotangent[index].astype(F32) + d_part
        d_proj = d_middle.astype(BF)
        d_attended = dot_last(d_proj, w_out).astype(BF)
        d_query, d_pair, d_gain = attention_back(
            after(queries[part], *[d_mids[later][1] for later in range(index + 1, micro)]),
            queries_raw[part],
            everyone[index],
            masks[index],
            d_attended,
            attended[index],
            inverses[index],
            cosine[part],
            sine[part],
            q_gain,
        )
        d_q_gain = d_q_gain + d_gain
        d_middles.append(d_middle)
        d_projs.append(d_proj)
        d_query_parts.append(d_query)
        d_pair_parts.append(scatter_ctx(d_pair))
        token = d_query
        if index == 0:
            sent_down = []
            for far in range(1, high):
                sent_down.append(down_terms(after(act_b, token), far, []))
                token = sent_down[-1]
            got_down = [swap(piece, 4 * (far + 1)) for far, piece in enumerate(sent_down)]

    d_query_b = jnp.concatenate(d_query_parts, axis=0)
    d_proj_b = jnp.concatenate(d_projs, axis=0)
    attended_b = jnp.concatenate(attended, axis=0)
    bits = [2**i for i in range(count.bit_length() - 1)]
    half_size = count // 2

    def plain_terms(left, right, order, added, name, cost=COST):
        starts = (me ^ jnp.array(order, jnp.int32)) * shard
        return weight_terms(
            [left], zero, starts, D, shard, [(right, 0)], BLOCK, added, False, name, cost=cost
        )

    order = order_of(bits)
    sent_query = plain_terms(after(normed_b, token), d_query_b, order[half_size:], [], "grad_q")
    sent_output = plain_terms(
        after(attended_b, sent_query), d_proj_b, order[half_size:], [], "grad_o"
    )

    outs = []
    token = sent_output
    for index in range(micro):
        parts = feed_out(after(act_b, token), wd, index, (4, local), False, "feed_forward")
        token = parts[0]
        outs.append((middles[index] + group_sum(parts)).astype(BF))
    outputs = jnp.stack(outs)

    own_pair = pair_terms(after(mid_pieces[0], token), 0, got_pair)
    own_down = down_terms(after(act_b, own_pair), 0, got_down, LOW)
    pair_piece = scatter_ctx(own_pair)
    down_piece = scatter_ctx(after(own_down, own_pair))
    own_query = plain_terms(
        after(normed_b, own_down, *d_pair_parts),
        d_query_b,
        order[:half_size],
        [swap(sent_query, 1)],
        "grad_q",
        LOW,
    )
    own_output = plain_terms(
        after(attended_b, own_query),
        d_proj_b,
        order[:half_size],
        [swap(sent_output, 1)],
        "grad_o",
        LOW,
    )

    d_pairs = after(jnp.concatenate(d_pair_parts, axis=0), own_output)
    d_pair_b, d_k_gain = pair_back(d_pairs, pairs_raw, cosine, sine, k_gain)
    sent_kv = plain_terms(normed_b, d_pair_b, order[half_size:], [], "grad_kv", LOW)
    d_normed = dot_last(
        jnp.concatenate([after(d_query_b, sent_kv), d_pair_b], axis=1), w_qkv
    )
    own_kv = plain_terms(
        after(normed_b, d_normed, pair_piece), d_pair_b, order[:half_size], [swap(sent_kv, 1)], "grad_kv"
    )
    d_source, d_attn_gain = rms_back(source, inv_in, attn_gain, after(d_normed, own_kv))
    grad_inputs = jnp.concatenate(d_middles, axis=0) + d_source

    def spread(vector):
        return jnp.pad(vector.reshape(count, -1), ((0, 0), (0, shard - vector.size // count)))

    columns = jnp.stack(
        [
            d_attn_gain.reshape(count, shard),
            d_ffn_gain.reshape(count, shard),
            spread(d_q_gain),
            spread(d_k_gain),
        ],
        axis=2,
    ).astype(BF)
    columns = jnp.pad(columns, ((0, 0), (0, 0), (0, DH - 4))).reshape(D, DH)
    columns = jnp.concatenate(
        [
            lax.dynamic_slice_in_dim(columns, (me ^ entry) * shard, shard, 0)
            for entry in order
        ],
        axis=0,
    )
    columns = fold(columns, bits[:1])
    part_qo = [fold(own, bits[1:2], own_kv) for own in (own_query, own_output)]
    part_qo = fold(jnp.concatenate(part_qo, axis=1), bits[2:])
    part_kv = fold(jnp.concatenate([own_kv, columns], axis=1), bits[1:])

    grad_gate, grad_up = spread_pairs(pair_piece, me, unit)

    def whole(piece):
        return lax.all_gather(piece, "ctx", axis=0, tiled=True).astype(F32)

    grad_down = whole(down_piece)
    both = whole(scatter_ctx(part_qo))
    grad_query, grad_output = both[:, :D], both[:, D:]
    rest = whole(scatter_ctx(part_kv))
    pair_both = rest[:, : 2 * KVH * DH].reshape(shard, KVH, 2, DH)
    grad_key = pair_both[:, :, 0].reshape(shard, KVH * DH)
    grad_value = pair_both[:, :, 1].reshape(shard, KVH * DH)
    sums = rest[:, 2 * KVH * DH :]

    return (
        outputs,
        grad_inputs.reshape(micro, local, D),
        sums[:, 0],
        grad_query,
        grad_key,
        grad_value,
        sums[:head_shard, 2],
        sums[:head_shard, 3],
        grad_output,
        sums[:, 1],
        grad_gate,
        grad_up,
        grad_down,
    )


def solution(mesh):
    rows = P(None, ("fsdp", "ctx"), None)
    tree = P(None, "fsdp", None)
    vector = P("fsdp")
    weight = P("fsdp", None)
    in_specs = (
        rows,
        P(None, ("fsdp", "ctx")),
        tree,
        tree,
        vector,
        weight,
        weight,
        weight,
        vector,
        vector,
        weight,
        vector,
        weight,
        weight,
        weight,
        rows,
    )
    out_specs = (
        rows,
        rows,
        vector,
        weight,
        weight,
        weight,
        vector,
        vector,
        weight,
        vector,
        weight,
        weight,
        weight,
    )
    return jax.shard_map(body, mesh=mesh, in_specs=in_specs, out_specs=out_specs, check_vma=False)
```

time: 1710 us -> 1400 us (0.82)
  Pallas kernels: 0 us -> 339 us
  matrix products: 365 us -> 34.2 us
  waiting for transfers between devices: 868 us -> 757 us
  local copies, waits for them, and re-layouts: 199 us -> 98.7 us
  other arithmetic: 168 us -> 97.2 us
  blocking collectives: 43.5 us -> 0 us
    pallas_call x0 -> x26, Pallas kernels: none -> 339 us  [the longest x10 114 us: weight_terms(): call(kernel, name, (steps,), [pl.BlockSpec((left.shape[0], width), lambda...]
    dot_general x19 -> x0, matrix products: 183 us -> none  [the longest x5 85.1 us: outer(): lax.dot_general(left, right, (((0,), (0,)), ((), ())), preferred_element_...]
    psum x1 -> x0, waiting for transfers between devices: 117 us -> none  [scatter_plain(): return lax.psum(piece, 'ctx')]
    dot_general x5 -> x2, matrix products: 95.1 us -> 12.8 us  [mat(): return jnp.dot(left, right, preferred_element_type=F32)]
    dot_general x5 -> x3, matrix products: 86.8 us -> 21.4 us  [dot_last(): lax.dot_general(left, right, (((1,), (1,)), ((), ())), preferred_element_...]
    ppermute x0 -> x3, waiting for transfers between devices: none -> 56.1 us  [gather_ctx(): lax.ppermute(chunk, 'ctx', [(i, i ^ step) for i in range(count)])]
    reduce_scatter x7 -> x6, waiting for transfers between devices: 119 us -> 62.9 us  [scatter_ctx(): return lax.psum_scatter(array, 'ctx', scatter_dimension=0, tiled=True)]
    dynamic_update_slice x26 -> x8, local copies, waits for them, and re-layouts: 71.3 us -> 17.7 us  [body(): lax.dynamic_update_slice_in_dim(w_out, out_block[index * shard:(index + 1...]
  transfers between devices with their start and end apart: 56 -> 58, of which waited for: 23 -> 25; matrix products, arithmetic and copies ran while one was open for 31% -> 15% of each run, Pallas kernels for 0% -> 25%
where the time goes in v2:
time: 1400 us; the launch traced here: 1380 us
  waiting for transfers between devices  757 us (54%)
  Pallas kernels  339 us (24%)
  local copies, waits for them, and re-layouts  98.7 us (7%)
  other arithmetic  97.2 us (7%)
  matrix products  34.2 us (2%)
  starting transfers between devices  33.8 us (2%)
  between operations  15.8 us (1%)
    ppermute x43, waiting for transfers between devices, swap(): return lax.ppermute(value, 'fsdp', [(i, i ^ bits) for i in range(count)])  434 us
    all_gather x3, waiting for transfers between devices, whole(): return lax.all_gather(piece, 'ctx', axis=0, tiled=True).astype(F32)  125 us
    pallas_call x10, Pallas kernels, weight_terms(): call(kernel, name, (steps,), [pl.BlockSpec((left.shape[0], width), lambda...  114 us
    all_gather x1, waiting for transfers between devices, body(): lax.all_gather(jnp.concatenate([w_query, pair_shard], axis=1), 'fsdp', ax...  65.3 us
    reduce_scatter x6, waiting for transfers between devices, scatter_ctx(): return lax.psum_scatter(array, 'ctx', scatter_dimension=0, tiled=True)  62.9 us
    pallas_call x2, Pallas kernels, feed(): call(kernel, 'feed', (steps,), [fixed((rows, depth))] * parts + [pl.Block...  61.4 us
    pallas_call x4, Pallas kernels, feed_out(): call(kernel, name, (cols // BLOCK,), [pl.BlockSpec((parts[0] * rows, dept...  57.6 us
    ppermute x3, waiting for transfers between devices, gather_ctx(): lax.ppermute(chunk, 'ctx', [(i, i ^ step) for i in range(count)])  56.1 us
  transfers between devices with their start and end apart: 58, of which 25 were waited for; matrix products, arithmetic and copies ran while one was open for 15% of the time, Pallas kernels for 25%

profile of v2, /device:TPU:0, one launch (start us, length us, event | category | flops | bytes accessed | tf_op | source)
XLA Modules:
  0.0 1375.7 jit_solution(4292461998838947158)
XLA Ops:
  35.3 24.1 %collective-permute-done.2 = bf16[8,544]{1,0:T(8,128)(2,1)S(1)} collective-permute-done((bf16[8,544]{1,0:T(8,128)(2,1)S(1)}, bf16[8,544]{1,0:T(8,128)(2,1)S(1)}, u32[]{:S(2)}, u32[]{:S(2)}) %collective-permute-start.2) | collective-permute-done | bytes 8736 | tf_op jit(solution)/shard_map/ppermute | solution.py:48
  59.4 65.3 %all-gather.7.cloned.1.call-done.w_ref = bf16[2048,4096]{1,0:T(8,128)(2,1)} async-done(((bf16[256,4096]{1,0:T(8,128)(2,1)}), bf16[2048,4096]{1,0:T(8,128)(2,1)}) %all-gather.7.cloned.1.call-update) | async-done | bytes 16777232 | tf_op jit(solution)/shard_map/all_gather | solution.py:655
  153.7 41.6 %collective-permute-done.4 = bf16[512,3072]{1,0:T(8,128)(2,1)} collective-permute-done((bf16[512,3072]{1,0:T(8,128)(2,1)}, bf16[512,3072]{1,0:T(8,128)(2,1)}, u32[]{:S(2)}, u32[]{:S(2)}) %collective-permute-start.4) | collective-permute-done | bytes 3145760 | tf_op jit(solution)/shard_map/ppermute | solution.py:48
  232.6 13.8 project_queries.1
  256.0 39.3 %collective-permute-done.7 = bf16[512,2048]{1,0:T(8,128)(2,1)} collective-permute-done((bf16[512,2048]{1,0:T(8,128)(2,1)}, bf16[512,2048]{1,0:T(8,128)(2,1)}, u32[]{:S(2)}, u32[]{:S(2)}) %collective-permute-start.7) | collective-permute-done | bytes 2097184 | tf_op jit(solution)/shard_map/ppermute | solution.py:48
  308.4 29.8 %collective-permute-done.9.refs_6_.refs_3_.refs_7_ = bf16[512,2048]{1,0:T(8,128)(2,1)} collective-permute-done((bf16[512,2048]{1,0:T(8,128)(2,1)}, bf16[512,2048]{1,0:T(8,128)(2,1)}, u32[]{:S(2)}, u32[]{:S(2)}) %collective-permute-start.9) | collective-permute-done | bytes 2097184 | tf_op jit(solution)/shard_map/ppermute | solution.py:48
  361.8 13.9 %all-gather.11.cloned.1.call-done.kv_ref = bf16[1024,2048]{1,0:T(8,128)(2,1)} async-done(((bf16[256,2048]{1,0:T(8,128)(2,1)}), bf16[1024,2048]{1,0:T(8,128)(2,1)}) %all-gather.11.cloned.1.call-update) | async-done | bytes 4194320 | tf_op jit(solution)/shard_map/all_gather | solution.py:709
  401.5 18.5 %collective-permute-done.17.refs_2_.refs_6_ = bf16[256,2048]{1,0:T(8,128)(2,1)} collective-permute-done((bf16[256,2048]{1,0:T(8,128)(2,1)}, bf16[256,2048]{1,0:T(8,128)(2,1)}, u32[]{:S(2)}, u32[]{:S(2)}) %collective-permute-start.17) | collective-permute-done | bytes 1048608 | tf_op jit(solution)/shard_map/ppermute | solution.py:48
  420.0 32.9 %feed.2 = (bf16[2048,1536]{1,0:T(8,128)(2,1)}, bf16[2048,3072]{1,0:T(8,128)(2,1)}, bf16[2048,3072]{1,0:T(8,128)(2,1)}) custom-call(s32[1]{0:T(128)} %bitcast.13.me_ref, bf16[256,2048]{1,0:T(8,128)(2,1)} %multiply_convert_fusion.1.refs_0_, bf16[256,2048]{1,0:T(8,128)(2,1)} %collective-permute-done.10.refs_1_, ...), custom_call_target="tpu_custom_call" | custom-call | flops 1932735283200 | bytes 3670016000 | tf_op jit(solution)/shard_map/feed/pallas_call | solution.py:350
  452.9 18.5 %feed_back.2 = (bf16[256,2048]{1,0:T(8,128)(2,1)}, bf16[256,2048]{1,0:T(8,128)(2,1)}, bf16[256,2048]{1,0:T(8,128)(2,1)}, bf16[256,2048]{1,0:T(8,128)(2,1)}) custom-call(bf16[2048,3072]{1,0:T(8,128)(2,1)} %get-tuple-element.102.a_ref.refs_11_, bf16[2048,3072]{1,0:T(8,128)(2,1)} %get-tuple-element.103.w_ref.refs_8_), custom_call_target="tpu_custom_call" | custom-call | flops 1288490188800 | bytes 2306867200 | tf_op jit(solution)/shard_map/feed_back/pallas_call | solution.py:384
  475.0 28.5 %feed.3 = (bf16[2048,1536]{1,0:T(8,128)(2,1)}, bf16[2048,3072]{1,0:T(8,128)(2,1)}) custom-call(s32[1]{0:T(128)} %bitcast.13.me_ref, bf16[256,2048]{1,0:T(8,128)(2,1)} %multiply_convert_fusion.refs_0_.refs_4_, bf16[256,2048]{1,0:T(8,128)(2,1)} %collective-permute-done.16.refs_1_.refs_5_, ...), custom_call_target="tpu_custom_call", output_to_operand_aliasing={{0}: (11, {}), {1}: (12, {})} | custom-call | flops 1932735283200 | bytes 3670016000 | tf_op jit(solution)/shard_map/feed/pallas_call | solution.py:350
  503.5 19.7 %grad_pair.2 = bf16[4096,768]{1,0:T(8,128)(2,1)} custom-call(s32[1]{0:T(128)} %bitcast.17.block_ref, s32[1]{0:T(128)} %constant.139.clone.1.start_ref.block_ref, bf16[256,2048]{1,0:T(8,128)(2,1)} %multiply_convert_fusion.1.refs_0_, bf16[256,2048]{1,0:T(8,128)(2,1)} %collective-permute-done.10.refs_1_, bf16[256,2048]{1,0:T(8,128)(2,1)} %collective-permute-done.11.refs_2_, ...), custom_call_target="tpu_custom_call" | custom-call | flops 1288490188800 | bytes 2306867200 | tf_op jit(solution)/shard_map/grad_pair/pallas_call | solution.py:440
  528.6 18.4 %feed_back.3 = (bf16[256,2048]{1,0:T(8,128)(2,1)}, bf16[256,2048]{1,0:T(8,128)(2,1)}, bf16[256,2048]{1,0:T(8,128)(2,1)}, bf16[256,2048]{1,0:T(8,128)(2,1)}) custom-call(bf16[2048,3072]{1,0:T(8,128)(2,1)} %get-tuple-element.114.refs_8_.a_ref, bf16[2048,3072]{1,0:T(8,128)(2,1)} %get-tuple-element.103.w_ref.refs_8_), custom_call_target="tpu_custom_call" | custom-call | flops 1288490188800 | bytes 2306867200 | tf_op jit(solution)/shard_map/feed_back/pallas_call | solution.py:384
  566.6 19.5 %attention_back.2 = (bf16[256,2048]{1,0:T(8,128)(2,1)}, bf16[1024,2048]{1,0:T(8,128)(2,1)}, f32[1,128]{1,0:T(1,128)}) custom-call(bf16[256,2048]{1,0:T(8,128)(2,1)} %get-tuple-element.119.q_ref, bf16[256,2048]{1,0:T(8,128)(2,1)} %get-tuple-element.187.r_ref, bf16[1024,2048]{1,0:T(8,128)(2,1)} %all-gather.9.cloned.1.call-done.kv_ref, ...), custom_call_target="tpu_custom_call" | custom-call | flops 536870912000 | bytes 1363148800 | tf_op jit(solution)/shard_map/attention_back/pallas_call | solution.py:231
  586.1 12.8 grad_down.2
  612.7 19.5 %attention_back.3 = (bf16[256,2048]{1,0:T(8,128)(2,1)}, bf16[1024,2048]{1,0:T(8,128)(2,1)}, f32[1,128]{1,0:T(1,128)}) custom-call(bf16[256,2048]{1,0:T(8,128)(2,1)} %get-tuple-element.99.q_ref, bf16[256,2048]{1,0:T(8,128)(2,1)} %get-tuple-element.188.r_ref, bf16[1024,2048]{1,0:T(8,128)(2,1)} %all-gather.11.cloned.1.call-done.kv_ref, ...), custom_call_target="tpu_custom_call" | custom-call | flops 536870912000 | bytes 1363148800 | tf_op jit(solution)/shard_map/attention_back/pallas_call | solution.py:231
  660.0 10.4 feed_forward.3
  670.5 20.8 %grad_pair.3 = bf16[4096,768]{1,0:T(8,128)(2,1)} custom-call(s32[1]{0:T(128)} %bitcast.2.block_ref, s32[1]{0:T(128)} %constant.139.clone.1.start_ref.block_ref, bf16[256,2048]{1,0:T(8,128)(2,1)} %multiply_convert_fusion.1.refs_0_, bf16[256,2048]{1,0:T(8,128)(2,1)} %collective-permute-done.10.refs_1_, bf16[256,2048]{1,0:T(8,128)(2,1)} %collective-permute-done.11.refs_2_, ...), custom_call_target="tpu_custom_call" | custom-call | flops 1288490188800 | bytes 2936012800 | tf_op jit(solution)/shard_map/grad_pair/pallas_call | solution.py:440
  692.5 69.8 %collective-permute-done.30.refs_9_ = bf16[768,2048]{1,0:T(8,128)(2,1)S(1)} collective-permute-done((bf16[768,2048]{1,0:T(8,128)(2,1)}, bf16[768,2048]{1,0:T(8,128)(2,1)S(1)}, u32[]{:S(2)}, u32[]{:S(2)}) %collective-permute-start.30) | collective-permute-done | bytes 3145760 | tf_op jit(solution)/shard_map/ppermute | solution.py:48
  763.9 12.8 grad_down.3
  810.2 14.7 %fusion = f32[512,2048]{1,0:T(8,128)} fusion(bf16[2048,4096]{1,0:T(8,128)(2,1)} %all-gather.7.cloned.1.call-done.w_ref, bf16[512,2048]{1,0:T(8,128)(2,1)} %get-tuple-element.147.refs_1_, bf16[512,2048]{1,0:T(8,128)(2,1)S(1)} %copy-done.23), kind=kOutput, calls=%fused_computation.6 | convolution fusion | flops 8598323200 | bytes 25165824 | tf_op jit(solution)/shard_map/dot_general | solution.py:35
  824.9 33.1 %reduce-scatter.11.cloned.1.call-done = bf16[1024,768]{1,0:T(8,128)(2,1)} async-done(((bf16[4096,768]{1,0:T(8,128)(2,1)}), bf16[1024,768]{1,0:T(8,128)(2,1)}) %reduce-scatter.11.cloned.1.call-update) | async-done | bytes 1572880 | tf_op jit(solution)/shard_map/reduce_scatter | solution.py:591
  878.8 43.5 %collective-permute-done.37 = bf16[512,2048]{1,0:T(8,128)(2,1)S(1)} collective-permute-done((bf16[512,2048]{1,0:T(8,128)(2,1)S(1)}, bf16[512,2048]{1,0:T(8,128)(2,1)S(1)}, u32[]{:S(2)}, u32[]{:S(2)}) %collective-permute-start.37) | collective-permute-done | bytes 2097184 | tf_op jit(solution)/shard_map/ppermute | solution.py:48
  923.2 46.8 %collective-permute-done.35 = bf16[512,2176]{1,0:T(8,128)(2,1)S(1)} collective-permute-done((bf16[512,2176]{1,0:T(8,128)(2,1)S(1)}, bf16[512,2176]{1,0:T(8,128)(2,1)S(1)}, u32[]{:S(2)}, u32[]{:S(2)}) %collective-permute-start.35) | collective-permute-done | bytes 2228256 | tf_op jit(solution)/shard_map/ppermute | solution.py:48
  972.3 42.2 %collective-permute-done.38 = bf16[512,2048]{1,0:T(8,128)(2,1)S(1)} collective-permute-done((bf16[512,2048]{1,0:T(8,128)(2,1)S(1)}, bf16[512,2048]{1,0:T(8,128)(2,1)S(1)}, u32[]{:S(2)}, u32[]{:S(2)}) %collective-permute-start.38) | collective-permute-done | bytes 2097184 | tf_op jit(solution)/shard_map/ppermute | solution.py:48
  1020.4 44.5 %collective-permute-done.39 = bf16[256,4096]{1,0:T(8,128)(2,1)} collective-permute-done((bf16[256,4096]{1,0:T(8,128)(2,1)}, bf16[256,4096]{1,0:T(8,128)(2,1)}, u32[]{:S(2)}, u32[]{:S(2)}) %collective-permute-start.39) | collective-permute-done | bytes 2097184 | tf_op jit(solution)/shard_map/ppermute | solution.py:48
  1084.3 29.7 %reduce-scatter.15.cloned.1.call-done = bf16[64,4096]{1,0:T(8,128)(2,1)} async-done(((bf16[256,4096]{1,0:T(8,128)(2,1)}), bf16[64,4096]{1,0:T(8,128)(2,1)}) %reduce-scatter.15.cloned.1.call-update) | async-done | bytes 524304 | tf_op jit(solution)/shard_map/reduce_scatter | solution.py:591
  1118.3 14.6 %collective-permute-done.41 = bf16[256,768]{1,0:T(8,128)(2,1)S(1)} collective-permute-done((bf16[256,768]{1,0:T(8,128)(2,1)}, bf16[256,768]{1,0:T(8,128)(2,1)S(1)}, u32[]{:S(2)}, u32[]{:S(2)}) %collective-permute-start.41) | collective-permute-done | bytes 393248 | tf_op jit(solution)/shard_map/ppermute | solution.py:48
  1150.3 73.7 %all-gather.17.cloned.1.call-done = bf16[768,2048]{1,0:T(8,128)(2,1)} async-done(((bf16[192,2048]{1,0:T(8,128)(2,1)}), bf16[768,2048]{1,0:T(8,128)(2,1)}) %all-gather.17.cloned.1.call-update) | async-done | bytes 3145744 | tf_op jit(solution)/shard_map/all_gather | solution.py:961
  1232.9 17.0 %collective-permute-done.43.refs_1_ = bf16[4,256,768]{2,1,0:T(8,128)(2,1)} collective-permute-done((bf16[4,256,768]{2,1,0:T(8,128)(2,1)}, bf16[4,256,768]{2,1,0:T(8,128)(2,1)}, u32[]{:S(2)}, u32[]{:S(2)}) %collective-permute-start.43) | collective-permute-done | bytes 1572896 | tf_op jit(solution)/shard_map/ppermute | solution.py:585
  1250.0 39.1 %collective-permute-done.45.refs_3_ = bf16[4,256,768]{2,1,0:T(8,128)(2,1)} collective-permute-done((bf16[4,256,768]{2,1,0:T(8,128)(2,1)}, bf16[4,256,768]{2,1,0:T(8,128)(2,1)}, u32[]{:S(2)}, u32[]{:S(2)}) %collective-permute-start.45) | collective-permute-done | bytes 1572896 | tf_op jit(solution)/shard_map/ppermute | solution.py:585
  1322.0 42.3 %all-gather.15.cloned.1.call-done = bf16[256,4096]{1,0:T(8,128)(2,1)} async-done(((bf16[64,4096]{1,0:T(8,128)(2,1)}), bf16[256,4096]{1,0:T(8,128)(2,1)}) %all-gather.15.cloned.1.call-update) | async-done | bytes 2097168 | tf_op jit(solution)/shard_map/all_gather | solution.py:961
  (474 shorter events, 389.0 us)
Async XLA Ops:
  7.2 117.5 %all-gather.7.cloned.1.call-start = ((), (), s32[]{:S(2)}) async-start(), calls=%async_computation.6 | async-start | bytes 18874368 | tf_op jit(solution)/shard_map/all_gather | solution.py:655
  17.7 281.1 %all-gather.9.cloned.1.call-start = ((), (), s32[]{:S(2)}) async-start(), calls=%async_computation.7 | async-start | bytes 5242880 | tf_op jit(solution)/shard_map/all_gather | solution.py:709
  19.0 130.9 %collective-permute-start.3 = (bf16[256,2048]{1,0:T(8,128)(2,1)S(1)}, bf16[256,2048]{1,0:T(8,128)(2,1)}, u32[]{:S(2)}, u32[]{:S(2)}) collective-permute-start(bf16[256,2048]{1,0:T(8,128)(2,1)S(1)} %copy-done.25), channel_id=1, source_target_pairs={{0,16},{4,20},{8,24},{12,28},{16,0},{20,4},{24,8},{28,12},{1,17},{... | collective-permute-start | bytes 3145736 | tf_op jit(solution)/shard_map/ppermute | solution.py:48
  124.7 70.6 %collective-permute-start.4 = (bf16[512,3072]{1,0:T(8,128)(2,1)}, bf16[512,3072]{1,0:T(8,128)(2,1)}, u32[]{:S(2)}, u32[]{:S(2)}) collective-permute-start(bf16[512,3072]{1,0:T(8,128)(2,1)} %column_parts.2), channel_id=1, source_target_pairs={{0,8},{4,12},{8,0},{12,4},{16,24},{20,28},{24,16},{28,20},{1,9},{5... | collective-permute-start | bytes 9437192 | tf_op jit(solution)/shard_map/ppermute | solution.py:48
  152.3 70.3 %collective-permute-start.6 = (bf16[768,2048]{1,0:T(8,128)(2,1)}, bf16[768,2048]{1,0:T(8,128)(2,1)}, u32[]{:S(2)}, u32[]{:S(2)}) collective-permute-start(bf16[768,2048]{1,0:T(8,128)(2,1)} %param.36), channel_id=1, source_target_pairs={{0,16},{4,20},{8,24},{12,28},{16,0},{20,4},{24,8},{28,12},{1,17},{... | collective-permute-start | bytes 9437192 | tf_op jit(solution)/shard_map/ppermute | solution.py:48
  213.7 162.0 %all-gather.11.cloned.1.call-start = ((), (), s32[]{:S(2)}) async-start(), calls=%async_computation.8 | async-start | bytes 5242880 | tf_op jit(solution)/shard_map/all_gather | solution.py:709
  246.9 147.8 %collective-permute-start.13 = (bf16[512,2048]{1,0:T(8,128)(2,1)}, bf16[512,2048]{1,0:T(8,128)(2,1)}, u32[]{:S(2)}, u32[]{:S(2)}) collective-permute-start(bf16[512,2048]{1,0:T(8,128)(2,1)} %bitcast.15.refs_4_.refs_1_.refs_5_), channel_id=1, source_target_pairs={{0,4},{4,0},{8,12},{12,8},{16,20},{20,16},{24,28},{28,24},{1,5},{5... | collective-permute-start | bytes 6291464 | tf_op jit(solution)/shard_map/ppermute | solution.py:48
  250.7 525.9 %reduce-scatter.7.cloned.1.call-start = ((), (), s32[]{:S(2)}) async-start(), calls=%async_computation.9 | async-start | bytes 5242880 | tf_op jit(solution)/shard_map/reduce_scatter | solution.py:591
  250.8 169.2 %collective-permute-start.15 = (bf16[1024,3072]{1,0:T(8,128)(2,1)}, bf16[1024,3072]{1,0:T(8,128)(2,1)}, u32[]{:S(2)}, u32[]{:S(2)}) collective-permute-start(bf16[1024,3072]{1,0:T(8,128)(2,1)} %pad_maximum_fusion.refs_8_), channel_id=1, source_target_pairs={{0,16},{4,20},{8,24},{12,28},{16,0},{20,4},{24,8},{28,12},{1,17},{... | collective-permute-start | bytes 18874376 | tf_op jit(solution)/shard_map/ppermute | solution.py:48
  254.8 83.4 %collective-permute-start.9 = (bf16[512,2048]{1,0:T(8,128)(2,1)}, bf16[512,2048]{1,0:T(8,128)(2,1)}, u32[]{:S(2)}, u32[]{:S(2)}) collective-permute-start(bf16[512,2048]{1,0:T(8,128)(2,1)} %bitcast.15.refs_4_.refs_1_.refs_5_), channel_id=1, source_target_pairs={{0,8},{4,12},{8,0},{12,4},{16,24},{20,28},{24,16},{28,20},{1,9},{5... | collective-permute-start | bytes 6291464 | tf_op jit(solution)/shard_map/ppermute | solution.py:48
  338.2 62.7 %collective-permute-start.14 = (bf16[512,2048]{1,0:T(8,128)(2,1)}, bf16[512,2048]{1,0:T(8,128)(2,1)}, u32[]{:S(2)}, u32[]{:S(2)}) collective-permute-start(bf16[512,2048]{1,0:T(8,128)(2,1)} %collective-permute-done.9.refs_6_.refs_3_.refs_7_), channel_id=1, source_target_pairs={{0,4},{4,0},{8,12},{12,8},{16,20},{20,16},{24,28},{28,24},{1,5},{5... | collective-permute-start | bytes 6291464 | tf_op jit(solution)/shard_map/ppermute | solution.py:48
  361.6 58.4 %collective-permute-start.10 = (bf16[256,2048]{1,0:T(8,128)(2,1)}, bf16[256,2048]{1,0:T(8,128)(2,1)}, u32[]{:S(2)}, u32[]{:S(2)}) collective-permute-start(bf16[256,2048]{1,0:T(8,128)(2,1)} %multiply_convert_fusion.1.refs_0_), channel_id=1, source_target_pairs={{0,4},{4,0},{8,12},{12,8},{16,20},{20,16},{24,28},{28,24},{1,5},{5... | collective-permute-start | bytes 3145736 | tf_op jit(solution)/shard_map/ppermute | solution.py:48
  401.0 74.0 %collective-permute-start.16 = (bf16[256,2048]{1,0:T(8,128)(2,1)}, bf16[256,2048]{1,0:T(8,128)(2,1)}, u32[]{:S(2)}, u32[]{:S(2)}) collective-permute-start(bf16[256,2048]{1,0:T(8,128)(2,1)} %multiply_convert_fusion.refs_0_.refs_4_), channel_id=1, source_target_pairs={{0,4},{4,0},{8,12},{12,8},{16,20},{20,16},{24,28},{28,24},{1,5},{5... | collective-permute-start | bytes 3145736 | tf_op jit(solution)/shard_map/ppermute | solution.py:48
  523.2 147.3 %collective-permute-start.29 = (bf16[4096,768]{1,0:T(8,128)(2,1)}, bf16[4096,768]{1,0:T(8,128)(2,1)}, u32[]{:S(2)}, u32[]{:S(2)}) collective-permute-start(bf16[4096,768]{1,0:T(8,128)(2,1)} %grad_pair.2), channel_id=1, source_target_pairs={{0,16},{4,20},{8,24},{12,28},{16,0},{20,4},{24,8},{28,12},{1,17},{... | collective-permute-start | bytes 18874376 | tf_op jit(solution)/shard_map/ppermute | solution.py:48
  586.1 190.6 %reduce-scatter.9.cloned.1.call-start = ((), (), s32[]{:S(2)}) async-start(), calls=%async_computation.10 | async-start | bytes 5242880 | tf_op jit(solution)/shard_map/reduce_scatter | solution.py:591
  670.4 187.7 %reduce-scatter.11.cloned.1.call-start = ((), (), s32[]{:S(2)}) async-start(), calls=%async_computation.11 | async-start | bytes 7864320 | tf_op jit(solution)/shard_map/reduce_scatter | solution.py:591
  691.3 377.9 %reduce-scatter.17.cloned.1.call-start = ((), (), s32[]{:S(2)}) async-start(), calls=%async_computation.16 | async-start | bytes 3932160 | tf_op jit(solution)/shard_map/reduce_scatter | solution.py:591
  691.4 85.3 %collective-permute-start.31 = (bf16[1024,2048]{1,0:T(8,128)(2,1)}, bf16[1024,2048]{1,0:T(8,128)(2,1)}, u32[]{:S(2)}, u32[]{:S(2)}) collective-permute-start(bf16[1024,2048]{1,0:T(8,128)(2,1)} %grad_q.2), channel_id=1, source_target_pairs={{0,4},{4,0},{8,12},{12,8},{16,20},{20,16},{24,28},{28,24},{1,5},{5... | collective-permute-start | bytes 12582920 | tf_op jit(solution)/shard_map/ppermute | solution.py:48
  691.4 93.7 %collective-permute-start.32 = (bf16[1024,2048]{1,0:T(8,128)(2,1)}, bf16[1024,2048]{1,0:T(8,128)(2,1)}, u32[]{:S(2)}, u32[]{:S(2)}) collective-permute-start(bf16[1024,2048]{1,0:T(8,128)(2,1)} %grad_o.2), channel_id=1, source_target_pairs={{0,4},{4,0},{8,12},{12,8},{16,20},{20,16},{24,28},{28,24},{1,5},{5... | collective-permute-start | bytes 12582920 | tf_op jit(solution)/shard_map/ppermute | solution.py:48
  691.9 70.3 %collective-permute-start.30 = (bf16[768,2048]{1,0:T(8,128)(2,1)}, bf16[768,2048]{1,0:T(8,128)(2,1)S(1)}, u32[]{:S(2)}, u32[]{:S(2)}) collective-permute-start(bf16[768,2048]{1,0:T(8,128)(2,1)} %grad_down.2), channel_id=1, source_target_pairs={{0,16},{4,20},{8,24},{12,28},{16,0},{20,4},{24,8},{28,12},{1,17},{... | collective-permute-start | bytes 9437192 | tf_op jit(solution)/shard_map/ppermute | solution.py:48
  809.5 260.9 %reduce-scatter.13.cloned.1.call-start = ((), (), s32[]{:S(2)}) async-start(), calls=%async_computation.12 | async-start | bytes 1392640 | tf_op jit(solution)/shard_map/reduce_scatter | solution.py:591
  875.7 94.3 %collective-permute-start.35 = (bf16[512,2176]{1,0:T(8,128)(2,1)S(1)}, bf16[512,2176]{1,0:T(8,128)(2,1)S(1)}, u32[]{:S(2)}, u32[]{:S(2)}) collective-permute-start(bf16[512,2176]{1,0:T(8,128)(2,1)S(1)} %pad_maximum_fusion.3), channel_id=1, source_target_pairs={{0,8},{4,12},{8,0},{12,4},{16,24},{20,28},{24,16},{28,20},{1,9},{5... | collective-permute-start | bytes 6684680 | tf_op jit(solution)/shard_map/ppermute | solution.py:48
  878.2 136.2 %collective-permute-start.38 = (bf16[512,2048]{1,0:T(8,128)(2,1)S(1)}, bf16[512,2048]{1,0:T(8,128)(2,1)S(1)}, u32[]{:S(2)}, u32[]{:S(2)}) collective-permute-start(bf16[512,2048]{1,0:T(8,128)(2,1)S(1)} %get-tuple-element.178), channel_id=1, source_target_pairs={{0,8},{4,12},{8,0},{12,4},{16,24},{20,28},{24,16},{28,20},{1,9},{5... | collective-permute-start | bytes 6291464 | tf_op jit(solution)/shard_map/ppermute | solution.py:48
  1020.3 93.6 %reduce-scatter.15.cloned.1.call-start = ((), (), s32[]{:S(2)}) async-start(), calls=%async_computation.14 | async-start | bytes 2621440 | tf_op jit(solution)/shard_map/reduce_scatter | solution.py:591
  1069.2 154.8 %all-gather.17.cloned.1.call-start = ((), (), s32[]{:S(2)}) async-start(), calls=%async_computation.17 | async-start | bytes 3932160 | tf_op jit(solution)/shard_map/all_gather | solution.py:961
  1069.8 236.8 %all-gather.13.cloned.1.call-start = ((), (), s32[]{:S(2)}) async-start(), calls=%async_computation.13 | async-start | bytes 1392640 | tf_op jit(solution)/shard_map/all_gather | solution.py:961
  1070.5 293.9 %all-gather.15.cloned.1.call-start = ((), (), s32[]{:S(2)}) async-start(), calls=%async_computation.15 | async-start | bytes 2621440 | tf_op jit(solution)/shard_map/all_gather | solution.py:961
  1077.5 69.1 %collective-permute-start.26 = (bf16[256,2048]{1,0:T(8,128)(2,1)}, bf16[256,2048]{1,0:T(8,128)(2,1)}, u32[]{:S(2)}, u32[]{:S(2)}) collective-permute-start(bf16[256,2048]{1,0:T(8,128)(2,1)} %get-tuple-element.136), channel_id=1, source_target_pairs={{0,4},{4,0},{8,12},{12,8},{16,20},{20,16},{24,28},{28,24},{1,5},{5... | collective-permute-start | bytes 3145736 | tf_op jit(solution)/shard_map/ppermute | solution.py:48
  1080.1 66.5 %collective-permute-start.28 = (bf16[256,2048]{1,0:T(8,128)(2,1)}, bf16[256,2048]{1,0:T(8,128)(2,1)}, u32[]{:S(2)}, u32[]{:S(2)}) collective-permute-start(bf16[256,2048]{1,0:T(8,128)(2,1)} %add_convert_fusion.6), channel_id=1, source_target_pairs={{0,8},{4,12},{8,0},{12,4},{16,24},{20,28},{24,16},{28,20},{1,9},{5... | collective-permute-start | bytes 3145736 | tf_op jit(solution)/shard_map/ppermute | solution.py:48
  1142.2 107.8 %collective-permute-start.43 = (bf16[4,256,768]{2,1,0:T(8,128)(2,1)}, bf16[4,256,768]{2,1,0:T(8,128)(2,1)}, u32[]{:S(2)}, u32[]{:S(2)}) collective-permute-start(bf16[4,256,768]{2,1,0:T(8,128)(2,1)} %pad_maximum_fusion.11.refs_0_), channel_id=1, source_target_pairs={{0,1},{1,0},{2,3},{3,2},{4,5},{5,4},{6,7},{7,6},{8,9},{9,8},{10,11... | collective-permute-start | bytes 4718600 | tf_op jit(solution)/shard_map/ppermute | solution.py:585
  1143.8 106.2 %collective-permute-start.44 = (bf16[4,256,768]{2,1,0:T(8,128)(2,1)}, bf16[4,256,768]{2,1,0:T(8,128)(2,1)}, u32[]{:S(2)}, u32[]{:S(2)}) collective-permute-start(bf16[4,256,768]{2,1,0:T(8,128)(2,1)} %pad_maximum_fusion.11.refs_0_), channel_id=1, source_target_pairs={{0,2},{1,3},{2,0},{3,1},{4,6},{5,7},{6,4},{7,5},{8,10},{9,11},{10,... | collective-permute-start | bytes 4718600 | tf_op jit(solution)/shard_map/ppermute | solution.py:585
  1145.7 143.3 %collective-permute-start.45 = (bf16[4,256,768]{2,1,0:T(8,128)(2,1)}, bf16[4,256,768]{2,1,0:T(8,128)(2,1)}, u32[]{:S(2)}, u32[]{:S(2)}) collective-permute-start(bf16[4,256,768]{2,1,0:T(8,128)(2,1)} %pad_maximum_fusion.11.refs_0_), channel_id=1, source_target_pairs={{0,3},{1,2},{2,1},{3,0},{4,7},{5,6},{6,5},{7,4},{8,11},{9,10},{10,... | collective-permute-start | bytes 4718600 | tf_op jit(solution)/shard_map/ppermute | solution.py:585
  (117 other events, 1558.0 us)
Sparse Core Ops, SparseCore 0:
  17.8 106.7 all-gather.6
  213.9 80.8 all-gather.8
  296.4 79.2 all-gather.10
  586.2 73.6 reduce-scatter.6
  670.5 73.4 reduce-scatter.8
  746.8 111.2 reduce-scatter.10
  860.4 60.7 reduce-scatter.16
  1020.5 27.8 reduce-scatter.12
  1069.3 44.5 reduce-scatter.14
  1115.4 108.6 all-gather.16
  1225.6 80.9 all-gather.12
  1308.0 56.3 all-gather.14

commit v3 on v2

--- a/solution.py
+++ b/solution.py
@@ -23,7 +23,7 @@
 F32 = jnp.float32
 BLOCK = 512
 COST = 100.0
-LOW = 0.01
+LOW = 45.0
 VMEM = 60 * 1024 * 1024
 
 
@@ -99,7 +99,7 @@
     )
 
 
-def project(x, weight, first, cols, cosine, sine, gain, kinds, name):
+def project(x, weight, first, cols, cosine, sine, gain, kinds, name, cost=COST):
     rows, depth = x.shape
     width = DH * len(kinds)
 
@@ -130,6 +130,7 @@
         [jax.ShapeDtypeStruct((rows, cols), BF)] * 2,
         2 * rows * depth * cols,
         2 * (rows * depth + depth * cols + 2 * rows * cols),
+        cost=cost,
     )(x, weight, cosine, sine, gain)
 
 
@@ -370,7 +371,7 @@
     )(place[0], *mids, *cots, *pieces, w_down, *earlier)
 
 
-def feed_out(left, weight, index, parts, transposed, name):
+def feed_out(left, weight, index, parts, transposed, name, dtype=BF):
     depth = left.shape[1]
     cols = weight.shape[0] if transposed else weight.shape[1]
     rows = parts[1]
@@ -379,7 +380,7 @@
         for part in range(parts[0]):
             now = a_ref[part * rows : (part + 1) * rows]
             result = dot_last(now, w_ref[...]) if transposed else mat(now, w_ref[...])
-            outs[part][...] = result.astype(BF)
+            outs[part][...] = result.astype(dtype)
 
     return call(
         kernel,
@@ -392,7 +393,7 @@
             else pl.BlockSpec((depth, BLOCK), lambda j: (0, j)),
         ],
         [pl.BlockSpec((rows, BLOCK), lambda j: (0, j))] * parts[0],
-        [jax.ShapeDtypeStruct((rows, cols), BF)] * parts[0],
+        [jax.ShapeDtypeStruct((rows, cols), dtype)] * parts[0],
         2 * parts[0] * rows * depth * cols,
         2 * (parts[0] * rows * (depth + cols) + depth * cols),
     )(left, weight)
@@ -565,13 +566,6 @@
     return [rows, from_core, from_x, from_both]
 
 
-def group_sum(parts):
-    for_x = (parts[2].astype(F32) + swap(parts[3], 1).astype(F32)).astype(BF)
-    got_x = swap(for_x, 2)
-    got_core = swap(parts[1], 1)
-    return parts[0].astype(F32) + got_core.astype(F32) + got_x.astype(F32)
-
-
 def group_half(parts):
     got = swap(jnp.concatenate([parts[1], parts[3]], axis=0), 1)
     rows = parts[0].shape[0]
@@ -591,15 +585,11 @@
     return lax.psum_scatter(array, "ctx", scatter_dimension=0, tiled=True)
 
 
-def spread_pairs(piece, me, unit):
-    high = lax.axis_size("fsdp") // 4
+def spread_near(piece, me):
     slot = me % 4
     rows = piece.shape[0] // 4
     near = [lax.dynamic_slice_in_dim(piece, (slot ^ which) * rows, rows, 0) for which in range(4)]
-    near = [near[0]] + [swap(near[which], which) for which in range(1, 4)]
-    chunks = gather_ctx(jnp.stack(near))
-    place = jnp.stack([lax.axis_index("ctx"), me // 4, slot])
-    return lay_pairs(chunks, place, high, unit)
+    return near, jnp.stack([near[0]] + [swap(near[which], which) for which in range(1, 4)])
 
 
 def fold(value, bits, *others):
@@ -693,7 +683,6 @@
     inv_in = inv_rms(source)
     normed_b = (source * inv_in * attn_gain).astype(BF)
     normed_now = after(normed_b, parts_own, out_block, *masks)
-    got_core = swap(jnp.concatenate([parts_own[shard:], got_x[shard:]], axis=0), 1)
     pairs, pairs_raw = project(
         normed_now,
         w_qkv,
@@ -708,6 +697,9 @@
     everyone = [
         lax.all_gather(pairs[rows_of(index)], "ctx", axis=0, tiled=True) for index in range(micro)
     ]
+    got_core = swap(
+        jnp.concatenate([parts_own[shard:], after(got_x, pairs, wd)[shard:]], axis=0), 1
+    )
     near = jnp.concatenate(
         [parts_own[:shard], got_core[:shard], got_x[:shard], got_core[shard:]], axis=0
     )
@@ -721,9 +713,10 @@
         q_gain,
         "rrrr",
         "project_queries",
+        0.01,
     )
     pieces = [near] + [swap(near, 4 * far) for far in range(1, high)]
-    for bit, earlier in ((2, queries), (1, everyone[0])):
+    for bit, earlier in ((2, near), (1, everyone[0])):
         out_block = jnp.concatenate([out_block, swap(after(out_block, earlier), bit)], axis=0)
         out_order = out_order + [entry ^ bit for entry in out_order]
     w_out = jnp.zeros((QH * DH, D), BF)
@@ -731,7 +724,7 @@
         w_out = lax.dynamic_update_slice_in_dim(
             w_out, out_block[index * shard : (index + 1) * shard], (me ^ entry) * shard, 0
         )
-    cot_x = swap(after(cot_all, queries), 2)
+    cot_x = swap(after(cot_all, near), 2)
     cot_rows = [cot_all, swap(cot_all, 1), cot_x, swap(cot_x, 1)]
 
     attended = []
@@ -793,7 +786,6 @@
         )
 
     d_mids = []
-    sent_pair = []
     me_array = me[None]
     act_b, dgu_b, wgu = feed(
         [after(mid_rows[0][0], token)] + mid_rows[0][1:],
@@ -817,17 +809,20 @@
                 (act_b, dgu_b),
                 (me_array, unit),
             )
-        if index == micro - 1:
-            token = act_b
-            for far in range(1, high):
-                sent_pair.append(pair_terms(after(mid_pieces[0], token), far, []))
-                token = sent_pair[-1]
-            dgu_now = after(dgu_b, token, d_mids[0][1])
-        else:
-            dgu_now = dgu_b
-        parts = feed_out(dgu_now, wgu, index, (4, local), True, "feed_back")
+        parts = feed_out(
+            after(dgu_b, act_b, *[d_mid[1] for d_mid in d_mids]),
+            wgu,
+            index,
+            (4, local),
+            True,
+            "feed_back",
+        )
         d_mids.append(group_half(parts))
         token = parts[0]
+    sent_pair = []
+    for far in range(1, high):
+        sent_pair.append(pair_terms(after(mid_pieces[0], token), far, []))
+        token = sent_pair[-1]
     got_pair = [swap(piece, 4 * (far + 1)) for far, piece in enumerate(sent_pair)]
 
     d_middles = []
@@ -884,48 +879,45 @@
         )
 
     order = order_of(bits)
+    out_parts = []
+    for index in range(micro):
+        out_parts.append(
+            feed_out(after(act_b, token), wd, index, (4, local), False, "feed_forward")
+        )
+        token = out_parts[-1][0]
+    out_half = group_half([jnp.concatenate(list(pair), axis=0) for pair in zip(*out_parts)])
     sent_query = plain_terms(after(normed_b, token), d_query_b, order[half_size:], [], "grad_q")
     sent_output = plain_terms(
         after(attended_b, sent_query), d_proj_b, order[half_size:], [], "grad_o"
     )
-
-    outs = []
-    token = sent_output
-    for index in range(micro):
-        parts = feed_out(after(act_b, token), wd, index, (4, local), False, "feed_forward")
-        token = parts[0]
-        outs.append((middles[index] + group_sum(parts)).astype(BF))
-    outputs = jnp.stack(outs)
-
-    own_pair = pair_terms(after(mid_pieces[0], token), 0, got_pair)
-    own_down = down_terms(after(act_b, own_pair), 0, got_down, LOW)
+    own_pair = pair_terms(after(mid_pieces[0], sent_output, out_half[1]), 0, got_pair)
+    own_query = plain_terms(
+        after(normed_b, own_pair), d_query_b, order[:half_size], [swap(sent_query, 1)], "grad_q"
+    )
+    own_output = plain_terms(
+        after(attended_b, own_query), d_proj_b, order[:half_size], [swap(sent_output, 1)], "grad_o"
+    )
+    own_down = down_terms(after(act_b, own_output), 0, got_down)
+    outputs = jnp.concatenate(middles, axis=0) + out_half[0]
+    outputs = (outputs + swap(out_half[1], 2).astype(F32)).astype(BF).reshape(micro, local, D)
     pair_piece = scatter_ctx(own_pair)
     down_piece = scatter_ctx(after(own_down, own_pair))
-    own_query = plain_terms(
-        after(normed_b, own_down, *d_pair_parts),
-        d_query_b,
-        order[:half_size],
-        [swap(sent_query, 1)],
-        "grad_q",
-        LOW,
-    )
-    own_output = plain_terms(
-        after(attended_b, own_query),
-        d_proj_b,
-        order[:half_size],
-        [swap(sent_output, 1)],
-        "grad_o",
-        LOW,
-    )
-
-    d_pairs = after(jnp.concatenate(d_pair_parts, axis=0), own_output)
+
+    d_pairs = after(jnp.concatenate(d_pair_parts, axis=0), own_down, outputs)
     d_pair_b, d_k_gain = pair_back(d_pairs, pairs_raw, cosine, sine, k_gain)
-    sent_kv = plain_terms(normed_b, d_pair_b, order[half_size:], [], "grad_kv", LOW)
-    d_normed = dot_last(
-        jnp.concatenate([after(d_query_b, sent_kv), d_pair_b], axis=1), w_qkv
+    part_qo = [fold(own_query, bits[1:2], d_pair_b), fold(own_output, bits[1:2], d_pair_b)]
+    sent_kv = plain_terms(after(normed_b, *part_qo), d_pair_b, order[half_size:], [], "grad_kv", LOW)
+    (d_normed,) = feed_out(
+        jnp.concatenate([after(d_query_b, sent_kv), d_pair_b], axis=1),
+        w_qkv,
+        0,
+        (1, total),
+        True,
+        "d_normed",
+        F32,
     )
     own_kv = plain_terms(
-        after(normed_b, d_normed, pair_piece), d_pair_b, order[:half_size], [swap(sent_kv, 1)], "grad_kv"
+        after(normed_b, d_normed), d_pair_b, order[:half_size], [swap(sent_kv, 1)], "grad_kv"
     )
     d_source, d_attn_gain = rms_back(source, inv_in, attn_gain, after(d_normed, own_kv))
     grad_inputs = jnp.concatenate(d_middles, axis=0) + d_source
@@ -951,16 +943,23 @@
         axis=0,
     )
     columns = fold(columns, bits[:1])
-    part_qo = [fold(own, bits[1:2], own_kv) for own in (own_query, own_output)]
+    near_parts, pair_near = spread_near(pair_piece, me)
+    chunks = gather_ctx(pair_near)
+    down_whole = lax.all_gather(down_piece, "ctx", axis=0, tiled=True)
     part_qo = fold(jnp.concatenate(part_qo, axis=1), bits[2:])
-    part_kv = fold(jnp.concatenate([own_kv, columns], axis=1), bits[1:])
-
-    grad_gate, grad_up = spread_pairs(pair_piece, me, unit)
+    part_kv = fold(
+        jnp.concatenate([after(own_kv, *near_parts), columns], axis=1), bits[1:2], pair_near
+    )
+    part_kv = fold(part_kv, bits[2:])
+
+    grad_gate, grad_up = lay_pairs(
+        chunks, jnp.stack([lax.axis_index("ctx"), me // 4, slot]), high, unit
+    )
 
     def whole(piece):
-        return lax.all_gather(piece, "ctx", axis=0, tiled=True).astype(F32)
-
-    grad_down = whole(down_piece)
+        return lax.all_gather(after(piece, *chunks[1:]), "ctx", axis=0, tiled=True).astype(F32)
+
+    grad_down = down_whole.astype(F32)
     both = whole(scatter_ctx(part_qo))
     grad_query, grad_output = both[:, :D], both[:, D:]
     rest = whole(scatter_ctx(part_kv))

time: 1400 us -> 1250 us (0.89)
  waiting for transfers between devices: 757 us -> 608 us
  other arithmetic: 97.2 us -> 117 us
  matrix products: 34.2 us -> 19.3 us
  Pallas kernels: 339 us -> 353 us
    ppermute x43 -> x39, waiting for transfers between devices: 434 us -> 294 us  [swap(): return lax.ppermute(value, 'fsdp', [(i, i ^ bits) for i in range(count)])]
    ppermute x3, waiting for transfers between devices: 56.1 us -> 120 us  [gather_ctx(): lax.ppermute(chunk, 'ctx', [(i, i ^ step) for i in range(count)])]
    reduce_scatter x6, waiting for transfers between devices: 62.9 us -> 0.06 us  [scatter_ctx(): return lax.psum_scatter(array, 'ctx', scatter_dimension=0, tiled=True)]
    pallas_call x4 -> x5, Pallas kernels: 57.6 us -> 72.9 us  [feed_out(): call(kernel, name, (cols // BLOCK,), [pl.BlockSpec((parts[0] * rows, dept...]
    dot_general x3 -> x2, matrix products: 21.4 us -> 6.67 us  [dot_last(): lax.dot_general(left, right, (((1,), (1,)), ((), ())), preferred_element_...]
    ppermute x43 -> x39, starting transfers between devices: 28.4 us -> 26 us  [swap(): return lax.ppermute(value, 'fsdp', [(i, i ^ bits) for i in range(count)])]
  transfers between devices with their start and end apart: 58 -> 54, of which waited for: 25 -> 24; matrix products, arithmetic and copies ran while one was open for 15% -> 15% of each run, Pallas kernels for 25% -> 29%
where the time goes in v3:
time: 1250 us; the launch traced here: 1240 us
  waiting for transfers between devices  608 us (49%)
  Pallas kernels  353 us (28%)
  other arithmetic  117 us (9%)
  local copies, waits for them, and re-layouts  90.4 us (7%)
  starting transfers between devices  31.6 us (3%)
  matrix products  19.3 us (2%)
  between operations  15.8 us (1%)
    ppermute x39, waiting for transfers between devices, swap(): return lax.ppermute(value, 'fsdp', [(i, i ^ bits) for i in range(count)])  294 us
    ppermute x3, waiting for transfers between devices, gather_ctx(): lax.ppermute(chunk, 'ctx', [(i, i ^ step) for i in range(count)])  120 us
    pallas_call x10, Pallas kernels, weight_terms(): call(kernel, name, (steps,), [pl.BlockSpec((left.shape[0], width), lambda...  112 us
    all_gather x1, waiting for transfers between devices, body(): down_whole = lax.all_gather(down_piece, 'ctx', axis=0, tiled=True)  77.1 us
    pallas_call x5, Pallas kernels, feed_out(): call(kernel, name, (cols // BLOCK,), [pl.BlockSpec((parts[0] * rows, dept...  72.9 us
    pallas_call x2, Pallas kernels, feed(): call(kernel, 'feed', (steps,), [fixed((rows, depth))] * parts + [pl.Block...  61.5 us
    all_gather x1, waiting for transfers between devices, body(): lax.all_gather(jnp.concatenate([w_query, pair_shard], axis=1), 'fsdp', ax...  59.3 us
    all_gather x2, waiting for transfers between devices, whole(): lax.all_gather(after(piece, *chunks[1:]), 'ctx', axis=0, tiled=True)  57.1 us
  transfers between devices with their start and end apart: 54, of which 24 were waited for; matrix products, arithmetic and copies ran while one was open for 15% of the time, Pallas kernels for 29%

profile of v3, /device:TPU:0, one launch (start us, length us, event | category | flops | bytes accessed | tf_op | source)
XLA Modules:
  0.0 1235.6 jit_solution(18014157984408677923)
XLA Ops:
  64.9 59.3 %all-gather.7.cloned.1.call-done.w_ref = bf16[2048,4096]{1,0:T(8,128)(2,1)} async-done(((bf16[256,4096]{1,0:T(8,128)(2,1)}), bf16[2048,4096]{1,0:T(8,128)(2,1)}) %all-gather.7.cloned.1.call-update) | async-done | bytes 16777232 | tf_op jit(solution)/shard_map/all_gather | solution.py:645
  126.2 10.2 project_pairs.1
  143.8 50.9 %collective-permute-done.5 = bf16[768,2048]{1,0:T(8,128)(2,1)} collective-permute-done((bf16[768,2048]{1,0:T(8,128)(2,1)}, bf16[768,2048]{1,0:T(8,128)(2,1)}, u32[]{:S(2)}, u32[]{:S(2)}) %collective-permute-start.5) | collective-permute-done | bytes 3145760 | tf_op jit(solution)/shard_map/ppermute | solution.py:48
  216.8 13.6 %project_queries.1 = (bf16[512,2048]{1,0:T(8,128)(2,1)}, bf16[512,2048]{1,0:T(8,128)(2,1)}) custom-call(bf16[512,2048]{1,0:T(8,128)(2,1)} %fusion.3.x_ref.refs_0_, bf16[2048,4096]{1,0:T(8,128)(2,1)} %all-gather.7.cloned.1.call-done.w_ref, f32[512,128]{1,0:T(8,128)} %get-tuple-element.256.c_ref, f32[512,128]{1,0:T(8,128)} %get-tuple-element.257.s_ref, ...), custom_call_target="tpu_custom_call" | custom-call | flops 42949672 | bytes 146800 | tf_op jit(solution)/shard_map/project_queries/pallas_call | solution.py:118
  234.5 24.0 %collective-permute-done.7 = bf16[512,2048]{1,0:T(8,128)(2,1)} collective-permute-done((bf16[512,2048]{1,0:T(8,128)(2,1)}, bf16[512,2048]{1,0:T(8,128)(2,1)}, u32[]{:S(2)}, u32[]{:S(2)}) %collective-permute-start.7) | collective-permute-done | bytes 2097184 | tf_op jit(solution)/shard_map/ppermute | solution.py:48
  262.1 9.5 attention.2
  271.7 31.1 %collective-permute-done.9.refs_6_.refs_3_.refs_7_ = bf16[512,2048]{1,0:T(8,128)(2,1)} collective-permute-done((bf16[512,2048]{1,0:T(8,128)(2,1)}, bf16[512,2048]{1,0:T(8,128)(2,1)}, u32[]{:S(2)}, u32[]{:S(2)}) %collective-permute-start.9) | collective-permute-done | bytes 2097184 | tf_op jit(solution)/shard_map/ppermute | solution.py:48
  327.2 9.5 attention.3
  356.4 17.5 %collective-permute-done.17.refs_2_.refs_6_ = bf16[256,2048]{1,0:T(8,128)(2,1)} collective-permute-done((bf16[256,2048]{1,0:T(8,128)(2,1)}, bf16[256,2048]{1,0:T(8,128)(2,1)}, u32[]{:S(2)}, u32[]{:S(2)}) %collective-permute-start.17) | collective-permute-done | bytes 1048608 | tf_op jit(solution)/shard_map/ppermute | solution.py:48
  373.9 32.9 %feed.2 = (bf16[2048,1536]{1,0:T(8,128)(2,1)}, bf16[2048,3072]{1,0:T(8,128)(2,1)}, bf16[2048,3072]{1,0:T(8,128)(2,1)}) custom-call(s32[1]{0:T(128)} %bitcast.15.me_ref, bf16[256,2048]{1,0:T(8,128)(2,1)} %multiply_convert_fusion.1.refs_0_, bf16[256,2048]{1,0:T(8,128)(2,1)} %collective-permute-done.10.refs_1_, ...), custom_call_target="tpu_custom_call" | custom-call | flops 1932735283200 | bytes 3670016000 | tf_op jit(solution)/shard_map/feed/pallas_call | solution.py:351
  406.9 18.5 %feed_back.2 = (bf16[256,2048]{1,0:T(8,128)(2,1)}, bf16[256,2048]{1,0:T(8,128)(2,1)}, bf16[256,2048]{1,0:T(8,128)(2,1)}, bf16[256,2048]{1,0:T(8,128)(2,1)}) custom-call(bf16[2048,3072]{1,0:T(8,128)(2,1)} %get-tuple-element.112.a_ref.refs_11_, bf16[2048,3072]{1,0:T(8,128)(2,1)} %get-tuple-element.113.w_ref.refs_8_), custom_call_target="tpu_custom_call" | custom-call | flops 1288490188800 | bytes 2306867200 | tf_op jit(solution)/shard_map/feed_back/pallas_call | solution.py:385
  429.0 28.6 %feed.3 = (bf16[2048,1536]{1,0:T(8,128)(2,1)}, bf16[2048,3072]{1,0:T(8,128)(2,1)}) custom-call(s32[1]{0:T(128)} %bitcast.15.me_ref, bf16[256,2048]{1,0:T(8,128)(2,1)} %multiply_convert_fusion.refs_0_.refs_4_, bf16[256,2048]{1,0:T(8,128)(2,1)} %collective-permute-done.16.refs_1_.refs_5_, ...), custom_call_target="tpu_custom_call", output_to_operand_aliasing={{0}: (11, {}), {1}: (12, {})} | custom-call | flops 1932735283200 | bytes 3670016000 | tf_op jit(solution)/shard_map/feed/pallas_call | solution.py:351
  461.6 18.6 %feed_back.3 = (bf16[256,2048]{1,0:T(8,128)(2,1)}, bf16[256,2048]{1,0:T(8,128)(2,1)}, bf16[256,2048]{1,0:T(8,128)(2,1)}, bf16[256,2048]{1,0:T(8,128)(2,1)}) custom-call(bf16[2048,3072]{1,0:T(8,128)(2,1)} %get-tuple-element.122.a_ref.refs_8_, bf16[2048,3072]{1,0:T(8,128)(2,1)} %get-tuple-element.113.w_ref.refs_8_), custom_call_target="tpu_custom_call" | custom-call | flops 1288490188800 | bytes 2306867200 | tf_op jit(solution)/shard_map/feed_back/pallas_call | solution.py:385
  483.3 19.5 %grad_pair.2 = bf16[4096,768]{1,0:T(8,128)(2,1)} custom-call(s32[1]{0:T(128)} %bitcast.18.block_ref, s32[1]{0:T(128)} %constant.140.clone.1.start_ref.block_ref, bf16[256,2048]{1,0:T(8,128)(2,1)} %multiply_convert_fusion.1.refs_0_, bf16[256,2048]{1,0:T(8,128)(2,1)} %collective-permute-done.10.refs_1_, bf16[256,2048]{1,0:T(8,128)(2,1)} %collective-permute-done.11.refs_2_, ...), custom_call_target="tpu_custom_call" | custom-call | flops 1288490188800 | bytes 2306867200 | tf_op jit(solution)/shard_map/grad_pair/pallas_call | solution.py:441
  516.9 19.9 %attention_back.2 = (bf16[256,2048]{1,0:T(8,128)(2,1)}, bf16[1024,2048]{1,0:T(8,128)(2,1)}, f32[1,128]{1,0:T(1,128)}) custom-call(bf16[256,2048]{1,0:T(8,128)(2,1)} %get-tuple-element.127.q_ref, bf16[256,2048]{1,0:T(8,128)(2,1)} %get-tuple-element.201.r_ref, bf16[1024,2048]{1,0:T(8,128)(2,1)} %all-gather.9.cloned.1.call-done.kv_ref, ...), custom_call_target="tpu_custom_call" | custom-call | flops 536870912000 | bytes 1363148800 | tf_op jit(solution)/shard_map/attention_back/pallas_call | solution.py:232
  536.8 12.0 grad_down.2
  564.1 19.8 %attention_back.3 = (bf16[256,2048]{1,0:T(8,128)(2,1)}, bf16[1024,2048]{1,0:T(8,128)(2,1)}, f32[1,128]{1,0:T(1,128)}) custom-call(bf16[256,2048]{1,0:T(8,128)(2,1)} %get-tuple-element.107.q_ref, bf16[256,2048]{1,0:T(8,128)(2,1)} %get-tuple-element.202.r_ref, bf16[1024,2048]{1,0:T(8,128)(2,1)} %all-gather.11.cloned.1.call-done.kv_ref, ...), custom_call_target="tpu_custom_call" | custom-call | flops 536870912000 | bytes 1363148800 | tf_op jit(solution)/shard_map/attention_back/pallas_call | solution.py:232
  585.2 11.1 feed_forward.2
  596.4 10.4 feed_forward.3
  632.4 9.0 collective-permute-done.25.refs_9_
  641.5 19.8 %grad_pair.3 = bf16[4096,768]{1,0:T(8,128)(2,1)} custom-call(s32[1]{0:T(128)} %bitcast.2.block_ref, s32[1]{0:T(128)} %constant.140.clone.1.start_ref.block_ref, bf16[256,2048]{1,0:T(8,128)(2,1)} %multiply_convert_fusion.1.refs_0_, bf16[256,2048]{1,0:T(8,128)(2,1)} %collective-permute-done.10.refs_1_, bf16[256,2048]{1,0:T(8,128)(2,1)} %collective-permute-done.11.refs_2_, ...), custom_call_target="tpu_custom_call" | custom-call | flops 1288490188800 | bytes 2936012800 | tf_op jit(solution)/shard_map/grad_pair/pallas_call | solution.py:441
  687.9 20.5 %collective-permute-done.28.refs_9_ = bf16[768,2048]{1,0:T(8,128)(2,1)} collective-permute-done((bf16[768,2048]{1,0:T(8,128)(2,1)}, bf16[768,2048]{1,0:T(8,128)(2,1)}, u32[]{:S(2)}, u32[]{:S(2)}) %collective-permute-start.28) | collective-permute-done | bytes 3145760 | tf_op jit(solution)/shard_map/ppermute | solution.py:48
  708.4 13.2 %grad_down.3 = bf16[768,2048]{1,0:T(8,128)(2,1)} custom-call(s32[1]{0:T(128)} %constant.140.clone.1.start_ref.block_ref, s32[1]{0:T(128)} %constant.140.clone.1.start_ref.block_ref, bf16[2048,1536]{1,0:T(8,128)(2,1)} %get-tuple-element.153.refs_0_.a_ref, bf16[512,2048]{1,0:T(8,128)(2,1)} %bitcast.14.refs_4_.refs_1_.refs_5_, ...), custom_call_target="tpu_custom_call" | custom-call | flops 644245094400 | bytes 1782579200 | tf_op jit(solution)/shard_map/grad_down/pallas_call | solution.py:441
  739.6 35.8 %collective-permute-done.29 = bf16[512,2048]{1,0:T(8,128)(2,1)} collective-permute-done((bf16[512,2048]{1,0:T(8,128)(2,1)}, bf16[512,2048]{1,0:T(8,128)(2,1)}, u32[]{:S(2)}, u32[]{:S(2)}) %collective-permute-start.29) | collective-permute-done | bytes 2097184 | tf_op jit(solution)/shard_map/ppermute | solution.py:48
  792.9 14.3 %d_normed.1 = f32[512,2048]{1,0:T(8,128)} custom-call(bf16[512,4096]{1,0:T(8,128)(2,1)} %pad_maximum_fusion.3.a_ref, bf16[2048,4096]{1,0:T(8,128)(2,1)} %all-gather.7.cloned.1.call-done.w_ref), custom_call_target="tpu_custom_call" | custom-call | flops 858993459200 | bytes 2306867200 | tf_op jit(solution)/shard_map/d_normed/pallas_call | solution.py:385
  842.4 45.9 %collective-permute-done.34 = bf16[256,768]{1,0:T(8,128)(2,1)S(1)} collective-permute-done((bf16[256,768]{1,0:T(8,128)(2,1)S(1)}, bf16[256,768]{1,0:T(8,128)(2,1)S(1)}, u32[]{:S(2)}, u32[]{:S(2)}) %collective-permute-start.34) | collective-permute-done | bytes 393248 | tf_op jit(solution)/shard_map/ppermute | solution.py:48
  900.4 26.0 %collective-permute-done.37 = bf16[256,2176]{1,0:T(8,128)(2,1)S(1)} collective-permute-done((bf16[256,2176]{1,0:T(8,128)(2,1)S(1)}, bf16[256,2176]{1,0:T(8,128)(2,1)S(1)}, u32[]{:S(2)}, u32[]{:S(2)}) %collective-permute-start.37) | collective-permute-done | bytes 1114144 | tf_op jit(solution)/shard_map/ppermute | solution.py:48
  932.8 83.9 %collective-permute-done.38.refs_1_ = bf16[4,256,768]{2,1,0:T(8,128)(2,1)} collective-permute-done((bf16[4,256,768]{2,1,0:T(8,128)(2,1)}, bf16[4,256,768]{2,1,0:T(8,128)(2,1)}, u32[]{:S(2)}, u32[]{:S(2)}) %collective-permute-start.38) | collective-permute-done | bytes 1572896 | tf_op jit(solution)/shard_map/ppermute | solution.py:579
  1016.7 35.8 %collective-permute-done.39.refs_2_ = bf16[4,256,768]{2,1,0:T(8,128)(2,1)} collective-permute-done((bf16[4,256,768]{2,1,0:T(8,128)(2,1)}, bf16[4,256,768]{2,1,0:T(8,128)(2,1)}, u32[]{:S(2)}, u32[]{:S(2)}) %collective-permute-start.39) | collective-permute-done | bytes 1572896 | tf_op jit(solution)/shard_map/ppermute | solution.py:579
  1060.2 77.1 %all-gather.17.cloned.1.call-done = bf16[768,2048]{1,0:T(8,128)(2,1)} async-done(((bf16[192,2048]{1,0:T(8,128)(2,1)}), bf16[768,2048]{1,0:T(8,128)(2,1)}) %all-gather.17.cloned.1.call-update) | async-done | bytes 3145744 | tf_op jit(solution)/shard_map/all_gather | solution.py:948
  1151.5 32.0 %all-gather.15.cloned.1.call-done = bf16[256,4096]{1,0:T(8,128)(2,1)} async-done(((bf16[64,4096]{1,0:T(8,128)(2,1)}), bf16[256,4096]{1,0:T(8,128)(2,1)}) %all-gather.15.cloned.1.call-update) | async-done | bytes 2097168 | tf_op jit(solution)/shard_map/all_gather | solution.py:960
  1187.7 25.1 %all-gather.13.cloned.1.call-done = bf16[256,2176]{1,0:T(8,128)(2,1)} async-done(((bf16[64,2176]{1,0:T(8,128)(2,1)}), bf16[256,2176]{1,0:T(8,128)(2,1)}) %all-gather.13.cloned.1.call-update) | async-done | bytes 1114128 | tf_op jit(solution)/shard_map/all_gather | solution.py:960
  (456 shorter events, 364.5 us)
Async XLA Ops:
  7.2 117.0 %all-gather.7.cloned.1.call-start = ((), (), s32[]{:S(2)}) async-start(), calls=%async_computation.6 | async-start | bytes 18874368 | tf_op jit(solution)/shard_map/all_gather | solution.py:645
  17.7 244.4 %all-gather.9.cloned.1.call-start = ((), (), s32[]{:S(2)}) async-start(), calls=%async_computation.7 | async-start | bytes 5242880 | tf_op jit(solution)/shard_map/all_gather | solution.py:698
  124.1 70.6 %collective-permute-start.5 = (bf16[768,2048]{1,0:T(8,128)(2,1)}, bf16[768,2048]{1,0:T(8,128)(2,1)}, u32[]{:S(2)}, u32[]{:S(2)}) collective-permute-start(bf16[768,2048]{1,0:T(8,128)(2,1)} %param.36), channel_id=1, source_target_pairs={{0,16},{4,20},{8,24},{12,28},{16,0},{20,4},{24,8},{28,12},{1,17},{... | collective-permute-start | bytes 9437192 | tf_op jit(solution)/shard_map/ppermute | solution.py:48
  124.9 73.8 %collective-permute-start.4 = (bf16[512,3072]{1,0:T(8,128)(2,1)}, bf16[512,3072]{1,0:T(8,128)(2,1)}, u32[]{:S(2)}, u32[]{:S(2)}) collective-permute-start(bf16[512,3072]{1,0:T(8,128)(2,1)} %column_parts.2), channel_id=1, source_target_pairs={{0,8},{4,12},{8,0},{12,4},{16,24},{20,28},{24,16},{28,20},{1,9},{5... | collective-permute-start | bytes 9437192 | tf_op jit(solution)/shard_map/ppermute | solution.py:48
  139.5 187.6 %all-gather.11.cloned.1.call-start = ((), (), s32[]{:S(2)}) async-start(), calls=%async_computation.8 | async-start | bytes 5242880 | tf_op jit(solution)/shard_map/all_gather | solution.py:698
  209.8 48.8 %collective-permute-start.7 = (bf16[512,2048]{1,0:T(8,128)(2,1)}, bf16[512,2048]{1,0:T(8,128)(2,1)}, u32[]{:S(2)}, u32[]{:S(2)}) collective-permute-start(bf16[512,2048]{1,0:T(8,128)(2,1)} %get-tuple-element.103), channel_id=1, source_target_pairs={{0,8},{4,12},{8,0},{12,4},{16,24},{20,28},{24,16},{28,20},{1,9},{5... | collective-permute-start | bytes 6291464 | tf_op jit(solution)/shard_map/ppermute | solution.py:48
  211.3 134.7 %collective-permute-start.13 = (bf16[512,2048]{1,0:T(8,128)(2,1)}, bf16[512,2048]{1,0:T(8,128)(2,1)}, u32[]{:S(2)}, u32[]{:S(2)}) collective-permute-start(bf16[512,2048]{1,0:T(8,128)(2,1)} %bitcast.14.refs_4_.refs_1_.refs_5_), channel_id=1, source_target_pairs={{0,4},{4,0},{8,12},{12,8},{16,20},{20,16},{24,28},{28,24},{1,5},{5... | collective-permute-start | bytes 6291464 | tf_op jit(solution)/shard_map/ppermute | solution.py:48
  216.1 512.2 %reduce-scatter.7.cloned.1.call-start = ((), (), s32[]{:S(2)}) async-start(), calls=%async_computation.9 | async-start | bytes 5242880 | tf_op jit(solution)/shard_map/reduce_scatter | solution.py:585
  216.2 157.7 %collective-permute-start.15 = (bf16[1024,3072]{1,0:T(8,128)(2,1)}, bf16[1024,3072]{1,0:T(8,128)(2,1)}, u32[]{:S(2)}, u32[]{:S(2)}) collective-permute-start(bf16[1024,3072]{1,0:T(8,128)(2,1)} %pad_maximum_fusion.refs_8_), channel_id=1, source_target_pairs={{0,16},{4,20},{8,24},{12,28},{16,0},{20,4},{24,8},{28,12},{1,17},{... | collective-permute-start | bytes 18874376 | tf_op jit(solution)/shard_map/ppermute | solution.py:48
  233.6 69.1 %collective-permute-start.9 = (bf16[512,2048]{1,0:T(8,128)(2,1)}, bf16[512,2048]{1,0:T(8,128)(2,1)}, u32[]{:S(2)}, u32[]{:S(2)}) collective-permute-start(bf16[512,2048]{1,0:T(8,128)(2,1)} %bitcast.14.refs_4_.refs_1_.refs_5_), channel_id=1, source_target_pairs={{0,8},{4,12},{8,0},{12,4},{16,24},{20,28},{24,16},{28,20},{1,9},{5... | collective-permute-start | bytes 6291464 | tf_op jit(solution)/shard_map/ppermute | solution.py:48
  302.7 53.1 %collective-permute-start.14 = (bf16[512,2048]{1,0:T(8,128)(2,1)}, bf16[512,2048]{1,0:T(8,128)(2,1)}, u32[]{:S(2)}, u32[]{:S(2)}) collective-permute-start(bf16[512,2048]{1,0:T(8,128)(2,1)} %collective-permute-done.9.refs_6_.refs_3_.refs_7_), channel_id=1, source_target_pairs={{0,4},{4,0},{8,12},{12,8},{16,20},{20,16},{24,28},{28,24},{1,5},{5... | collective-permute-start | bytes 6291464 | tf_op jit(solution)/shard_map/ppermute | solution.py:48
  355.9 73.1 %collective-permute-start.16 = (bf16[256,2048]{1,0:T(8,128)(2,1)}, bf16[256,2048]{1,0:T(8,128)(2,1)}, u32[]{:S(2)}, u32[]{:S(2)}) collective-permute-start(bf16[256,2048]{1,0:T(8,128)(2,1)} %multiply_convert_fusion.refs_0_.refs_4_), channel_id=1, source_target_pairs={{0,4},{4,0},{8,12},{12,8},{16,20},{20,16},{24,28},{28,24},{1,5},{5... | collective-permute-start | bytes 3145736 | tf_op jit(solution)/shard_map/ppermute | solution.py:48
  373.9 55.1 %collective-permute-start.18 = (bf16[256,2048]{1,0:T(8,128)(2,1)}, bf16[256,2048]{1,0:T(8,128)(2,1)}, u32[]{:S(2)}, u32[]{:S(2)}) collective-permute-start(bf16[256,2048]{1,0:T(8,128)(2,1)} %collective-permute-done.17.refs_2_.refs_6_), channel_id=1, source_target_pairs={{0,4},{4,0},{8,12},{12,8},{16,20},{20,16},{24,28},{28,24},{1,5},{5... | collective-permute-start | bytes 3145736 | tf_op jit(solution)/shard_map/ppermute | solution.py:48
  502.8 138.7 %collective-permute-start.25 = (bf16[4096,768]{1,0:T(8,128)(2,1)}, bf16[4096,768]{1,0:T(8,128)(2,1)}, u32[]{:S(2)}, u32[]{:S(2)}) collective-permute-start(bf16[4096,768]{1,0:T(8,128)(2,1)} %grad_pair.2), channel_id=1, source_target_pairs={{0,16},{4,20},{8,24},{12,28},{16,0},{20,4},{24,8},{28,12},{1,17},{... | collective-permute-start | bytes 18874376 | tf_op jit(solution)/shard_map/ppermute | solution.py:48
  548.8 159.6 %collective-permute-start.28 = (bf16[768,2048]{1,0:T(8,128)(2,1)}, bf16[768,2048]{1,0:T(8,128)(2,1)}, u32[]{:S(2)}, u32[]{:S(2)}) collective-permute-start(bf16[768,2048]{1,0:T(8,128)(2,1)} %grad_down.2), channel_id=1, source_target_pairs={{0,16},{4,20},{8,24},{12,28},{16,0},{20,4},{24,8},{28,12},{1,17},{... | collective-permute-start | bytes 9437192 | tf_op jit(solution)/shard_map/ppermute | solution.py:48
  550.3 178.1 %reduce-scatter.9.cloned.1.call-start = ((), (), s32[]{:S(2)}) async-start(), calls=%async_computation.10 | async-start | bytes 5242880 | tf_op jit(solution)/shard_map/reduce_scatter | solution.py:585
  626.5 195.5 %reduce-scatter.11.cloned.1.call-start = ((), (), s32[]{:S(2)}) async-start(), calls=%async_computation.11 | async-start | bytes 7864320 | tf_op jit(solution)/shard_map/reduce_scatter | solution.py:585
  631.6 90.2 %collective-permute-start.24 = (bf16[512,2048]{1,0:T(8,128)(2,1)}, bf16[512,2048]{1,0:T(8,128)(2,1)}, u32[]{:S(2)}, u32[]{:S(2)}) collective-permute-start(bf16[512,2048]{1,0:T(8,128)(2,1)} %add_convert_fusion.4), channel_id=1, source_target_pairs={{0,8},{4,12},{8,0},{12,4},{16,24},{20,28},{24,16},{28,20},{1,9},{5... | collective-permute-start | bytes 6291464 | tf_op jit(solution)/shard_map/ppermute | solution.py:48
  678.0 249.7 %reduce-scatter.17.cloned.1.call-start = ((), (), s32[]{:S(2)}) async-start(), calls=%async_computation.16 | async-start | bytes 3932160 | tf_op jit(solution)/shard_map/reduce_scatter | solution.py:585
  683.3 53.8 %collective-permute-start.30 = (bf16[512,2048]{1,0:T(8,128)(2,1)}, bf16[512,2048]{1,0:T(8,128)(2,1)}, u32[]{:S(2)}, u32[]{:S(2)}) collective-permute-start(bf16[512,2048]{1,0:T(8,128)(2,1)} %get-tuple-element.192), channel_id=1, source_target_pairs={{0,8},{4,12},{8,0},{12,4},{16,24},{20,28},{24,16},{28,20},{1,9},{5... | collective-permute-start | bytes 6291464 | tf_op jit(solution)/shard_map/ppermute | solution.py:48
  686.7 88.7 %collective-permute-start.29 = (bf16[512,2048]{1,0:T(8,128)(2,1)}, bf16[512,2048]{1,0:T(8,128)(2,1)}, u32[]{:S(2)}, u32[]{:S(2)}) collective-permute-start(bf16[512,2048]{1,0:T(8,128)(2,1)} %get-tuple-element.194), channel_id=1, source_target_pairs={{0,8},{4,12},{8,0},{12,4},{16,24},{20,28},{24,16},{28,20},{1,9},{5... | collective-permute-start | bytes 6291464 | tf_op jit(solution)/shard_map/ppermute | solution.py:48
  721.7 211.1 %reduce-scatter.15.cloned.1.call-start = ((), (), s32[]{:S(2)}) async-start(), calls=%async_computation.14 | async-start | bytes 2621440 | tf_op jit(solution)/shard_map/reduce_scatter | solution.py:585
  788.2 48.4 %collective-permute-start.41 = (bf16[256,4096]{1,0:T(8,128)(2,1)}, bf16[256,4096]{1,0:T(8,128)(2,1)}, u32[]{:S(2)}, u32[]{:S(2)}) collective-permute-start(bf16[256,4096]{1,0:T(8,128)(2,1)} %pad_maximum_fusion.6), channel_id=1, source_target_pairs={{0,16},{4,20},{8,24},{12,28},{16,0},{20,4},{24,8},{28,12},{1,17},{... | collective-permute-start | bytes 6291464 | tf_op jit(solution)/shard_map/ppermute | solution.py:48
  828.3 68.4 %collective-permute-start.36 = (bf16[512,2176]{1,0:T(8,128)(2,1)}, bf16[512,2176]{1,0:T(8,128)(2,1)}, u32[]{:S(2)}, u32[]{:S(2)}) collective-permute-start(bf16[512,2176]{1,0:T(8,128)(2,1)} %get-tuple-element.190), channel_id=1, source_target_pairs={{0,8},{4,12},{8,0},{12,4},{16,24},{20,28},{24,16},{28,20},{1,9},{5... | collective-permute-start | bytes 6684680 | tf_op jit(solution)/shard_map/ppermute | solution.py:48
  840.3 212.5 %reduce-scatter.13.cloned.1.call-start = ((), (), s32[]{:S(2)}) async-start(), calls=%async_computation.12 | async-start | bytes 1392640 | tf_op jit(solution)/shard_map/reduce_scatter | solution.py:585
  841.0 54.4 %collective-permute-start.35 = (bf16[256,768]{1,0:T(8,128)(2,1)S(1)}, bf16[256,768]{1,0:T(8,128)(2,1)S(1)}, u32[]{:S(2)}, u32[]{:S(2)}) collective-permute-start(bf16[256,768]{1,0:T(8,128)(2,1)S(1)} %get-tuple-element.207), channel_id=1, source_target_pairs={{0,12},{4,8},{8,4},{12,0},{16,28},{20,24},{24,20},{28,16},{1,13},{... | collective-permute-start | bytes 1179656 | tf_op jit(solution)/shard_map/ppermute | solution.py:48
  927.7 209.6 %all-gather.17.cloned.1.call-start = ((), (), s32[]{:S(2)}) async-start(), calls=%async_computation.17 | async-start | bytes 3932160 | tf_op jit(solution)/shard_map/all_gather | solution.py:948
  928.3 255.3 %all-gather.15.cloned.1.call-start = ((), (), s32[]{:S(2)}) async-start(), calls=%async_computation.15 | async-start | bytes 2621440 | tf_op jit(solution)/shard_map/all_gather | solution.py:960
  928.3 88.3 %collective-permute-start.38 = (bf16[4,256,768]{2,1,0:T(8,128)(2,1)}, bf16[4,256,768]{2,1,0:T(8,128)(2,1)}, u32[]{:S(2)}, u32[]{:S(2)}) collective-permute-start(bf16[4,256,768]{2,1,0:T(8,128)(2,1)} %pad_maximum_fusion.12.refs_0_), channel_id=1, source_target_pairs={{0,1},{1,0},{2,3},{3,2},{4,5},{5,4},{6,7},{7,6},{8,9},{9,8},{10,11... | collective-permute-start | bytes 4718600 | tf_op jit(solution)/shard_map/ppermute | solution.py:579
  930.0 122.4 %collective-permute-start.39 = (bf16[4,256,768]{2,1,0:T(8,128)(2,1)}, bf16[4,256,768]{2,1,0:T(8,128)(2,1)}, u32[]{:S(2)}, u32[]{:S(2)}) collective-permute-start(bf16[4,256,768]{2,1,0:T(8,128)(2,1)} %pad_maximum_fusion.12.refs_0_), channel_id=1, source_target_pairs={{0,2},{1,3},{2,0},{3,1},{4,6},{5,7},{6,4},{7,5},{8,10},{9,11},{10,... | collective-permute-start | bytes 4718600 | tf_op jit(solution)/shard_map/ppermute | solution.py:579
  932.2 120.2 %collective-permute-start.40 = (bf16[4,256,768]{2,1,0:T(8,128)(2,1)}, bf16[4,256,768]{2,1,0:T(8,128)(2,1)}, u32[]{:S(2)}, u32[]{:S(2)}) collective-permute-start(bf16[4,256,768]{2,1,0:T(8,128)(2,1)} %pad_maximum_fusion.12.refs_0_), channel_id=1, source_target_pairs={{0,3},{1,2},{2,1},{3,0},{4,7},{5,6},{6,5},{7,4},{8,11},{9,10},{10,... | collective-permute-start | bytes 4718600 | tf_op jit(solution)/shard_map/ppermute | solution.py:579
  1052.5 160.3 %all-gather.13.cloned.1.call-start = ((), (), s32[]{:S(2)}) async-start(), calls=%async_computation.13 | async-start | bytes 1392640 | tf_op jit(solution)/shard_map/all_gather | solution.py:960
  (108 other events, 1231.2 us)
Sparse Core Ops, SparseCore 0:
  17.8 106.2 all-gather.6
  139.7 80.7 all-gather.8
  222.1 79.2 all-gather.10
  550.4 76.6 reduce-scatter.6
  629.3 77.2 reduce-scatter.8
  709.3 111.2 reduce-scatter.10
  822.9 60.7 reduce-scatter.16
  886.6 43.8 reduce-scatter.14
  933.5 61.7 reduce-scatter.12
  996.7 140.5 all-gather.16
  1138.9 44.6 all-gather.14
  1185.0 27.7 all-gather.12

commit v4 on v3

--- a/solution.py
+++ b/solution.py
@@ -486,38 +486,33 @@
 
 
 def lay_pairs(chunks, place, high, unit):
-    depth = len(chunks)
-    rows = chunks[0].shape[1]
+    depth = chunks.shape[0] // 4
+    rows = chunks.shape[1]
     cols = 4 * high * unit
     size = rows // 4
 
     def kernel(place_ref, *refs):
-        gate_ref, up_ref = refs[-2:]
         for which in range(depth):
-            chunk = place_ref[0] ^ which
-            far = place_ref[1] ^ (chunk // 2)
+            out_ref = refs[depth + which % 2]
+            far = place_ref[0] ^ (which // 2)
             for near in range(4):
-                start = pl.multiple_of((far * 4 + (place_ref[2] ^ near)) * unit, 128)
-
-                @pl.when(chunk % 2 == 0)
-                def _():
-                    gate_ref[:, pl.ds(start, unit)] = refs[which][near].astype(F32)
-
-                @pl.when(chunk % 2 == 1)
-                def _():
-                    up_ref[:, pl.ds(start, unit)] = refs[which][near].astype(F32)
+                start = pl.multiple_of((far * 4 + (place_ref[1] ^ near)) * unit, 128)
+                out_ref[:, pl.ds(start, unit)] = refs[which][near].astype(F32)
 
     return call(
         kernel,
         "lay_pairs",
         (4,),
-        [pl.BlockSpec((4, size, unit), lambda i, at: (0, i, 0))] * depth,
+        [
+            pl.BlockSpec((4, size, unit), functools.partial(lambda w, i, at: (w, i, 0), which))
+            for which in range(depth)
+        ],
         [pl.BlockSpec((size, cols), lambda i, at: (i, 0))] * 2,
         [jax.ShapeDtypeStruct((rows, cols), F32)] * 2,
         0,
         12 * rows * cols,
         scalars=1,
-    )(place, *chunks)
+    )(place, *[chunks] * depth)
 
 
 def visibility(parent, layout, offset, count):
@@ -571,14 +566,6 @@
     rows = parts[0].shape[0]
     own = parts[0].astype(F32) + got[:rows].astype(F32)
     return own, (parts[2].astype(F32) + got[rows:].astype(F32)).astype(BF)
-
-
-def gather_ctx(chunk):
-    count = lax.axis_size("ctx")
-    return [chunk] + [
-        lax.ppermute(chunk, "ctx", [(i, i ^ step) for i in range(count)])
-        for step in range(1, count)
-    ]
 
 
 def scatter_ctx(array):
@@ -797,33 +784,12 @@
         (),
         (me_array, unit),
     )
-    for index in range(micro):
-        if index:
-            act_b, dgu_b = feed(
-                [after(mid_rows[index][0], token)] + mid_rows[index][1:],
-                cot_rows,
-                [wgu],
-                wd,
-                index,
-                micro,
-                (act_b, dgu_b),
-                (me_array, unit),
-            )
+    def send_back(index, token):
         parts = feed_out(
-            after(dgu_b, act_b, *[d_mid[1] for d_mid in d_mids]),
-            wgu,
-            index,
-            (4, local),
-            True,
-            "feed_back",
+            after(dgu_b, token), wgu, index, (4, local), True, "feed_back"
         )
         d_mids.append(group_half(parts))
-        token = parts[0]
-    sent_pair = []
-    for far in range(1, high):
-        sent_pair.append(pair_terms(after(mid_pieces[0], token), far, []))
-        token = sent_pair[-1]
-    got_pair = [swap(piece, 4 * (far + 1)) for far, piece in enumerate(sent_pair)]
+        return parts[0]
 
     d_middles = []
     d_projs = []
@@ -831,8 +797,34 @@
     d_pair_parts = []
     d_ffn_gain = jnp.zeros((D,), F32)
     d_q_gain = jnp.zeros((1, DH), F32)
+    token = act_b
+    for index in range(1, micro):
+        token = send_back(index - 1, token)
+        act_b, dgu_b = feed(
+            [after(mid_rows[index][0], token, d_mids[index - 1][1])] + mid_rows[index][1:],
+            cot_rows,
+            [wgu],
+            wd,
+            index,
+            micro,
+            (act_b, dgu_b),
+            (me_array, unit),
+        )
+        token = act_b
+    sent_pair = []
+    sent_down = []
+    for far in range(1, high):
+        sent_pair.append(pair_terms(after(mid_pieces[0], token), far, []))
+        token = sent_pair[-1]
+    got_pair = [swap(piece, 4 * (far + 1)) for far, piece in enumerate(sent_pair)]
     for index in range(micro):
         part = rows_of(index)
+        if index == micro - 1:
+            token = send_back(index, token)
+            for far in range(1, high):
+                sent_down.append(down_terms(after(act_b, token, d_mids[index][1]), far, []))
+                token = sent_down[-1]
+            got_down = [swap(piece, 4 * (far + 1)) for far, piece in enumerate(sent_down)]
         d_mid = d_mids[index][0] + swap(d_mids[index][1], 2).astype(F32)
         d_part, d_gain = rms_back(
             middles[index], mid_inverses[index], ffn_gain, after(d_mid, token)
@@ -842,7 +834,7 @@
         d_proj = d_middle.astype(BF)
         d_attended = dot_last(d_proj, w_out).astype(BF)
         d_query, d_pair, d_gain = attention_back(
-            after(queries[part], *[d_mids[later][1] for later in range(index + 1, micro)]),
+            queries[part],
             queries_raw[part],
             everyone[index],
             masks[index],
@@ -859,12 +851,6 @@
         d_query_parts.append(d_query)
         d_pair_parts.append(scatter_ctx(d_pair))
         token = d_query
-        if index == 0:
-            sent_down = []
-            for far in range(1, high):
-                sent_down.append(down_terms(after(act_b, token), far, []))
-                token = sent_down[-1]
-            got_down = [swap(piece, 4 * (far + 1)) for far, piece in enumerate(sent_down)]
 
     d_query_b = jnp.concatenate(d_query_parts, axis=0)
     d_proj_b = jnp.concatenate(d_projs, axis=0)
@@ -944,7 +930,7 @@
     )
     columns = fold(columns, bits[:1])
     near_parts, pair_near = spread_near(pair_piece, me)
-    chunks = gather_ctx(pair_near)
+    chunks = lax.all_gather(pair_near, "ctx", axis=0, tiled=True)
     down_whole = lax.all_gather(down_piece, "ctx", axis=0, tiled=True)
     part_qo = fold(jnp.concatenate(part_qo, axis=1), bits[2:])
     part_kv = fold(
@@ -953,11 +939,11 @@
     part_kv = fold(part_kv, bits[2:])
 
     grad_gate, grad_up = lay_pairs(
-        chunks, jnp.stack([lax.axis_index("ctx"), me // 4, slot]), high, unit
+        chunks, jnp.stack([me // 4, slot]), high, unit
     )
 
     def whole(piece):
-        return lax.all_gather(after(piece, *chunks[1:]), "ctx", axis=0, tiled=True).astype(F32)
+        return lax.all_gather(piece, "ctx", axis=0, tiled=True).astype(F32)
 
     grad_down = down_whole.astype(F32)
     both = whole(scatter_ctx(part_qo))

time: 1250 us -> 1290 us (1.032)
  waiting for transfers between devices: 608 us -> 651 us
    ppermute x3 -> x0, waiting for transfers between devices: 120 us -> none  [gather_ctx(): lax.ppermute(chunk, 'ctx', [(i, i ^ step) for i in range(count)])]
    all_gather x2 -> x3, waiting for transfers between devices: 57.1 us -> 167 us  [the longest x1 101 us: body(): chunks = lax.all_gather(pair_near, 'ctx', axis=0, tiled=True)]
    ppermute x39, waiting for transfers between devices: 294 us -> 340 us  [swap(): return lax.ppermute(value, 'fsdp', [(i, i ^ bits) for i in range(count)])]
    reduce_scatter x6, waiting for transfers between devices: 0.06 us -> 27.4 us  [scatter_ctx(): return lax.psum_scatter(array, 'ctx', scatter_dimension=0, tiled=True)]
    all_gather x1, waiting for transfers between devices: 77.1 us -> 55.7 us  [body(): down_whole = lax.all_gather(down_piece, 'ctx', axis=0, tiled=True)]
  transfers between devices with their start and end apart: 54 -> 52, of which waited for: 24 -> 25; matrix products, arithmetic and copies ran while one was open for 15% -> 15% of each run, Pallas kernels for 29% -> 20%
where the time goes in v4:
time: 1290 us; the launch traced here: 1280 us
  waiting for transfers between devices  651 us (50%)
  Pallas kernels  353 us (27%)
  other arithmetic  114 us (9%)
  local copies, waits for them, and re-layouts  95.9 us (7%)
  starting transfers between devices  28 us (2%)
  matrix products  19.3 us (1%)
  between operations  15.5 us (1%)
    ppermute x39, waiting for transfers between devices, swap(): return lax.ppermute(value, 'fsdp', [(i, i ^ bits) for i in range(count)])  340 us
    pallas_call x10, Pallas kernels, weight_terms(): call(kernel, name, (steps,), [pl.BlockSpec((left.shape[0], width), lambda...  113 us
    all_gather x1, waiting for transfers between devices, body(): chunks = lax.all_gather(pair_near, 'ctx', axis=0, tiled=True)  101 us
    pallas_call x5, Pallas kernels, feed_out(): call(kernel, name, (cols // BLOCK,), [pl.BlockSpec((parts[0] * rows, dept...  72.9 us
    all_gather x2, waiting for transfers between devices, whole(): return lax.all_gather(piece, 'ctx', axis=0, tiled=True).astype(F32)  65.9 us
    pallas_call x2, Pallas kernels, feed(): call(kernel, 'feed', (steps,), [fixed((rows, depth))] * parts + [pl.Block...  61.7 us
    all_gather x1, waiting for transfers between devices, body(): lax.all_gather(jnp.concatenate([w_query, pair_shard], axis=1), 'fsdp', ax...  59.3 us
    all_gather x1, waiting for transfers between devices, body(): down_whole = lax.all_gather(down_piece, 'ctx', axis=0, tiled=True)  55.7 us
  transfers between devices with their start and end apart: 52, of which 25 were waited for; matrix products, arithmetic and copies ran while one was open for 15% of the time, Pallas kernels for 20%

profile of v4, /device:TPU:0, one launch (start us, length us, event | category | flops | bytes accessed | tf_op | source)
XLA Modules:
  0.0 1276.7 jit_solution(10546110275457009838)
XLA Ops:
  64.9 59.3 %all-gather.8.cloned.1.call-done.w_ref = bf16[2048,4096]{1,0:T(8,128)(2,1)} async-done(((bf16[256,4096]{1,0:T(8,128)(2,1)}), bf16[2048,4096]{1,0:T(8,128)(2,1)}) %all-gather.8.cloned.1.call-update) | async-done | bytes 16777232 | tf_op jit(solution)/shard_map/all_gather | solution.py:632
  126.2 10.2 project_pairs.1
  143.8 50.9 %collective-permute-done.5 = bf16[768,2048]{1,0:T(8,128)(2,1)} collective-permute-done((bf16[768,2048]{1,0:T(8,128)(2,1)}, bf16[768,2048]{1,0:T(8,128)(2,1)}, u32[]{:S(2)}, u32[]{:S(2)}) %collective-permute-start.5) | collective-permute-done | bytes 3145760 | tf_op jit(solution)/shard_map/ppermute | solution.py:48
  215.7 13.6 %project_queries.1 = (bf16[512,2048]{1,0:T(8,128)(2,1)}, bf16[512,2048]{1,0:T(8,128)(2,1)}) custom-call(bf16[512,2048]{1,0:T(8,128)(2,1)} %fusion.3.x_ref.refs_0_, bf16[2048,4096]{1,0:T(8,128)(2,1)} %all-gather.8.cloned.1.call-done.w_ref, f32[512,128]{1,0:T(8,128)} %get-tuple-element.250.c_ref, f32[512,128]{1,0:T(8,128)} %get-tuple-element.251.s_ref, ...), custom_call_target="tpu_custom_call" | custom-call | flops 42949672 | bytes 146800 | tf_op jit(solution)/shard_map/project_queries/pallas_call | solution.py:118
  233.4 25.2 %collective-permute-done.7 = bf16[512,2048]{1,0:T(8,128)(2,1)} collective-permute-done((bf16[512,2048]{1,0:T(8,128)(2,1)}, bf16[512,2048]{1,0:T(8,128)(2,1)}, u32[]{:S(2)}, u32[]{:S(2)}) %collective-permute-start.7) | collective-permute-done | bytes 2097184 | tf_op jit(solution)/shard_map/ppermute | solution.py:48
  271.7 31.1 %collective-permute-done.9.refs_6_.refs_3_.refs_7_ = bf16[512,2048]{1,0:T(8,128)(2,1)} collective-permute-done((bf16[512,2048]{1,0:T(8,128)(2,1)}, bf16[512,2048]{1,0:T(8,128)(2,1)}, u32[]{:S(2)}, u32[]{:S(2)}) %collective-permute-start.9) | collective-permute-done | bytes 2097184 | tf_op jit(solution)/shard_map/ppermute | solution.py:48
  336.5 14.7 %collective-permute-done.11.refs_2_ = bf16[256,2048]{1,0:T(8,128)(2,1)} collective-permute-done((bf16[256,2048]{1,0:T(8,128)(2,1)}, bf16[256,2048]{1,0:T(8,128)(2,1)}, u32[]{:S(2)}, u32[]{:S(2)}) %collective-permute-start.11) | collective-permute-done | bytes 1048608 | tf_op jit(solution)/shard_map/ppermute | solution.py:48
  361.7 32.8 %feed.2 = (bf16[2048,1536]{1,0:T(8,128)(2,1)}, bf16[2048,3072]{1,0:T(8,128)(2,1)}, bf16[2048,3072]{1,0:T(8,128)(2,1)}) custom-call(s32[1]{0:T(128)} %bitcast.15.me_ref, bf16[256,2048]{1,0:T(8,128)(2,1)} %multiply_convert_fusion.1.refs_0_, bf16[256,2048]{1,0:T(8,128)(2,1)} %collective-permute-done.10.refs_1_, ...), custom_call_target="tpu_custom_call" | custom-call | flops 1932735283200 | bytes 3670016000 | tf_op jit(solution)/shard_map/feed/pallas_call | solution.py:351
  394.5 18.5 %feed_back.2 = (bf16[256,2048]{1,0:T(8,128)(2,1)}, bf16[256,2048]{1,0:T(8,128)(2,1)}, bf16[256,2048]{1,0:T(8,128)(2,1)}, bf16[256,2048]{1,0:T(8,128)(2,1)}) custom-call(bf16[2048,3072]{1,0:T(8,128)(2,1)} %get-tuple-element.109.a_ref.refs_11_, bf16[2048,3072]{1,0:T(8,128)(2,1)} %get-tuple-element.110.w_ref.refs_8_), custom_call_target="tpu_custom_call" | custom-call | flops 1288490188800 | bytes 2306867200 | tf_op jit(solution)/shard_map/feed_back/pallas_call | solution.py:385
  419.1 23.0 %collective-permute-done.18.refs_2_.refs_6_ = bf16[256,2048]{1,0:T(8,128)(2,1)} collective-permute-done((bf16[256,2048]{1,0:T(8,128)(2,1)}, bf16[256,2048]{1,0:T(8,128)(2,1)}, u32[]{:S(2)}, u32[]{:S(2)}) %collective-permute-start.18) | collective-permute-done | bytes 1048608 | tf_op jit(solution)/shard_map/ppermute | solution.py:48
  449.3 28.9 %feed.3 = (bf16[2048,1536]{1,0:T(8,128)(2,1)}, bf16[2048,3072]{1,0:T(8,128)(2,1)}) custom-call(s32[1]{0:T(128)} %bitcast.15.me_ref, bf16[256,2048]{1,0:T(8,128)(2,1)} %multiply_convert_fusion.refs_0_.refs_4_, bf16[256,2048]{1,0:T(8,128)(2,1)} %copy-done.78, ...), custom_call_target="tpu_custom_call", output_to_operand_aliasing={{0}: (11, {}), {1}: (12, {})} | custom-call | flops 1932735283200 | bytes 3670016000 | tf_op jit(solution)/shard_map/feed/pallas_call | solution.py:351
  478.3 19.7 %grad_pair.2 = bf16[4096,768]{1,0:T(8,128)(2,1)} custom-call(s32[1]{0:T(128)} %bitcast.18.block_ref, s32[1]{0:T(128)} %constant.139.clone.1.start_ref.block_ref, bf16[256,2048]{1,0:T(8,128)(2,1)} %multiply_convert_fusion.1.refs_0_, bf16[256,2048]{1,0:T(8,128)(2,1)} %collective-permute-done.10.refs_1_, bf16[256,2048]{1,0:T(8,128)(2,1)} %collective-permute-done.11.refs_2_, ...), custom_call_target="tpu_custom_call" | custom-call | flops 1288490188800 | bytes 2306867200 | tf_op jit(solution)/shard_map/grad_pair/pallas_call | solution.py:441
  508.1 19.4 %attention_back.2 = (bf16[256,2048]{1,0:T(8,128)(2,1)}, bf16[1024,2048]{1,0:T(8,128)(2,1)}, f32[1,128]{1,0:T(1,128)}) custom-call(bf16[256,2048]{1,0:T(8,128)(2,1)} %get-tuple-element.98.q_ref, bf16[256,2048]{1,0:T(8,128)(2,1)} %get-tuple-element.195.r_ref, bf16[1024,2048]{1,0:T(8,128)(2,1)} %all-gather.10.cloned.1.call-done.kv_ref, ...), custom_call_target="tpu_custom_call" | custom-call | flops 536870912000 | bytes 1363148800 | tf_op jit(solution)/shard_map/attention_back/pallas_call | solution.py:232
  527.5 18.8 %feed_back.3 = (bf16[256,2048]{1,0:T(8,128)(2,1)}, bf16[256,2048]{1,0:T(8,128)(2,1)}, bf16[256,2048]{1,0:T(8,128)(2,1)}, bf16[256,2048]{1,0:T(8,128)(2,1)}) custom-call(bf16[2048,3072]{1,0:T(8,128)(2,1)} %get-tuple-element.123.refs_8_.a_ref, bf16[2048,3072]{1,0:T(8,128)(2,1)} %get-tuple-element.110.w_ref.refs_8_), custom_call_target="tpu_custom_call" | custom-call | flops 1288490188800 | bytes 2306867200 | tf_op jit(solution)/shard_map/feed_back/pallas_call | solution.py:385
  558.0 12.9 %grad_down.2 = bf16[768,2048]{1,0:T(8,128)(2,1)} custom-call(s32[1]{0:T(128)} %constant.140.clone.1.block_ref, s32[1]{0:T(128)} %constant.139.clone.1.start_ref.block_ref, bf16[2048,1536]{1,0:T(8,128)(2,1)} %get-tuple-element.149.refs_0_.a_ref, bf16[512,2048]{1,0:T(8,128)(2,1)} %bitcast.14.refs_4_.refs_1_.refs_5_, ...), custom_call_target="tpu_custom_call" | custom-call | flops 644245094400 | bytes 1468006400 | tf_op jit(solution)/shard_map/grad_down/pallas_call | solution.py:441
  572.3 10.3 collective-permute-done.22
  594.2 19.6 %attention_back.3 = (bf16[256,2048]{1,0:T(8,128)(2,1)}, bf16[1024,2048]{1,0:T(8,128)(2,1)}, f32[1,128]{1,0:T(1,128)}) custom-call(bf16[256,2048]{1,0:T(8,128)(2,1)} %get-tuple-element.104.q_ref, bf16[256,2048]{1,0:T(8,128)(2,1)} %get-tuple-element.196.r_ref, bf16[1024,2048]{1,0:T(8,128)(2,1)} %all-gather.12.cloned.1.call-done.kv_ref, ...), custom_call_target="tpu_custom_call" | custom-call | flops 536870912000 | bytes 1363148800 | tf_op jit(solution)/shard_map/attention_back/pallas_call | solution.py:232
  615.2 11.1 feed_forward.2
  626.3 10.4 feed_forward.3
  662.3 28.8 %collective-permute-done.25.refs_9_ = bf16[4096,768]{1,0:T(8,128)(2,1)} collective-permute-done((bf16[4096,768]{1,0:T(8,128)(2,1)}, bf16[4096,768]{1,0:T(8,128)(2,1)}, u32[]{:S(2)}, u32[]{:S(2)}) %collective-permute-start.25) | collective-permute-done | bytes 6291488 | tf_op jit(solution)/shard_map/ppermute | solution.py:48
  691.2 19.9 %grad_pair.3 = bf16[4096,768]{1,0:T(8,128)(2,1)} custom-call(s32[1]{0:T(128)} %bitcast.2.block_ref, s32[1]{0:T(128)} %constant.139.clone.1.start_ref.block_ref, bf16[256,2048]{1,0:T(8,128)(2,1)} %multiply_convert_fusion.1.refs_0_, bf16[256,2048]{1,0:T(8,128)(2,1)} %collective-permute-done.10.refs_1_, bf16[256,2048]{1,0:T(8,128)(2,1)} %collective-permute-done.11.refs_2_, ...), custom_call_target="tpu_custom_call" | custom-call | flops 1288490188800 | bytes 2936012800 | tf_op jit(solution)/shard_map/grad_pair/pallas_call | solution.py:441
  737.5 20.4 %collective-permute-done.28.refs_9_ = bf16[768,2048]{1,0:T(8,128)(2,1)} collective-permute-done((bf16[768,2048]{1,0:T(8,128)(2,1)}, bf16[768,2048]{1,0:T(8,128)(2,1)}, u32[]{:S(2)}, u32[]{:S(2)}) %collective-permute-start.28) | collective-permute-done | bytes 3145760 | tf_op jit(solution)/shard_map/ppermute | solution.py:48
  757.9 12.6 grad_down.3
  788.5 36.0 %collective-permute-done.29 = bf16[512,2048]{1,0:T(8,128)(2,1)} collective-permute-done((bf16[512,2048]{1,0:T(8,128)(2,1)}, bf16[512,2048]{1,0:T(8,128)(2,1)}, u32[]{:S(2)}, u32[]{:S(2)}) %collective-permute-start.29) | collective-permute-done | bytes 2097184 | tf_op jit(solution)/shard_map/ppermute | solution.py:48
  841.9 14.2 %d_normed.1 = f32[512,2048]{1,0:T(8,128)} custom-call(bf16[512,4096]{1,0:T(8,128)(2,1)} %pad_maximum_fusion.3.a_ref, bf16[2048,4096]{1,0:T(8,128)(2,1)} %all-gather.8.cloned.1.call-done.w_ref), custom_call_target="tpu_custom_call" | custom-call | flops 858993459200 | bytes 2306867200 | tf_op jit(solution)/shard_map/d_normed/pallas_call | solution.py:385
  891.3 45.8 %collective-permute-done.34 = bf16[256,768]{1,0:T(8,128)(2,1)S(1)} collective-permute-done((bf16[256,768]{1,0:T(8,128)(2,1)S(1)}, bf16[256,768]{1,0:T(8,128)(2,1)S(1)}, u32[]{:S(2)}, u32[]{:S(2)}) %collective-permute-start.34) | collective-permute-done | bytes 393248 | tf_op jit(solution)/shard_map/ppermute | solution.py:48
  950.1 25.9 %collective-permute-done.37 = bf16[256,2176]{1,0:T(8,128)(2,1)S(1)} collective-permute-done((bf16[256,2176]{1,0:T(8,128)(2,1)S(1)}, bf16[256,2176]{1,0:T(8,128)(2,1)S(1)}, u32[]{:S(2)}, u32[]{:S(2)}) %collective-permute-start.37) | collective-permute-done | bytes 1114144 | tf_op jit(solution)/shard_map/ppermute | solution.py:48
  978.6 27.3 %reduce-scatter.13.cloned.1.call-done = bf16[64,2176]{1,0:T(8,128)(2,1)} async-done(((bf16[256,2176]{1,0:T(8,128)(2,1)}), bf16[64,2176]{1,0:T(8,128)(2,1)}) %reduce-scatter.13.cloned.1.call-update) | async-done | bytes 278544 | tf_op jit(solution)/shard_map/reduce_scatter | solution.py:572
  1013.9 55.7 %all-gather.20.cloned.1.call-done = bf16[768,2048]{1,0:T(8,128)(2,1)} async-done(((bf16[192,2048]{1,0:T(8,128)(2,1)}), bf16[768,2048]{1,0:T(8,128)(2,1)}) %all-gather.20.cloned.1.call-update) | async-done | bytes 3145744 | tf_op jit(solution)/shard_map/all_gather | solution.py:934
  1075.0 40.8 %all-gather.16.cloned.1.call-done = bf16[256,4096]{1,0:T(8,128)(2,1)} async-done(((bf16[64,4096]{1,0:T(8,128)(2,1)}), bf16[256,4096]{1,0:T(8,128)(2,1)}) %all-gather.16.cloned.1.call-update) | async-done | bytes 2097168 | tf_op jit(solution)/shard_map/all_gather | solution.py:946
  1119.8 25.1 %all-gather.14.cloned.1.call-done = bf16[256,2176]{1,0:T(8,128)(2,1)} async-done(((bf16[64,2176]{1,0:T(8,128)(2,1)}), bf16[256,2176]{1,0:T(8,128)(2,1)}) %all-gather.14.cloned.1.call-update) | async-done | bytes 1114128 | tf_op jit(solution)/shard_map/all_gather | solution.py:946
  1160.4 101.0 %all-gather.18.cloned.1.call-done.refs_0_.refs_1_.refs_2_.refs_3_ = bf16[16,256,768]{2,1,0:T(8,128)(2,1)} async-done(((bf16[4,256,768]{2,1,0:T(8,128)(2,1)}), bf16[16,256,768]{2,1,0:T(8,128)(2,1)}) %all-gather.18.cloned.1.call-update) | async-done | bytes 6291472 | tf_op jit(solution)/shard_map/all_gather | solution.py:933
  (457 shorter events, 377.5 us)
Async XLA Ops:
  7.2 117.0 %all-gather.8.cloned.1.call-start = ((), (), s32[]{:S(2)}) async-start(), calls=%async_computation.6 | async-start | bytes 18874368 | tf_op jit(solution)/shard_map/all_gather | solution.py:632
  17.7 244.4 %all-gather.10.cloned.1.call-start = ((), (), s32[]{:S(2)}) async-start(), calls=%async_computation.7 | async-start | bytes 5242880 | tf_op jit(solution)/shard_map/all_gather | solution.py:685
  124.1 70.6 %collective-permute-start.5 = (bf16[768,2048]{1,0:T(8,128)(2,1)}, bf16[768,2048]{1,0:T(8,128)(2,1)}, u32[]{:S(2)}, u32[]{:S(2)}) collective-permute-start(bf16[768,2048]{1,0:T(8,128)(2,1)} %param.36), channel_id=1, source_target_pairs={{0,16},{4,20},{8,24},{12,28},{16,0},{20,4},{24,8},{28,12},{1,17},{... | collective-permute-start | bytes 9437192 | tf_op jit(solution)/shard_map/ppermute | solution.py:48
  124.9 73.8 %collective-permute-start.4 = (bf16[512,3072]{1,0:T(8,128)(2,1)}, bf16[512,3072]{1,0:T(8,128)(2,1)}, u32[]{:S(2)}, u32[]{:S(2)}) collective-permute-start(bf16[512,3072]{1,0:T(8,128)(2,1)} %column_parts.2), channel_id=1, source_target_pairs={{0,8},{4,12},{8,0},{12,4},{16,24},{20,28},{24,16},{28,20},{1,9},{5... | collective-permute-start | bytes 9437192 | tf_op jit(solution)/shard_map/ppermute | solution.py:48
  139.6 187.4 %all-gather.12.cloned.1.call-start = ((), (), s32[]{:S(2)}) async-start(), calls=%async_computation.8 | async-start | bytes 5242880 | tf_op jit(solution)/shard_map/all_gather | solution.py:685
  209.8 48.8 %collective-permute-start.7 = (bf16[512,2048]{1,0:T(8,128)(2,1)}, bf16[512,2048]{1,0:T(8,128)(2,1)}, u32[]{:S(2)}, u32[]{:S(2)}) collective-permute-start(bf16[512,2048]{1,0:T(8,128)(2,1)} %get-tuple-element.100), channel_id=1, source_target_pairs={{0,8},{4,12},{8,0},{12,4},{16,24},{20,28},{24,16},{28,20},{1,9},{5... | collective-permute-start | bytes 6291464 | tf_op jit(solution)/shard_map/ppermute | solution.py:48
  211.3 149.3 %collective-permute-start.13 = (bf16[512,2048]{1,0:T(8,128)(2,1)}, bf16[512,2048]{1,0:T(8,128)(2,1)}, u32[]{:S(2)}, u32[]{:S(2)}) collective-permute-start(bf16[512,2048]{1,0:T(8,128)(2,1)} %bitcast.14.refs_4_.refs_1_.refs_5_), channel_id=1, source_target_pairs={{0,4},{4,0},{8,12},{12,8},{16,20},{20,16},{24,28},{28,24},{1,5},{5... | collective-permute-start | bytes 6291464 | tf_op jit(solution)/shard_map/ppermute | solution.py:48
  215.0 562.2 %reduce-scatter.7.cloned.1.call-start = ((), (), s32[]{:S(2)}) async-start(), calls=%async_computation.9 | async-start | bytes 5242880 | tf_op jit(solution)/shard_map/reduce_scatter | solution.py:572
  215.1 145.5 %collective-permute-start.15 = (bf16[1024,3072]{1,0:T(8,128)(2,1)}, bf16[1024,3072]{1,0:T(8,128)(2,1)}, u32[]{:S(2)}, u32[]{:S(2)}) collective-permute-start(bf16[1024,3072]{1,0:T(8,128)(2,1)} %pad_maximum_fusion.refs_8_), channel_id=1, source_target_pairs={{0,16},{4,20},{8,24},{12,28},{16,0},{20,4},{24,8},{28,12},{1,17},{... | collective-permute-start | bytes 18874376 | tf_op jit(solution)/shard_map/ppermute | solution.py:48
  232.7 70.1 %collective-permute-start.9 = (bf16[512,2048]{1,0:T(8,128)(2,1)}, bf16[512,2048]{1,0:T(8,128)(2,1)}, u32[]{:S(2)}, u32[]{:S(2)}) collective-permute-start(bf16[512,2048]{1,0:T(8,128)(2,1)} %bitcast.14.refs_4_.refs_1_.refs_5_), channel_id=1, source_target_pairs={{0,8},{4,12},{8,0},{12,4},{16,24},{20,28},{24,16},{28,20},{1,9},{5... | collective-permute-start | bytes 6291464 | tf_op jit(solution)/shard_map/ppermute | solution.py:48
  302.7 57.9 %collective-permute-start.14 = (bf16[512,2048]{1,0:T(8,128)(2,1)}, bf16[512,2048]{1,0:T(8,128)(2,1)}, u32[]{:S(2)}, u32[]{:S(2)}) collective-permute-start(bf16[512,2048]{1,0:T(8,128)(2,1)} %collective-permute-done.9.refs_6_.refs_3_.refs_7_), channel_id=1, source_target_pairs={{0,4},{4,0},{8,12},{12,8},{16,20},{20,16},{24,28},{28,24},{1,5},{5... | collective-permute-start | bytes 6291464 | tf_op jit(solution)/shard_map/ppermute | solution.py:48
  446.9 51.2 %collective-permute-start.20 = (bf16[256,2048]{1,0:T(8,128)(2,1)}, bf16[256,2048]{1,0:T(8,128)(2,1)}, u32[]{:S(2)}, u32[]{:S(2)}) collective-permute-start(bf16[256,2048]{1,0:T(8,128)(2,1)} %add_convert_fusion.7), channel_id=1, source_target_pairs={{0,8},{4,12},{8,0},{12,4},{16,24},{20,28},{24,16},{28,20},{1,9},{5... | collective-permute-start | bytes 3145736 | tf_op jit(solution)/shard_map/ppermute | solution.py:48
  552.5 138.7 %collective-permute-start.25 = (bf16[4096,768]{1,0:T(8,128)(2,1)}, bf16[4096,768]{1,0:T(8,128)(2,1)}, u32[]{:S(2)}, u32[]{:S(2)}) collective-permute-start(bf16[4096,768]{1,0:T(8,128)(2,1)} %grad_pair.2), channel_id=1, source_target_pairs={{0,16},{4,20},{8,24},{12,28},{16,0},{20,4},{24,8},{28,12},{1,17},{... | collective-permute-start | bytes 18874376 | tf_op jit(solution)/shard_map/ppermute | solution.py:48
  553.1 224.1 %reduce-scatter.9.cloned.1.call-start = ((), (), s32[]{:S(2)}) async-start(), calls=%async_computation.10 | async-start | bytes 5242880 | tf_op jit(solution)/shard_map/reduce_scatter | solution.py:572
  570.9 187.0 %collective-permute-start.28 = (bf16[768,2048]{1,0:T(8,128)(2,1)}, bf16[768,2048]{1,0:T(8,128)(2,1)}, u32[]{:S(2)}, u32[]{:S(2)}) collective-permute-start(bf16[768,2048]{1,0:T(8,128)(2,1)} %grad_down.2), channel_id=1, source_target_pairs={{0,16},{4,20},{8,24},{12,28},{16,0},{20,4},{24,8},{28,12},{1,17},{... | collective-permute-start | bytes 9437192 | tf_op jit(solution)/shard_map/ppermute | solution.py:48
  644.3 66.8 %collective-permute-start.26 = (bf16[1024,2048]{1,0:T(8,128)(2,1)}, bf16[1024,2048]{1,0:T(8,128)(2,1)}, u32[]{:S(2)}, u32[]{:S(2)}) collective-permute-start(bf16[1024,2048]{1,0:T(8,128)(2,1)} %grad_q.2), channel_id=1, source_target_pairs={{0,4},{4,0},{8,12},{12,8},{16,20},{20,16},{24,28},{28,24},{1,5},{5... | collective-permute-start | bytes 12582920 | tf_op jit(solution)/shard_map/ppermute | solution.py:48
  655.6 63.9 %collective-permute-start.27 = (bf16[1024,2048]{1,0:T(8,128)(2,1)}, bf16[1024,2048]{1,0:T(8,128)(2,1)}, u32[]{:S(2)}, u32[]{:S(2)}) collective-permute-start(bf16[1024,2048]{1,0:T(8,128)(2,1)} %grad_o.2), channel_id=1, source_target_pairs={{0,4},{4,0},{8,12},{12,8},{16,20},{20,16},{24,28},{28,24},{1,5},{5... | collective-permute-start | bytes 12582920 | tf_op jit(solution)/shard_map/ppermute | solution.py:48
  656.4 214.5 %reduce-scatter.11.cloned.1.call-start = ((), (), s32[]{:S(2)}) async-start(), calls=%async_computation.11 | async-start | bytes 7864320 | tf_op jit(solution)/shard_map/reduce_scatter | solution.py:572
  661.5 109.3 %collective-permute-start.24 = (bf16[512,2048]{1,0:T(8,128)(2,1)}, bf16[512,2048]{1,0:T(8,128)(2,1)}, u32[]{:S(2)}, u32[]{:S(2)}) collective-permute-start(bf16[512,2048]{1,0:T(8,128)(2,1)} %add_convert_fusion.4), channel_id=1, source_target_pairs={{0,8},{4,12},{8,0},{12,4},{16,24},{20,28},{24,16},{28,20},{1,9},{5... | collective-permute-start | bytes 6291464 | tf_op jit(solution)/shard_map/ppermute | solution.py:48
  732.8 53.1 %collective-permute-start.30 = (bf16[512,2048]{1,0:T(8,128)(2,1)}, bf16[512,2048]{1,0:T(8,128)(2,1)}, u32[]{:S(2)}, u32[]{:S(2)}) collective-permute-start(bf16[512,2048]{1,0:T(8,128)(2,1)} %get-tuple-element.186), channel_id=1, source_target_pairs={{0,8},{4,12},{8,0},{12,4},{16,24},{20,28},{24,16},{28,20},{1,9},{5... | collective-permute-start | bytes 6291464 | tf_op jit(solution)/shard_map/ppermute | solution.py:48
  736.1 88.4 %collective-permute-start.29 = (bf16[512,2048]{1,0:T(8,128)(2,1)}, bf16[512,2048]{1,0:T(8,128)(2,1)}, u32[]{:S(2)}, u32[]{:S(2)}) collective-permute-start(bf16[512,2048]{1,0:T(8,128)(2,1)} %get-tuple-element.188), channel_id=1, source_target_pairs={{0,8},{4,12},{8,0},{12,4},{16,24},{20,28},{24,16},{28,20},{1,9},{5... | collective-permute-start | bytes 6291464 | tf_op jit(solution)/shard_map/ppermute | solution.py:48
  737.4 239.9 %reduce-scatter.17.cloned.1.call-start = ((), (), s32[]{:S(2)}) async-start(), calls=%async_computation.17 | async-start | bytes 3932160 | tf_op jit(solution)/shard_map/reduce_scatter | solution.py:572
  770.5 207.4 %reduce-scatter.15.cloned.1.call-start = ((), (), s32[]{:S(2)}) async-start(), calls=%async_computation.14 | async-start | bytes 2621440 | tf_op jit(solution)/shard_map/reduce_scatter | solution.py:572
  837.2 48.4 %collective-permute-start.38 = (bf16[256,4096]{1,0:T(8,128)(2,1)}, bf16[256,4096]{1,0:T(8,128)(2,1)}, u32[]{:S(2)}, u32[]{:S(2)}) collective-permute-start(bf16[256,4096]{1,0:T(8,128)(2,1)} %pad_maximum_fusion.6), channel_id=1, source_target_pairs={{0,16},{4,20},{8,24},{12,28},{16,0},{20,4},{24,8},{28,12},{1,17},{... | collective-permute-start | bytes 6291464 | tf_op jit(solution)/shard_map/ppermute | solution.py:48
  877.2 68.6 %collective-permute-start.36 = (bf16[512,2176]{1,0:T(8,128)(2,1)}, bf16[512,2176]{1,0:T(8,128)(2,1)}, u32[]{:S(2)}, u32[]{:S(2)}) collective-permute-start(bf16[512,2176]{1,0:T(8,128)(2,1)} %get-tuple-element.184), channel_id=1, source_target_pairs={{0,8},{4,12},{8,0},{12,4},{16,24},{20,28},{24,16},{28,20},{1,9},{5... | collective-permute-start | bytes 6684680 | tf_op jit(solution)/shard_map/ppermute | solution.py:48
  889.3 116.7 %reduce-scatter.13.cloned.1.call-start = ((), (), s32[]{:S(2)}) async-start(), calls=%async_computation.12 | async-start | bytes 1392640 | tf_op jit(solution)/shard_map/reduce_scatter | solution.py:572
  889.4 47.7 %collective-permute-start.34 = (bf16[256,768]{1,0:T(8,128)(2,1)S(1)}, bf16[256,768]{1,0:T(8,128)(2,1)S(1)}, u32[]{:S(2)}, u32[]{:S(2)}) collective-permute-start(bf16[256,768]{1,0:T(8,128)(2,1)S(1)} %get-tuple-element.202), channel_id=1, source_target_pairs={{0,8},{4,12},{8,0},{12,4},{16,24},{20,28},{24,16},{28,20},{1,9},{5... | collective-permute-start | bytes 1179656 | tf_op jit(solution)/shard_map/ppermute | solution.py:48
  890.1 54.3 %collective-permute-start.35 = (bf16[256,768]{1,0:T(8,128)(2,1)S(1)}, bf16[256,768]{1,0:T(8,128)(2,1)S(1)}, u32[]{:S(2)}, u32[]{:S(2)}) collective-permute-start(bf16[256,768]{1,0:T(8,128)(2,1)S(1)} %get-tuple-element.201), channel_id=1, source_target_pairs={{0,12},{4,8},{8,4},{12,0},{16,28},{20,24},{24,20},{28,16},{1,13},{... | collective-permute-start | bytes 1179656 | tf_op jit(solution)/shard_map/ppermute | solution.py:48
  977.3 92.3 %all-gather.20.cloned.1.call-start = ((), (), s32[]{:S(2)}) async-start(), calls=%async_computation.18 | async-start | bytes 3932160 | tf_op jit(solution)/shard_map/all_gather | solution.py:934
  977.9 137.9 %all-gather.16.cloned.1.call-start = ((), (), s32[]{:S(2)}) async-start(), calls=%async_computation.15 | async-start | bytes 2621440 | tf_op jit(solution)/shard_map/all_gather | solution.py:946
  978.6 166.3 %all-gather.14.cloned.1.call-start = ((), (), s32[]{:S(2)}) async-start(), calls=%async_computation.13 | async-start | bytes 1392640 | tf_op jit(solution)/shard_map/all_gather | solution.py:946
  1006.0 255.4 %all-gather.18.cloned.1.call-start = ((), (), s32[]{:S(2)}) async-start(), calls=%async_computation.16 | async-start | bytes 7864320 | tf_op jit(solution)/shard_map/all_gather | solution.py:933
  (108 other events, 1065.0 us)
Sparse Core Ops, SparseCore 0:
  17.8 106.2 all-gather.7
  139.7 80.7 all-gather.9
  222.1 79.2 all-gather.11
  553.2 76.7 reduce-scatter.6
  656.5 76.9 reduce-scatter.8
  737.6 110.0 reduce-scatter.10
  850.0 60.7 reduce-scatter.16
  913.7 43.8 reduce-scatter.14
  977.4 28.5 reduce-scatter.12
  1007.4 62.1 all-gather.19
  1071.1 44.5 all-gather.15
  1117.2 27.7 all-gather.13
  1146.5 114.8 all-gather.17

commit v5 on v3

--- a/solution.py
+++ b/solution.py
@@ -859,7 +859,7 @@
         d_query_parts.append(d_query)
         d_pair_parts.append(scatter_ctx(d_pair))
         token = d_query
-        if index == 0:
+        if index == micro - 1:
             sent_down = []
             for far in range(1, high):
                 sent_down.append(down_terms(after(act_b, token), far, []))

time: 1250 us -> 1250 us (level)
  transfers between devices with their start and end apart: 54 -> 54, of which waited for: 24 -> 25; matrix products, arithmetic and copies ran while one was open for 15% -> 15% of each run, Pallas kernels for 29% -> 29%
where the time goes in v5:
time: 1250 us; the launch traced here: 1240 us
  waiting for transfers between devices  608 us (49%)
  Pallas kernels  354 us (28%)
  other arithmetic  117 us (9%)
  local copies, waits for them, and re-layouts  89.7 us (7%)
  starting transfers between devices  32.1 us (3%)
  matrix products  19.3 us (2%)
  between operations  15.8 us (1%)
    ppermute x39, waiting for transfers between devices, swap(): return lax.ppermute(value, 'fsdp', [(i, i ^ bits) for i in range(count)])  294 us
    ppermute x3, waiting for transfers between devices, gather_ctx(): lax.ppermute(chunk, 'ctx', [(i, i ^ step) for i in range(count)])  120 us
    pallas_call x10, Pallas kernels, weight_terms(): call(kernel, name, (steps,), [pl.BlockSpec((left.shape[0], width), lambda...  113 us
    all_gather x1, waiting for transfers between devices, body(): down_whole = lax.all_gather(down_piece, 'ctx', axis=0, tiled=True)  77 us
    pallas_call x5, Pallas kernels, feed_out(): call(kernel, name, (cols // BLOCK,), [pl.BlockSpec((parts[0] * rows, dept...  73.1 us
    pallas_call x2, Pallas kernels, feed(): call(kernel, 'feed', (steps,), [fixed((rows, depth))] * parts + [pl.Block...  61.6 us
    all_gather x1, waiting for transfers between devices, body(): lax.all_gather(jnp.concatenate([w_query, pair_shard], axis=1), 'fsdp', ax...  59.3 us
    all_gather x2, waiting for transfers between devices, whole(): lax.all_gather(after(piece, *chunks[1:]), 'ctx', axis=0, tiled=True)  57.3 us
  transfers between devices with their start and end apart: 54, of which 25 were waited for; matrix products, arithmetic and copies ran while one was open for 15% of the time, Pallas kernels for 29%

profile of v5, /device:TPU:0, one launch (start us, length us, event | category | flops | bytes accessed | tf_op | source)
XLA Modules:
  0.0 1235.7 jit_solution(7611772313711218457)
XLA Ops:
  64.9 59.3 %all-gather.7.cloned.1.call-done.w_ref = bf16[2048,4096]{1,0:T(8,128)(2,1)} async-done(((bf16[256,4096]{1,0:T(8,128)(2,1)}), bf16[2048,4096]{1,0:T(8,128)(2,1)}) %all-gather.7.cloned.1.call-update) | async-done | bytes 16777232 | tf_op jit(solution)/shard_map/all_gather | solution.py:645
  126.2 10.2 project_pairs.1
  143.7 51.0 %collective-permute-done.5 = bf16[768,2048]{1,0:T(8,128)(2,1)} collective-permute-done((bf16[768,2048]{1,0:T(8,128)(2,1)}, bf16[768,2048]{1,0:T(8,128)(2,1)}, u32[]{:S(2)}, u32[]{:S(2)}) %collective-permute-start.5) | collective-permute-done | bytes 3145760 | tf_op jit(solution)/shard_map/ppermute | solution.py:48
  216.9 13.6 %project_queries.1 = (bf16[512,2048]{1,0:T(8,128)(2,1)}, bf16[512,2048]{1,0:T(8,128)(2,1)}) custom-call(bf16[512,2048]{1,0:T(8,128)(2,1)} %fusion.3.x_ref.refs_0_, bf16[2048,4096]{1,0:T(8,128)(2,1)} %all-gather.7.cloned.1.call-done.w_ref, f32[512,128]{1,0:T(8,128)} %get-tuple-element.256.c_ref, f32[512,128]{1,0:T(8,128)} %get-tuple-element.257.s_ref, ...), custom_call_target="tpu_custom_call" | custom-call | flops 42949672 | bytes 146800 | tf_op jit(solution)/shard_map/project_queries/pallas_call | solution.py:118
  234.6 24.0 %collective-permute-done.7 = bf16[512,2048]{1,0:T(8,128)(2,1)} collective-permute-done((bf16[512,2048]{1,0:T(8,128)(2,1)}, bf16[512,2048]{1,0:T(8,128)(2,1)}, u32[]{:S(2)}, u32[]{:S(2)}) %collective-permute-start.7) | collective-permute-done | bytes 2097184 | tf_op jit(solution)/shard_map/ppermute | solution.py:48
  262.1 9.5 attention.2
  271.7 31.0 %collective-permute-done.9.refs_6_.refs_3_.refs_7_ = bf16[512,2048]{1,0:T(8,128)(2,1)} collective-permute-done((bf16[512,2048]{1,0:T(8,128)(2,1)}, bf16[512,2048]{1,0:T(8,128)(2,1)}, u32[]{:S(2)}, u32[]{:S(2)}) %collective-permute-start.9) | collective-permute-done | bytes 2097184 | tf_op jit(solution)/shard_map/ppermute | solution.py:48
  327.2 9.4 attention.3
  356.4 17.6 %collective-permute-done.17.refs_2_.refs_6_ = bf16[256,2048]{1,0:T(8,128)(2,1)} collective-permute-done((bf16[256,2048]{1,0:T(8,128)(2,1)}, bf16[256,2048]{1,0:T(8,128)(2,1)}, u32[]{:S(2)}, u32[]{:S(2)}) %collective-permute-start.17) | collective-permute-done | bytes 1048608 | tf_op jit(solution)/shard_map/ppermute | solution.py:48
  373.9 33.0 %feed.2 = (bf16[2048,1536]{1,0:T(8,128)(2,1)}, bf16[2048,3072]{1,0:T(8,128)(2,1)}, bf16[2048,3072]{1,0:T(8,128)(2,1)}) custom-call(s32[1]{0:T(128)} %bitcast.15.me_ref, bf16[256,2048]{1,0:T(8,128)(2,1)} %multiply_convert_fusion.1.refs_0_, bf16[256,2048]{1,0:T(8,128)(2,1)} %collective-permute-done.10.refs_1_, ...), custom_call_target="tpu_custom_call" | custom-call | flops 1932735283200 | bytes 3670016000 | tf_op jit(solution)/shard_map/feed/pallas_call | solution.py:351
  406.9 18.5 %feed_back.2 = (bf16[256,2048]{1,0:T(8,128)(2,1)}, bf16[256,2048]{1,0:T(8,128)(2,1)}, bf16[256,2048]{1,0:T(8,128)(2,1)}, bf16[256,2048]{1,0:T(8,128)(2,1)}) custom-call(bf16[2048,3072]{1,0:T(8,128)(2,1)} %get-tuple-element.112.a_ref.refs_11_, bf16[2048,3072]{1,0:T(8,128)(2,1)} %get-tuple-element.113.w_ref.refs_8_), custom_call_target="tpu_custom_call" | custom-call | flops 1288490188800 | bytes 2306867200 | tf_op jit(solution)/shard_map/feed_back/pallas_call | solution.py:385
  429.0 28.6 %feed.3 = (bf16[2048,1536]{1,0:T(8,128)(2,1)}, bf16[2048,3072]{1,0:T(8,128)(2,1)}) custom-call(s32[1]{0:T(128)} %bitcast.15.me_ref, bf16[256,2048]{1,0:T(8,128)(2,1)} %multiply_convert_fusion.refs_0_.refs_4_, bf16[256,2048]{1,0:T(8,128)(2,1)} %collective-permute-done.16.refs_1_.refs_5_, ...), custom_call_target="tpu_custom_call", output_to_operand_aliasing={{0}: (11, {}), {1}: (12, {})} | custom-call | flops 1932735283200 | bytes 3670016000 | tf_op jit(solution)/shard_map/feed/pallas_call | solution.py:351
  461.7 18.6 %feed_back.3 = (bf16[256,2048]{1,0:T(8,128)(2,1)}, bf16[256,2048]{1,0:T(8,128)(2,1)}, bf16[256,2048]{1,0:T(8,128)(2,1)}, bf16[256,2048]{1,0:T(8,128)(2,1)}) custom-call(bf16[2048,3072]{1,0:T(8,128)(2,1)} %get-tuple-element.122.a_ref.refs_8_, bf16[2048,3072]{1,0:T(8,128)(2,1)} %get-tuple-element.113.w_ref.refs_8_), custom_call_target="tpu_custom_call" | custom-call | flops 1288490188800 | bytes 2306867200 | tf_op jit(solution)/shard_map/feed_back/pallas_call | solution.py:385
  483.4 19.4 %grad_pair.2 = bf16[4096,768]{1,0:T(8,128)(2,1)} custom-call(s32[1]{0:T(128)} %bitcast.18.block_ref, s32[1]{0:T(128)} %constant.140.clone.1.start_ref.block_ref, bf16[256,2048]{1,0:T(8,128)(2,1)} %multiply_convert_fusion.1.refs_0_, bf16[256,2048]{1,0:T(8,128)(2,1)} %collective-permute-done.10.refs_1_, bf16[256,2048]{1,0:T(8,128)(2,1)} %collective-permute-done.11.refs_2_, ...), custom_call_target="tpu_custom_call" | custom-call | flops 1288490188800 | bytes 2306867200 | tf_op jit(solution)/shard_map/grad_pair/pallas_call | solution.py:441
  517.0 19.7 %attention_back.2 = (bf16[256,2048]{1,0:T(8,128)(2,1)}, bf16[1024,2048]{1,0:T(8,128)(2,1)}, f32[1,128]{1,0:T(1,128)}) custom-call(bf16[256,2048]{1,0:T(8,128)(2,1)} %get-tuple-element.127.q_ref, bf16[256,2048]{1,0:T(8,128)(2,1)} %get-tuple-element.201.r_ref, bf16[1024,2048]{1,0:T(8,128)(2,1)} %all-gather.9.cloned.1.call-done.kv_ref, ...), custom_call_target="tpu_custom_call" | custom-call | flops 536870912000 | bytes 1363148800 | tf_op jit(solution)/shard_map/attention_back/pallas_call | solution.py:232
  553.6 19.9 %attention_back.3 = (bf16[256,2048]{1,0:T(8,128)(2,1)}, bf16[1024,2048]{1,0:T(8,128)(2,1)}, f32[1,128]{1,0:T(1,128)}) custom-call(bf16[256,2048]{1,0:T(8,128)(2,1)} %get-tuple-element.107.q_ref, bf16[256,2048]{1,0:T(8,128)(2,1)} %get-tuple-element.202.r_ref, bf16[1024,2048]{1,0:T(8,128)(2,1)} %all-gather.11.cloned.1.call-done.kv_ref, ...), custom_call_target="tpu_custom_call" | custom-call | flops 536870912000 | bytes 1363148800 | tf_op jit(solution)/shard_map/attention_back/pallas_call | solution.py:232
  573.5 12.2 grad_down.2
  587.6 11.2 feed_forward.2
  598.8 10.4 feed_forward.3
  641.6 20.1 %grad_pair.3 = bf16[4096,768]{1,0:T(8,128)(2,1)} custom-call(s32[1]{0:T(128)} %bitcast.2.block_ref, s32[1]{0:T(128)} %constant.140.clone.1.start_ref.block_ref, bf16[256,2048]{1,0:T(8,128)(2,1)} %multiply_convert_fusion.1.refs_0_, bf16[256,2048]{1,0:T(8,128)(2,1)} %collective-permute-done.10.refs_1_, bf16[256,2048]{1,0:T(8,128)(2,1)} %collective-permute-done.11.refs_2_, ...), custom_call_target="tpu_custom_call" | custom-call | flops 1288490188800 | bytes 2936012800 | tf_op jit(solution)/shard_map/grad_pair/pallas_call | solution.py:441
  688.2 20.4 %collective-permute-done.28.refs_9_ = bf16[768,2048]{1,0:T(8,128)(2,1)} collective-permute-done((bf16[768,2048]{1,0:T(8,128)(2,1)}, bf16[768,2048]{1,0:T(8,128)(2,1)}, u32[]{:S(2)}, u32[]{:S(2)}) %collective-permute-start.28) | collective-permute-done | bytes 3145760 | tf_op jit(solution)/shard_map/ppermute | solution.py:48
  708.6 13.1 %grad_down.3 = bf16[768,2048]{1,0:T(8,128)(2,1)} custom-call(s32[1]{0:T(128)} %constant.140.clone.1.start_ref.block_ref, s32[1]{0:T(128)} %constant.140.clone.1.start_ref.block_ref, bf16[2048,1536]{1,0:T(8,128)(2,1)} %get-tuple-element.153.refs_0_.a_ref, bf16[512,2048]{1,0:T(8,128)(2,1)} %bitcast.14.refs_4_.refs_1_.refs_5_, ...), custom_call_target="tpu_custom_call" | custom-call | flops 644245094400 | bytes 1782579200 | tf_op jit(solution)/shard_map/grad_down/pallas_call | solution.py:441
  739.8 35.7 %collective-permute-done.29 = bf16[512,2048]{1,0:T(8,128)(2,1)} collective-permute-done((bf16[512,2048]{1,0:T(8,128)(2,1)}, bf16[512,2048]{1,0:T(8,128)(2,1)}, u32[]{:S(2)}, u32[]{:S(2)}) %collective-permute-start.29) | collective-permute-done | bytes 2097184 | tf_op jit(solution)/shard_map/ppermute | solution.py:48
  792.9 14.4 %d_normed.1 = f32[512,2048]{1,0:T(8,128)} custom-call(bf16[512,4096]{1,0:T(8,128)(2,1)} %pad_maximum_fusion.3.a_ref, bf16[2048,4096]{1,0:T(8,128)(2,1)} %all-gather.7.cloned.1.call-done.w_ref), custom_call_target="tpu_custom_call" | custom-call | flops 858993459200 | bytes 2306867200 | tf_op jit(solution)/shard_map/d_normed/pallas_call | solution.py:385
  842.3 46.2 %collective-permute-done.34 = bf16[256,768]{1,0:T(8,128)(2,1)S(1)} collective-permute-done((bf16[256,768]{1,0:T(8,128)(2,1)S(1)}, bf16[256,768]{1,0:T(8,128)(2,1)S(1)}, u32[]{:S(2)}, u32[]{:S(2)}) %collective-permute-start.34) | collective-permute-done | bytes 393248 | tf_op jit(solution)/shard_map/ppermute | solution.py:48
  900.6 25.9 %collective-permute-done.37 = bf16[256,2176]{1,0:T(8,128)(2,1)S(1)} collective-permute-done((bf16[256,2176]{1,0:T(8,128)(2,1)S(1)}, bf16[256,2176]{1,0:T(8,128)(2,1)S(1)}, u32[]{:S(2)}, u32[]{:S(2)}) %collective-permute-start.37) | collective-permute-done | bytes 1114144 | tf_op jit(solution)/shard_map/ppermute | solution.py:48
  932.9 83.9 %collective-permute-done.38.refs_1_ = bf16[4,256,768]{2,1,0:T(8,128)(2,1)} collective-permute-done((bf16[4,256,768]{2,1,0:T(8,128)(2,1)}, bf16[4,256,768]{2,1,0:T(8,128)(2,1)}, u32[]{:S(2)}, u32[]{:S(2)}) %collective-permute-start.38) | collective-permute-done | bytes 1572896 | tf_op jit(solution)/shard_map/ppermute | solution.py:579
  1016.8 35.7 %collective-permute-done.39.refs_2_ = bf16[4,256,768]{2,1,0:T(8,128)(2,1)} collective-permute-done((bf16[4,256,768]{2,1,0:T(8,128)(2,1)}, bf16[4,256,768]{2,1,0:T(8,128)(2,1)}, u32[]{:S(2)}, u32[]{:S(2)}) %collective-permute-start.39) | collective-permute-done | bytes 1572896 | tf_op jit(solution)/shard_map/ppermute | solution.py:579
  1060.2 77.0 %all-gather.17.cloned.1.call-done = bf16[768,2048]{1,0:T(8,128)(2,1)} async-done(((bf16[192,2048]{1,0:T(8,128)(2,1)}), bf16[768,2048]{1,0:T(8,128)(2,1)}) %all-gather.17.cloned.1.call-update) | async-done | bytes 3145744 | tf_op jit(solution)/shard_map/all_gather | solution.py:948
  1142.6 8.8 lay_pairs.1
  1151.5 32.2 %all-gather.15.cloned.1.call-done = bf16[256,4096]{1,0:T(8,128)(2,1)} async-done(((bf16[64,4096]{1,0:T(8,128)(2,1)}), bf16[256,4096]{1,0:T(8,128)(2,1)}) %all-gather.15.cloned.1.call-update) | async-done | bytes 2097168 | tf_op jit(solution)/shard_map/all_gather | solution.py:960
  1187.7 25.1 %all-gather.13.cloned.1.call-done = bf16[256,2176]{1,0:T(8,128)(2,1)} async-done(((bf16[64,2176]{1,0:T(8,128)(2,1)}), bf16[256,2176]{1,0:T(8,128)(2,1)}) %all-gather.13.cloned.1.call-update) | async-done | bytes 1114128 | tf_op jit(solution)/shard_map/all_gather | solution.py:960
  (458 shorter events, 364.3 us)
Async XLA Ops:
  7.2 117.0 %all-gather.7.cloned.1.call-start = ((), (), s32[]{:S(2)}) async-start(), calls=%async_computation.6 | async-start | bytes 18874368 | tf_op jit(solution)/shard_map/all_gather | solution.py:645
  17.7 244.4 %all-gather.9.cloned.1.call-start = ((), (), s32[]{:S(2)}) async-start(), calls=%async_computation.7 | async-start | bytes 5242880 | tf_op jit(solution)/shard_map/all_gather | solution.py:698
  124.1 70.6 %collective-permute-start.5 = (bf16[768,2048]{1,0:T(8,128)(2,1)}, bf16[768,2048]{1,0:T(8,128)(2,1)}, u32[]{:S(2)}, u32[]{:S(2)}) collective-permute-start(bf16[768,2048]{1,0:T(8,128)(2,1)} %param.36), channel_id=1, source_target_pairs={{0,16},{4,20},{8,24},{12,28},{16,0},{20,4},{24,8},{28,12},{1,17},{... | collective-permute-start | bytes 9437192 | tf_op jit(solution)/shard_map/ppermute | solution.py:48
  124.9 73.8 %collective-permute-start.4 = (bf16[512,3072]{1,0:T(8,128)(2,1)}, bf16[512,3072]{1,0:T(8,128)(2,1)}, u32[]{:S(2)}, u32[]{:S(2)}) collective-permute-start(bf16[512,3072]{1,0:T(8,128)(2,1)} %column_parts.2), channel_id=1, source_target_pairs={{0,8},{4,12},{8,0},{12,4},{16,24},{20,28},{24,16},{28,20},{1,9},{5... | collective-permute-start | bytes 9437192 | tf_op jit(solution)/shard_map/ppermute | solution.py:48
  139.5 187.7 %all-gather.11.cloned.1.call-start = ((), (), s32[]{:S(2)}) async-start(), calls=%async_computation.8 | async-start | bytes 5242880 | tf_op jit(solution)/shard_map/all_gather | solution.py:698
  209.8 48.8 %collective-permute-start.7 = (bf16[512,2048]{1,0:T(8,128)(2,1)}, bf16[512,2048]{1,0:T(8,128)(2,1)}, u32[]{:S(2)}, u32[]{:S(2)}) collective-permute-start(bf16[512,2048]{1,0:T(8,128)(2,1)} %get-tuple-element.103), channel_id=1, source_target_pairs={{0,8},{4,12},{8,0},{12,4},{16,24},{20,28},{24,16},{28,20},{1,9},{5... | collective-permute-start | bytes 6291464 | tf_op jit(solution)/shard_map/ppermute | solution.py:48
  211.3 134.7 %collective-permute-start.13 = (bf16[512,2048]{1,0:T(8,128)(2,1)}, bf16[512,2048]{1,0:T(8,128)(2,1)}, u32[]{:S(2)}, u32[]{:S(2)}) collective-permute-start(bf16[512,2048]{1,0:T(8,128)(2,1)} %bitcast.14.refs_4_.refs_1_.refs_5_), channel_id=1, source_target_pairs={{0,4},{4,0},{8,12},{12,8},{16,20},{20,16},{24,28},{28,24},{1,5},{5... | collective-permute-start | bytes 6291464 | tf_op jit(solution)/shard_map/ppermute | solution.py:48
  216.2 512.3 %reduce-scatter.7.cloned.1.call-start = ((), (), s32[]{:S(2)}) async-start(), calls=%async_computation.9 | async-start | bytes 5242880 | tf_op jit(solution)/shard_map/reduce_scatter | solution.py:585
  216.2 157.7 %collective-permute-start.15 = (bf16[1024,3072]{1,0:T(8,128)(2,1)}, bf16[1024,3072]{1,0:T(8,128)(2,1)}, u32[]{:S(2)}, u32[]{:S(2)}) collective-permute-start(bf16[1024,3072]{1,0:T(8,128)(2,1)} %pad_maximum_fusion.refs_8_), channel_id=1, source_target_pairs={{0,16},{4,20},{8,24},{12,28},{16,0},{20,4},{24,8},{28,12},{1,17},{... | collective-permute-start | bytes 18874376 | tf_op jit(solution)/shard_map/ppermute | solution.py:48
  233.7 69.0 %collective-permute-start.9 = (bf16[512,2048]{1,0:T(8,128)(2,1)}, bf16[512,2048]{1,0:T(8,128)(2,1)}, u32[]{:S(2)}, u32[]{:S(2)}) collective-permute-start(bf16[512,2048]{1,0:T(8,128)(2,1)} %bitcast.14.refs_4_.refs_1_.refs_5_), channel_id=1, source_target_pairs={{0,8},{4,12},{8,0},{12,4},{16,24},{20,28},{24,16},{28,20},{1,9},{5... | collective-permute-start | bytes 6291464 | tf_op jit(solution)/shard_map/ppermute | solution.py:48
  302.7 53.1 %collective-permute-start.14 = (bf16[512,2048]{1,0:T(8,128)(2,1)}, bf16[512,2048]{1,0:T(8,128)(2,1)}, u32[]{:S(2)}, u32[]{:S(2)}) collective-permute-start(bf16[512,2048]{1,0:T(8,128)(2,1)} %collective-permute-done.9.refs_6_.refs_3_.refs_7_), channel_id=1, source_target_pairs={{0,4},{4,0},{8,12},{12,8},{16,20},{20,16},{24,28},{28,24},{1,5},{5... | collective-permute-start | bytes 6291464 | tf_op jit(solution)/shard_map/ppermute | solution.py:48
  355.9 73.2 %collective-permute-start.16 = (bf16[256,2048]{1,0:T(8,128)(2,1)}, bf16[256,2048]{1,0:T(8,128)(2,1)}, u32[]{:S(2)}, u32[]{:S(2)}) collective-permute-start(bf16[256,2048]{1,0:T(8,128)(2,1)} %multiply_convert_fusion.refs_0_.refs_4_), channel_id=1, source_target_pairs={{0,4},{4,0},{8,12},{12,8},{16,20},{20,16},{24,28},{28,24},{1,5},{5... | collective-permute-start | bytes 3145736 | tf_op jit(solution)/shard_map/ppermute | solution.py:48
  373.9 55.1 %collective-permute-start.18 = (bf16[256,2048]{1,0:T(8,128)(2,1)}, bf16[256,2048]{1,0:T(8,128)(2,1)}, u32[]{:S(2)}, u32[]{:S(2)}) collective-permute-start(bf16[256,2048]{1,0:T(8,128)(2,1)} %collective-permute-done.17.refs_2_.refs_6_), channel_id=1, source_target_pairs={{0,4},{4,0},{8,12},{12,8},{16,20},{20,16},{24,28},{28,24},{1,5},{5... | collective-permute-start | bytes 3145736 | tf_op jit(solution)/shard_map/ppermute | solution.py:48
  502.9 138.7 %collective-permute-start.25 = (bf16[4096,768]{1,0:T(8,128)(2,1)}, bf16[4096,768]{1,0:T(8,128)(2,1)}, u32[]{:S(2)}, u32[]{:S(2)}) collective-permute-start(bf16[4096,768]{1,0:T(8,128)(2,1)} %grad_pair.2), channel_id=1, source_target_pairs={{0,16},{4,20},{8,24},{12,28},{16,0},{20,4},{24,8},{28,12},{1,17},{... | collective-permute-start | bytes 18874376 | tf_op jit(solution)/shard_map/ppermute | solution.py:48
  536.7 191.8 %reduce-scatter.9.cloned.1.call-start = ((), (), s32[]{:S(2)}) async-start(), calls=%async_computation.10 | async-start | bytes 5242880 | tf_op jit(solution)/shard_map/reduce_scatter | solution.py:585
  585.7 122.9 %collective-permute-start.28 = (bf16[768,2048]{1,0:T(8,128)(2,1)}, bf16[768,2048]{1,0:T(8,128)(2,1)}, u32[]{:S(2)}, u32[]{:S(2)}) collective-permute-start(bf16[768,2048]{1,0:T(8,128)(2,1)} %grad_down.2), channel_id=1, source_target_pairs={{0,16},{4,20},{8,24},{12,28},{16,0},{20,4},{24,8},{28,12},{1,17},{... | collective-permute-start | bytes 9437192 | tf_op jit(solution)/shard_map/ppermute | solution.py:48
  628.9 193.2 %reduce-scatter.11.cloned.1.call-start = ((), (), s32[]{:S(2)}) async-start(), calls=%async_computation.11 | async-start | bytes 7864320 | tf_op jit(solution)/shard_map/reduce_scatter | solution.py:585
  634.0 87.7 %collective-permute-start.24 = (bf16[512,2048]{1,0:T(8,128)(2,1)}, bf16[512,2048]{1,0:T(8,128)(2,1)}, u32[]{:S(2)}, u32[]{:S(2)}) collective-permute-start(bf16[512,2048]{1,0:T(8,128)(2,1)} %add_convert_fusion.4), channel_id=1, source_target_pairs={{0,8},{4,12},{8,0},{12,4},{16,24},{20,28},{24,16},{28,20},{1,9},{5... | collective-permute-start | bytes 6291464 | tf_op jit(solution)/shard_map/ppermute | solution.py:48
  678.6 249.2 %reduce-scatter.17.cloned.1.call-start = ((), (), s32[]{:S(2)}) async-start(), calls=%async_computation.16 | async-start | bytes 3932160 | tf_op jit(solution)/shard_map/reduce_scatter | solution.py:585
  683.7 53.6 %collective-permute-start.30 = (bf16[512,2048]{1,0:T(8,128)(2,1)}, bf16[512,2048]{1,0:T(8,128)(2,1)}, u32[]{:S(2)}, u32[]{:S(2)}) collective-permute-start(bf16[512,2048]{1,0:T(8,128)(2,1)} %get-tuple-element.192), channel_id=1, source_target_pairs={{0,8},{4,12},{8,0},{12,4},{16,24},{20,28},{24,16},{28,20},{1,9},{5... | collective-permute-start | bytes 6291464 | tf_op jit(solution)/shard_map/ppermute | solution.py:48
  686.6 88.9 %collective-permute-start.29 = (bf16[512,2048]{1,0:T(8,128)(2,1)}, bf16[512,2048]{1,0:T(8,128)(2,1)}, u32[]{:S(2)}, u32[]{:S(2)}) collective-permute-start(bf16[512,2048]{1,0:T(8,128)(2,1)} %get-tuple-element.194), channel_id=1, source_target_pairs={{0,8},{4,12},{8,0},{12,4},{16,24},{20,28},{24,16},{28,20},{1,9},{5... | collective-permute-start | bytes 6291464 | tf_op jit(solution)/shard_map/ppermute | solution.py:48
  721.7 211.2 %reduce-scatter.15.cloned.1.call-start = ((), (), s32[]{:S(2)}) async-start(), calls=%async_computation.14 | async-start | bytes 2621440 | tf_op jit(solution)/shard_map/reduce_scatter | solution.py:585
  788.2 48.4 %collective-permute-start.41 = (bf16[256,4096]{1,0:T(8,128)(2,1)}, bf16[256,4096]{1,0:T(8,128)(2,1)}, u32[]{:S(2)}, u32[]{:S(2)}) collective-permute-start(bf16[256,4096]{1,0:T(8,128)(2,1)} %pad_maximum_fusion.6), channel_id=1, source_target_pairs={{0,16},{4,20},{8,24},{12,28},{16,0},{20,4},{24,8},{28,12},{1,17},{... | collective-permute-start | bytes 6291464 | tf_op jit(solution)/shard_map/ppermute | solution.py:48
  828.6 68.2 %collective-permute-start.36 = (bf16[512,2176]{1,0:T(8,128)(2,1)}, bf16[512,2176]{1,0:T(8,128)(2,1)}, u32[]{:S(2)}, u32[]{:S(2)}) collective-permute-start(bf16[512,2176]{1,0:T(8,128)(2,1)} %get-tuple-element.190), channel_id=1, source_target_pairs={{0,8},{4,12},{8,0},{12,4},{16,24},{20,28},{24,16},{28,20},{1,9},{5... | collective-permute-start | bytes 6684680 | tf_op jit(solution)/shard_map/ppermute | solution.py:48
  840.3 212.5 %reduce-scatter.13.cloned.1.call-start = ((), (), s32[]{:S(2)}) async-start(), calls=%async_computation.12 | async-start | bytes 1392640 | tf_op jit(solution)/shard_map/reduce_scatter | solution.py:585
  841.2 54.2 %collective-permute-start.35 = (bf16[256,768]{1,0:T(8,128)(2,1)S(1)}, bf16[256,768]{1,0:T(8,128)(2,1)S(1)}, u32[]{:S(2)}, u32[]{:S(2)}) collective-permute-start(bf16[256,768]{1,0:T(8,128)(2,1)S(1)} %get-tuple-element.207), channel_id=1, source_target_pairs={{0,12},{4,8},{8,4},{12,0},{16,28},{20,24},{24,20},{28,16},{1,13},{... | collective-permute-start | bytes 1179656 | tf_op jit(solution)/shard_map/ppermute | solution.py:48
  927.8 209.4 %all-gather.17.cloned.1.call-start = ((), (), s32[]{:S(2)}) async-start(), calls=%async_computation.17 | async-start | bytes 3932160 | tf_op jit(solution)/shard_map/all_gather | solution.py:948
  928.4 255.3 %all-gather.15.cloned.1.call-start = ((), (), s32[]{:S(2)}) async-start(), calls=%async_computation.15 | async-start | bytes 2621440 | tf_op jit(solution)/shard_map/all_gather | solution.py:960
  928.4 88.4 %collective-permute-start.38 = (bf16[4,256,768]{2,1,0:T(8,128)(2,1)}, bf16[4,256,768]{2,1,0:T(8,128)(2,1)}, u32[]{:S(2)}, u32[]{:S(2)}) collective-permute-start(bf16[4,256,768]{2,1,0:T(8,128)(2,1)} %pad_maximum_fusion.12.refs_0_), channel_id=1, source_target_pairs={{0,1},{1,0},{2,3},{3,2},{4,5},{5,4},{6,7},{7,6},{8,9},{9,8},{10,11... | collective-permute-start | bytes 4718600 | tf_op jit(solution)/shard_map/ppermute | solution.py:579
  930.0 122.5 %collective-permute-start.39 = (bf16[4,256,768]{2,1,0:T(8,128)(2,1)}, bf16[4,256,768]{2,1,0:T(8,128)(2,1)}, u32[]{:S(2)}, u32[]{:S(2)}) collective-permute-start(bf16[4,256,768]{2,1,0:T(8,128)(2,1)} %pad_maximum_fusion.12.refs_0_), channel_id=1, source_target_pairs={{0,2},{1,3},{2,0},{3,1},{4,6},{5,7},{6,4},{7,5},{8,10},{9,11},{10,... | collective-permute-start | bytes 4718600 | tf_op jit(solution)/shard_map/ppermute | solution.py:579
  932.4 120.1 %collective-permute-start.40 = (bf16[4,256,768]{2,1,0:T(8,128)(2,1)}, bf16[4,256,768]{2,1,0:T(8,128)(2,1)}, u32[]{:S(2)}, u32[]{:S(2)}) collective-permute-start(bf16[4,256,768]{2,1,0:T(8,128)(2,1)} %pad_maximum_fusion.12.refs_0_), channel_id=1, source_target_pairs={{0,3},{1,2},{2,1},{3,0},{4,7},{5,6},{6,5},{7,4},{8,11},{9,10},{10,... | collective-permute-start | bytes 4718600 | tf_op jit(solution)/shard_map/ppermute | solution.py:579
  1052.5 160.4 %all-gather.13.cloned.1.call-start = ((), (), s32[]{:S(2)}) async-start(), calls=%async_computation.13 | async-start | bytes 1392640 | tf_op jit(solution)/shard_map/all_gather | solution.py:960
  (109 other events, 1234.6 us)
Sparse Core Ops, SparseCore 0:
  17.8 106.2 all-gather.6
  139.6 80.7 all-gather.8
  222.0 79.2 all-gather.10
  536.9 77.3 reduce-scatter.6
  629.0 76.4 reduce-scatter.8
  708.3 111.2 reduce-scatter.10
  821.9 60.7 reduce-scatter.16
  885.6 43.8 reduce-scatter.14
  932.5 62.6 reduce-scatter.12
  996.6 140.5 all-gather.16
  1138.8 44.8 all-gather.14
  1185.1 27.7 all-gather.12
